TPU v7x, 32 devices: a whole 2x2x4 slice. The times are simulated.
32 devices in a mesh: grp: 2 (over x), feed: 16 (over z, y, core).
Axes of the slice: x: 2, y: 2, z: 4, core: 2. Of those that a mesh axis runs over, the one named last changes fastest.
Arguments:
- samples: bfloat16 [512, 102, 8192], P('feed', 'grp'), parts along dimension 1, may hold values from -24 to 24
- fir_taps: float32 [4, 8192], replicated, may hold values from -3 to 3
- owner_map: int32 [256, 1], replicated, may hold values from 0 to 15; in each aligned block of 256 rows (0 to 255, 256 to 511, ...) at most 24 rows name the same one
- dropped_channels: int32 [64], P('grp'), parts along dimension 0, may hold values from 0 to 255
Outputs:
- visibilities: bfloat16 [768, 2, 512, 512], P(('grp', 'feed')), parts along dimension 0
There are 2 independent parts, one for each index of `grp`. A program takes and returns all parts, laid end to end along the dimension named above; an argument that names none is the same for every part. Nothing has to cross between parts.
Inputs may be any that keep to these rules, and one draw needn't show every extreme that they name: `owner_map`: no more than 24 channels share an owner, and some owner has exactly 24.
All inputs are finite; a program needn't handle non-finite values.
Results may differ from a plain program's by a relative error of at most 0.001.
Values sent between devices are 32-bit elements; how exact they have to be, the bound alone decides.
No kernel may reach another device: no remote copies, remote signals or barrier semaphores. Data moves between devices by JAX's collectives and lax.ppermute only.
A program may use at most 384 MiB of HBM per device.

v0:
```python
import math

import jax
import jax.numpy as jnp
from jax import lax
from jax.sharding import PartitionSpec as P

NIN = 512
NFFT = 8192
BAND = 256
BAND_START = 1536
SPEC = 48


def dft_table(length, first, width):
    row_ids = lax.broadcasted_iota(jnp.int32, (length, width), 0)
    chan_ids = first + lax.broadcasted_iota(jnp.int32, (length, width), 1)
    phase_int = row_ids * chan_ids % length
    angles = phase_int.astype(jnp.float32) * (2.0 * math.pi / length)
    return jnp.concatenate([jnp.cos(angles), -jnp.sin(angles)], axis=1)


def slot_tables(owner_map, dropped_channels, capacity, slot_total):
    owners = owner_map[:, 0]
    channels = jnp.arange(owners.shape[0], dtype=jnp.int32)
    same_owner = (owners[:, None] == owners[None, :]) & (channels[None, :] < channels[:, None])
    rank_in = jnp.sum(same_owner.astype(jnp.int32), axis=1)
    slot_of = owners * capacity + rank_in
    flagged = jnp.any(dropped_channels[:, None] == channels[None, :], axis=0)
    channel_live = jnp.logical_not(flagged)
    targets = jnp.arange(slot_total, dtype=jnp.int32)
    slot_hit = (slot_of[:, None] == targets[None, :]) & channel_live[:, None]
    chan_of = jnp.sum(slot_hit.astype(jnp.int32) * channels[:, None], axis=0)
    slot_used = jnp.any(slot_hit, axis=0)
    return (chan_of, slot_used, channel_live)


def window(block, fir_taps):
    taps = fir_taps.shape[0]
    spec_count = block.shape[1] - taps + 1
    summed = jnp.zeros((block.shape[0], spec_count, block.shape[2]), jnp.float32)
    for tap_index in range(taps):
        summed = summed + fir_taps[tap_index][None, None, :] * block[
            :, tap_index : tap_index + spec_count, :
        ].astype(jnp.float32)
    return summed


def pair_products(left, right):
    return jnp.einsum(
        "qis,qjs->qij",
        left,
        right,
        precision=lax.Precision.HIGHEST,
        preferred_element_type=jnp.float32,
    )


def correlate(received):
    columns = received[0]
    real_rows = columns[:, :, :SPEC]
    imag_rows = columns[:, :, SPEC:]
    rotated = jnp.concatenate([imag_rows, -real_rows], axis=2)
    real_vis = pair_products(columns, columns)
    imag_vis = pair_products(rotated, columns)
    return jnp.stack([real_vis, imag_vis], axis=1)


def local(samples, fir_taps, owner_map, dropped_channels):
    devices = lax.axis_size("feed")
    capacity = BAND // devices + BAND // (2 * devices)
    slot_total = devices * capacity
    in_local = samples.shape[0]
    dft_scale = 1.0 / math.sqrt(NFFT)
    chan_of, slot_used, channel_live = slot_tables(
        owner_map, dropped_channels, capacity, slot_total
    )
    live_mask = channel_live.astype(jnp.float32)
    kept = jnp.sum(live_mask)
    windowed = window(samples, fir_taps).reshape(in_local * SPEC, NFFT)
    table = dft_table(NFFT, BAND_START, BAND)
    spectra = (
        jnp.dot(
            windowed, table, precision=lax.Precision.HIGHEST, preferred_element_type=jnp.float32
        )
        * dft_scale
    )
    spectra = spectra.reshape(in_local, SPEC, 2, BAND)
    chosen = jnp.take(spectra, chan_of, axis=3) * slot_used.astype(jnp.float32)[None, None, None, :]
    outgoing = jnp.transpose(chosen, (3, 0, 2, 1)).reshape(devices, capacity, in_local, 2 * SPEC)
    raw_vis = correlate(lax.all_to_all(outgoing, "feed", split_axis=0, concat_axis=2, tiled=True))
    local_power = jnp.sum(jnp.trace(raw_vis[:, 0], axis1=1, axis2=2))
    power = lax.psum(local_power, "feed")
    mean_power = power / (NIN * SPEC * kept)
    factor = 1.0 / (SPEC * mean_power)
    return (raw_vis * factor).astype(jnp.bfloat16)


def solution(mesh):
    return jax.shard_map(
        local,
        mesh=mesh,
        in_specs=(P("feed", "grp", None), P(), P(), P("grp")),
        out_specs=P(("grp", "feed"), None, None, None),
        check_vma=False,
    )
```

profile of v0, /device:TPU:0, one launch (start us, length us, event | category | flops | bytes accessed | tf_op | source)
XLA Modules:
  0.0 655.2 jit_solution(3375887779262449799)
XLA Ops:
  0.0 0.7 fusion.21
  1.3 0.9 convert_reduce_fusion
  3.3 65.2 %fusion.25 = (bf16[32,48,8192]{2,0,1:T(8,128)(2,1)}, bf16[32,48,8192]{2,0,1:T(8,128)(2,1)}, bf16[32,48,8192]{2,0,1:T(8,128)(2,1)}, bf16[32,48,8192]{2,0,1:T(8,128)(2,1)}) fusion(bf16[32,51,8192]{2,0,1:T(8,128)(2,1)} %param.4), kind=kLoop, calls=%fused_computation.46 | loop fusion | bytes 201326592 | tf_op jit(solution)/shard_map/slice | solution.py:43
  68.6 34.7 %fusion.14 = (f32[8192,256]{1,0:T(8,128)}, f32[8192,256]{1,0:T(8,128)}) fusion(s32[256]{0:T(256)S(1)} %iota_add_fusion), kind=kLoop, calls=%fused_computation.24 | loop fusion | flops 31457280 | bytes 16778240 | tf_op jit(solution)/shard_map/cos | solution.py:20
  103.3 106.0 %multiply_add_fusion = f32[32,48,8192]{2,1,0:T(8,128)} fusion(bf16[32,48,8192]{2,0,1:T(8,128)(2,1)} %get-tuple-element.8, bf16[32,48,8192]{2,0,1:T(8,128)(2,1)} %get-tuple-element.6, bf16[32,48,8192]{2,0,1:T(8,128)(2,1)} %get-tuple-element.7, bf16[32,48,8192]{2,0,1:T(8,128)(2,1)} %get-tuple-element.5, f32[8192]{0:T(1024)S(1)} %bitcast.29, ...), kind=kLoop, calls=%fused_computation.3 | loop fusion | flops 138412032 | bytes 151126016 | tf_op jit(solution)/shard_map/add | solution.py:43
  209.3 86.8 %fusion.15 = f32[1536,512]{1,0:T(8,128)} fusion(f32[1536,8192]{1,0:T(8,128)} %bitcast.26, f32[8192,256]{1,0:T(8,128)} %get-tuple-element.16, f32[8192,256]{1,0:T(8,128)} %get-tuple-element.15), kind=kOutput, calls=%fused_computation.25 | convolution fusion | flops 77314392064 | bytes 70254592 | tf_op jit(solution)/shard_map/dot_general | solution.py:83
  296.1 3.8 reshape.42
  299.9 7.0 %copy.23 = f32[32,48,2,256]{1,0,2,3:T(8,128)} copy(f32[32,48,2,256]{3,2,1,0:T(2,128)S(1)} %reshape.42) | data formatting | bytes 6291456 | tf_op jit(solution)/shard_map/reshape | solution.py:88
  306.8 9.5 %gather_fusion = f32[384,32,48,2]{2,1,3,0:T(8,128)} fusion(f32[32,48,2,256]{1,0,2,3:T(8,128)} %copy.23, s32[1024]{0:T(1024)S(1)} %pad_clamp_fusion), kind=kCustom, calls=%fused_computation | custom fusion | bytes 9438720 | tf_op jit(solution)/shard_map/jit(_take)/gather | solution.py:89
  316.4 5.8 multiply_bitcast_fusion
  322.2 11.3 %copy.24 = f32[384,32,2,48]{3,2,1,0:T(2,128)} copy(f32[384,32,2,48]{3,1,2,0:T(8,128)S(1)} %multiply_bitcast_fusion) | data formatting | bytes 9437184 | tf_op jit(solution)/shard_map/mul | solution.py:89
  333.6 12.7 %reshape.43 = f32[16,24,32,96]{3,2,1,0:T(8,128)} reshape(f32[384,32,2,48]{3,2,1,0:T(2,128)} %copy.24) | data formatting | bytes 9437184 | tf_op jit(solution)/shard_map/reshape | solution.py:90
  346.3 7.6 %all-to-all-start = ((f32[16,24,32,96]{3,2,1,0:T(8,128)}), f32[16,24,32,96]{3,2,1,0:T(8,128)}, u32[]{:S(2)}, u32[]{:S(2)}) async-start(f32[16,24,32,96]{3,2,1,0:T(8,128)} %reshape.43), calls=%async_computation | async-start | bytes 12582912 | tf_op jit(solution)/shard_map/all_to_all | solution.py:91
  355.2 112.8 %all-to-all-done = f32[16,24,32,96]{3,2,1,0:T(8,128)} async-done(((f32[16,24,32,96]{3,2,1,0:T(8,128)}), f32[16,24,32,96]{3,2,1,0:T(8,128)}, u32[]{:S(2)}, u32[]{:S(2)}) %all-to-all-start) | async-done | bytes 4718624 | tf_op jit(solution)/shard_map/all_to_all | solution.py:91
  468.0 3.5 copy.25
  471.6 7.1 %fusion.26 = (f32[24,512,48]{2,1,0:T(8,128)}, f32[24,512,48]{2,1,0:T(8,128)}) fusion(f32[24,512,96]{2,1,0:T(8,128)S(1)} %bitcast.22), kind=kLoop, calls=%fused_computation.47 | loop fusion | bytes 9437184 | tf_op jit(solution)/shard_map/slice | solution.py:62
  478.6 5.9 copy.40
  484.5 2.0 neg.7
  486.5 5.8 copy.39
  492.4 31.0 %select_reduce_fusion = (f32[]{:T(128)}, f32[24,512,512]{2,1,0:T(8,128)}) fusion(pred[512,512]{1,0:T(8,128)(4,1)S(1)} %iota_compare_fusion, f32[24,512,96]{2,1,0:T(8,128)} %bitcast.23), kind=kOutput, calls=%fused_computation.4 | convolution fusion | flops 7260340224 | bytes 30146564 | tf_op jit(solution)/shard_map/qis,qjs->qij/dot_general | solution.py:50
  523.4 57.0 %psum.7 = f32[]{:T(128)} all-reduce(f32[]{:T(128)} %get-tuple-element.17), channel_id=1, replica_groups=mesh['grp'=2,'feed'=16] {'feed'}, use_global_device_ids=true, to_apply=%region_5.6 | all-reduce | flops 1 | bytes 8 | tf_op jit(solution)/shard_map/psum | solution.py:93
  580.4 25.6 %convolution_bitcast_fusion = f32[24,1,512,512]{3,2,0,1:T(8,128)} fusion(f32[24,512,96]{2,1,0:T(8,128)} %bitcast.24, f32[24,512,48]{1,2,0:T(8,128)S(1)} %neg.7, f32[24,512,48]{1,2,0:T(8,128)} %copy.39), kind=kOutput, calls=%fused_computation.13 | convolution fusion | flops 7248936960 | bytes 34603008 | tf_op jit(solution)/shard_map/qis,qjs->qij/dot_general | solution.py:50
  606.7 27.6 %fusion = bf16[24,2,512,512]{3,2,0,1:T(8,128)(2,1)} fusion(f32[24,1,512,512]{3,2,0,1:T(8,128)} %convolution_bitcast_fusion, f32[24,1,512,512]{3,2,0,1:T(8,128)} %bitcast.25, f32[]{:T(128)S(6)} %div.7), kind=kLoop, calls=%fused_computation.2 | loop fusion | flops 37748736 | bytes 75497472 | tf_op jit(solution)/shard_map/convert_element_type | solution.py:96
  634.3 20.5 %copy.31 = bf16[24,2,512,512]{3,2,1,0:T(8,128)(2,1)} copy(bf16[24,2,512,512]{3,2,0,1:T(8,128)(2,1)} %fusion) | data formatting | bytes 50331648 | tf_op jit(solution)/shard_map/convert_element_type | solution.py:96
  (20 shorter events, 2.4 us)
Async XLA Ops:
  0.8 0.5 copy-start.2
  3.3 65.2 %copy-start.1 = (f32[4,8192]{1,0:T(4,128)S(1)}, f32[4,8192]{1,0:T(4,128)}, u32[]{:S(2)}) copy-start(f32[4,8192]{1,0:T(4,128)} %param.5) | copy-start | bytes 393220
  333.6 20.3 %copy-start.3 = (pred[256]{0:T(512)(128)(4,1)S(1)}, pred[256]{0:T(512)(128)(4,1)}, u32[]{:S(2)}) copy-start(pred[256]{0:T(512)(128)(4,1)} %copy-done.2) | copy-start | bytes 772
  346.3 121.7 %all-to-all-start = ((f32[16,24,32,96]{3,2,1,0:T(8,128)}), f32[16,24,32,96]{3,2,1,0:T(8,128)}, u32[]{:S(2)}, u32[]{:S(2)}) async-start(f32[16,24,32,96]{3,2,1,0:T(8,128)} %reshape.43), calls=%async_computation | async-start | bytes 12582912 | tf_op jit(solution)/shard_map/all_to_all | solution.py:91
  471.5 7.1 %copy-start = (f32[1,24,16,32,96]{4,3,2,1,0:T(8,128)}, f32[1,24,16,32,96]{4,3,2,1,0:T(8,128)S(1)}, u32[]{:S(2)}) copy-start(f32[1,24,16,32,96]{4,3,2,1,0:T(8,128)S(1)} %copy.25) | copy-start | bytes 14155780
where the time goes:
time: 665 us; the launch traced here: 655 us
  other arithmetic  180 us (27%)
  local copies, waits for them, and re-layouts  153 us (23%)
  matrix products  143 us (22%)
  waiting for transfers between devices  113 us (17%)
  blocking collectives  57 us (9%)
  starting transfers between devices  7.56 us (1%)
    all_to_all x1, waiting for transfers between devices, local(): lax.all_to_all(outgoing, 'feed', split_axis=0, concat_axis=2, tiled=True)  113 us
    add x1, other arithmetic, window(): summed + fir_taps[tap_index][None, None, :] * block[:, tap_index:tap_inde...  106 us
    dot_general x1, matrix products, local(): jnp.dot(windowed, table, precision=lax.Precision.HIGHEST, preferred_eleme...  86.8 us
    slice x1, local copies, waits for them, and re-layouts, window(): block[:, tap_index:tap_index + spec_count, :].astype(jnp.float32)  65.2 us
    psum x1, blocking collectives, local(): power = lax.psum(local_power, 'feed')  57 us
    dot_general x2, matrix products, pair_products(): jnp.einsum('qis,qjs->qij', left, right, precision=lax.Precision.HIGHEST,...  56.7 us
    cos x1, other arithmetic, dft_table(): return jnp.concatenate([jnp.cos(angles), -jnp.sin(angles)], axis=1)  34.7 us
    convert_element_type x1, other arithmetic, local(): return (raw_vis * factor).astype(jnp.bfloat16)  27.6 us
  transfers between devices with their start and end apart: 1, of which 1 were waited for; matrix products, arithmetic and copies ran while one was open for 0% of the time, Pallas kernels for 0%

commit v1 on v0

--- a/solution.py
+++ b/solution.py
@@ -1,15 +1,25 @@
+import functools
 import math
 
 import jax
 import jax.numpy as jnp
+import ml_dtypes
+import numpy as np
 from jax import lax
+from jax.experimental import pallas as pl
+from jax.experimental.pallas import tpu as pltpu
 from jax.sharding import PartitionSpec as P
 
 NIN = 512
 NFFT = 8192
+HALF = NFFT // 2
 BAND = 256
 BAND_START = 1536
 SPEC = 48
+GROUP = 16
+NB = 256
+LANES = 128
+MIB = 1 << 20
 
 
 def dft_table(length, first, width):
@@ -18,6 +28,19 @@
     phase_int = row_ids * chan_ids % length
     angles = phase_int.astype(jnp.float32) * (2.0 * math.pi / length)
     return jnp.concatenate([jnp.cos(angles), -jnp.sin(angles)], axis=1)
+
+
+def folded_table():
+    n = np.arange(HALF, dtype=np.int64)
+    tables = []
+    for parity in range(2):
+        chans = BAND_START + 2 * np.arange(BAND // 2, dtype=np.int64) + parity
+        angles = (chans[:, None] * n[None, :] % NFFT) * (2.0 * math.pi / NFFT)
+        full = np.concatenate([np.cos(angles), -np.sin(angles)], axis=0) / math.sqrt(NFFT)
+        high = full.astype(np.float32).astype(ml_dtypes.bfloat16)
+        low = (full - high.astype(np.float64)).astype(np.float32).astype(ml_dtypes.bfloat16)
+        tables += [high, low]
+    return np.stack(tables)
 
 
 def slot_tables(owner_map, dropped_channels, capacity, slot_total):
@@ -66,7 +89,7 @@
     return jnp.stack([real_vis, imag_vis], axis=1)
 
 
-def local(samples, fir_taps, owner_map, dropped_channels):
+def local_plain(samples, fir_taps, owner_map, dropped_channels):
     devices = lax.axis_size("feed")
     capacity = BAND // devices + BAND // (2 * devices)
     slot_total = devices * capacity
@@ -96,9 +119,337 @@
     return (raw_vis * factor).astype(jnp.bfloat16)
 
 
+def split(value):
+    high = value.astype(jnp.bfloat16)
+    return high, (value - high.astype(jnp.float32)).astype(jnp.bfloat16)
+
+
+def contract_last(left, right):
+    return lax.dot_general(
+        left, right, (((1,), (1,)), ((), ())), preferred_element_type=jnp.float32
+    )
+
+
+def spectra_kernel(parts, carry_in, capacity, taps, in_local, *refs):
+    slot_ref, live_ref, taps_a, taps_b, main_a, halo_a, main_b, halo_b, table = refs[:9]
+    refs = refs[9:]
+    before, refs = refs[:carry_in], refs[carry_in:]
+    outs, refs = refs[: len(parts)], refs[len(parts) :]
+    power_out, frames, even_h, even_l, odd_h, odd_l, acc, flat = refs
+    step = pl.program_id(0)
+    tiles = NB // LANES
+
+    for half, (main, halo) in enumerate(((main_a, halo_a), (main_b, halo_b))):
+        for tile in range(tiles):
+            lanes = slice(tile * LANES, (tile + 1) * LANES)
+            for i in range(in_local):
+                frames[half, tile, pl.ds(i, GROUP, stride=in_local), :] = main[i, :, lanes].astype(
+                    jnp.float32
+                )
+                tail = halo[i, :, lanes].astype(jnp.float32)[:8]
+                frames[half, tile, pl.ds(GROUP * in_local + i, 8, stride=in_local), :] = tail
+
+    for tile in range(tiles):
+        lanes = slice(tile * LANES, (tile + 1) * LANES)
+        coef_a = [taps_a[t : t + 1, lanes] for t in range(taps)]
+        coef_b = [taps_b[t : t + 1, lanes] for t in range(taps)]
+        for first in range(0, in_local, 16):
+
+            def load(half, f):
+                return frames[half, tile, pl.ds(f * in_local + first, 16), :]
+
+            held_a = [load(0, f) for f in range(taps - 1)]
+            held_b = [load(1, f) for f in range(taps - 1)]
+            for s in range(GROUP):
+                held_a.append(load(0, s + taps - 1))
+                held_b.append(load(1, s + taps - 1))
+                low_half = sum(coef_a[t] * held_a[t] for t in range(1, taps)) + coef_a[0] * held_a[0]
+                high_half = sum(coef_b[t] * held_b[t] for t in range(1, taps)) + coef_b[0] * held_b[0]
+                rows = slice(s * in_local + first, s * in_local + first + 16)
+                even_h[rows, lanes], even_l[rows, lanes] = split(low_half + high_half)
+                odd_h[rows, lanes], odd_l[rows, lanes] = split(low_half - high_half)
+                held_a, held_b = held_a[1:], held_b[1:]
+
+    for parity, (high, low) in enumerate(((even_h, even_l), (odd_h, odd_l))):
+        total = contract_last(table[2 * parity], high[...])
+        total += contract_last(table[2 * parity + 1], high[...])
+        total += contract_last(table[2 * parity], low[...])
+        rows = slice(parity * BAND, (parity + 1) * BAND)
+
+        @pl.when(step == 0)
+        def _():
+            acc[rows, :] = total
+
+        @pl.when(step > 0)
+        def _():
+            acc[rows, :] += total
+
+    @pl.when(step == pl.num_programs(0) - 1)
+    def _():
+        width = GROUP * in_local // LANES
+        for parity in range(2):
+            for part in range(2):
+                for block in range(BAND // 16):
+                    for g in range(width):
+                        start = parity * BAND + part * (BAND // 2) + block * 8
+                        value = acc[start : start + 8, g * LANES : (g + 1) * LANES]
+                        row = block * 128 + parity * 8 + part * width + g
+                        flat[pl.ds(row, 8, stride=16), :] = value
+
+        def place(c, total):
+            value = flat[pl.ds(pl.multiple_of(c * 8, 8), 8), :]
+            slot = slot_ref[c]
+            dest, rank = lax.div(slot, capacity), lax.rem(slot, capacity)
+            for out, (low, high, extra) in zip(outs, parts):
+
+                @pl.when((rank >= low) & (rank < high))
+                def _(out=out, low=low):
+                    out[dest, rank - low] = value
+
+            weight = live_ref[c].astype(jnp.float32)
+            return total + weight * (value * value)
+
+        total = lax.fori_loop(0, BAND, place, jnp.zeros((8, LANES), jnp.float32), unroll=8)
+        for ref in before:
+            total = total + ref[...]
+        power_out[...] = total
+        for out, (low, high, extra) in zip(outs, parts):
+            if extra:
+                for d in range(out.shape[0]):
+                    out[d, high - low] = total
+
+
+def spectra_call(group, parts, before, table, slot_of, live, fir_taps, samples, devices, capacity):
+    in_local, _, _ = samples.shape
+    taps = fir_taps.shape[0]
+    steps = HALF // NB
+    far = HALF // NB
+
+    def frames_spec(offset, block):
+        return pl.BlockSpec((in_local, GROUP, NB), lambda j, *_: (0, block, j + offset))
+
+    def taps_spec(offset):
+        return pl.BlockSpec((taps, NB), lambda j, *_: (0, j + offset))
+
+    rows = GROUP * in_local
+    width = 2 * rows // LANES
+    shapes = [
+        jax.ShapeDtypeStruct((devices, high - low + extra, width, LANES), jnp.float32)
+        for low, high, extra in parts
+    ]
+    shapes.append(jax.ShapeDtypeStruct((8, LANES), jnp.float32))
+    grid_spec = pltpu.PrefetchScalarGridSpec(
+        num_scalar_prefetch=2,
+        grid=(steps,),
+        in_specs=[
+            taps_spec(0),
+            taps_spec(far),
+            frames_spec(0, group),
+            frames_spec(0, group + 1),
+            frames_spec(far, group),
+            frames_spec(far, group + 1),
+            pl.BlockSpec((4, BAND, NB), lambda j, *_: (0, 0, j)),
+        ]
+        + [pl.BlockSpec((8, LANES), lambda j, *_: (0, 0))] * len(before),
+        out_specs=[pl.BlockSpec(s.shape, lambda j, *_, n=len(s.shape): (0,) * n) for s in shapes],
+        scratch_shapes=[
+            pltpu.VMEM((2, NB // LANES, (GROUP + 8) * in_local, LANES), jnp.float32),
+            pltpu.VMEM((rows, NB), jnp.bfloat16),
+            pltpu.VMEM((rows, NB), jnp.bfloat16),
+            pltpu.VMEM((rows, NB), jnp.bfloat16),
+            pltpu.VMEM((rows, NB), jnp.bfloat16),
+            pltpu.VMEM((2 * BAND, rows), jnp.float32),
+            pltpu.VMEM((BAND * 8, LANES), jnp.float32),
+        ],
+    )
+    return pl.pallas_call(
+        functools.partial(spectra_kernel, parts, len(before), capacity, taps, in_local),
+        out_shape=shapes,
+        grid_spec=grid_spec,
+        compiler_params=pltpu.CompilerParams(vmem_limit_bytes=40 * MIB),
+        cost_estimate=pl.CostEstimate(
+            flops=3 * 2 * rows * HALF * 2 * BAND, bytes_accessed=30 * MIB, transcendentals=0
+        ),
+        name="spectra",
+    )(
+        slot_of,
+        live,
+        fir_taps,
+        fir_taps,
+        samples,
+        samples,
+        samples,
+        samples,
+        table,
+        *before,
+    )
+
+
+def exchange_lanes(values, in_local):
+    count = len(values)
+    lane = lax.broadcasted_iota(jnp.int32, values[0].shape, 1) // in_local
+    values = list(values)
+    distance = count // 2
+    while distance:
+        upper = (lane & distance) != 0
+        shift = distance * in_local
+        for a in range(count):
+            if a & distance:
+                continue
+            x, y = values[a], values[a + distance]
+            values[a] = jnp.where(upper, pltpu.roll(y, shift, 1), x)
+            values[a + distance] = jnp.where(upper, y, pltpu.roll(x, LANES - shift, 1))
+        distance //= 2
+    return values
+
+
+def correlate_kernel(counts, in_local, *refs):
+    used_ref, factor_ref = refs[:2]
+    groups = refs[2 : 2 + counts]
+    out, left_real, left_imag, right_a, right_b = refs[-5:]
+    slot = pl.program_id(0)
+    used = used_ref[slot] != 0
+    per_tile = LANES // in_local
+    sources = groups[0].shape[0]
+    row_tiles = per_tile * counts
+
+    @pl.when(used)
+    def _():
+        factor = factor_ref[0]
+        upper = lax.broadcasted_iota(jnp.int32, (8, LANES), 0) >= 4
+        for block in range(sources // per_tile):
+            lanes = slice(block * LANES, (block + 1) * LANES)
+            tiles = [None] * row_tiles
+            for g, ref in enumerate(groups):
+                mixed = [ref[block * per_tile + a, 0] for a in range(per_tile)]
+                for q, value in enumerate(exchange_lanes(mixed, in_local)):
+                    tiles[q * counts + g] = value
+            turned = [jnp.where(upper, -1.0, 1.0) * pltpu.roll(t, 4, 0) for t in tiles]
+            pad = [jnp.zeros((LANES - 8 * row_tiles, LANES), jnp.float32)]
+            columns = jnp.concatenate(tiles + pad, axis=0)
+            rotated = jnp.concatenate(turned + pad, axis=0)
+            high, low = split(columns)
+            right_a[:LANES, lanes] = high
+            right_a[LANES:, lanes] = high
+            right_b[:, lanes] = low
+            high, low = split(columns.T)
+            left_real[lanes, :LANES] = high
+            left_real[lanes, LANES:] = low
+            high, low = split(rotated.T)
+            left_imag[lanes, :LANES] = high
+            left_imag[lanes, LANES:] = low
+        for part, left in enumerate((left_real, left_imag)):
+            for block in range(sources // per_tile):
+                rows = slice(block * LANES, (block + 1) * LANES)
+                total = jnp.dot(left[rows, :], right_a[...], preferred_element_type=jnp.float32)
+                total += jnp.dot(
+                    left[rows, :LANES], right_b[...], preferred_element_type=jnp.float32
+                )
+                out[0, part, rows, :] = (total * factor).astype(jnp.bfloat16)
+
+    @pl.when(jnp.logical_not(used))
+    def _():
+        out[...] = jnp.zeros_like(out)
+
+
+def correlate_call(received, low, high, capacity, used, factor, total, in_local):
+    arrays = [r for r, _ in received]
+    sources = arrays[0].shape[0]
+    nin = sources * in_local
+    width = arrays[0].shape[2]
+    aliases = {}
+    extra, extra_specs = [], []
+    if total is not None:
+        extra, extra_specs = [total], [pl.BlockSpec(memory_space=pl.ANY)]
+        aliases = {2 + len(arrays): 0}
+    in_specs = [
+        pl.BlockSpec(memory_space=pltpu.SMEM),
+        pl.BlockSpec(memory_space=pltpu.SMEM),
+    ] + [
+        pl.BlockSpec((sources, 1, width, LANES), lambda s, d=low - first: (0, s + d, 0, 0))
+        for _, first in received
+    ]
+    return pl.pallas_call(
+        functools.partial(correlate_kernel, len(arrays), in_local),
+        out_shape=jax.ShapeDtypeStruct((capacity, 2, nin, nin), jnp.bfloat16),
+        grid=(high - low,),
+        in_specs=in_specs + extra_specs,
+        out_specs=pl.BlockSpec((1, 2, nin, nin), lambda s: (s + low, 0, 0, 0)),
+        scratch_shapes=[
+            pltpu.VMEM((nin, 2 * LANES), jnp.bfloat16),
+            pltpu.VMEM((nin, 2 * LANES), jnp.bfloat16),
+            pltpu.VMEM((2 * LANES, nin), jnp.bfloat16),
+            pltpu.VMEM((LANES, nin), jnp.bfloat16),
+        ],
+        input_output_aliases=aliases,
+        compiler_params=pltpu.CompilerParams(vmem_limit_bytes=40 * MIB),
+        cost_estimate=pl.CostEstimate(
+            flops=(high - low) * 8 * nin * nin * 256,
+            bytes_accessed=(high - low) * (4 * nin * nin + 8 * nin * SPEC),
+            transcendentals=0,
+        ),
+        name="correlate",
+    )(used[low:high], factor, *arrays, *extra)
+
+
+def local_blocks(samples, fir_taps, owner_map, dropped_channels):
+    devices = lax.axis_size("feed")
+    capacity = BAND // devices + BAND // (2 * devices)
+    in_local = samples.shape[0]
+    owners = owner_map[:, 0]
+    channels = jnp.arange(BAND, dtype=jnp.int32)
+    same_owner = (owners[:, None] == owners[None, :]) & (channels[None, :] < channels[:, None])
+    slot_of = owners * capacity + jnp.sum(same_owner.astype(jnp.int32), axis=1)
+    live = jnp.logical_not(jnp.any(dropped_channels[None, :] == channels[:, None], axis=1))
+    kept = jnp.sum(live.astype(jnp.float32))
+    mine = lax.axis_index("feed") * capacity + jnp.arange(capacity, dtype=jnp.int32)
+    used = jnp.any((slot_of[None, :] == mine[:, None]) & live[None, :], axis=1).astype(jnp.int32)
+
+    table = jnp.asarray(folded_table())
+    groups = SPEC // GROUP
+    middle = capacity // 2
+    received, powers = [], []
+    for group in range(groups):
+        if group < groups - 1:
+            parts = ((0, capacity, 0),)
+        else:
+            parts = ((0, middle, 1), (middle, capacity, 0))
+        *blocks, power = spectra_call(
+            group,
+            parts,
+            powers[-1:],
+            table,
+            slot_of,
+            live.astype(jnp.int32),
+            fir_taps,
+            samples,
+            devices,
+            capacity,
+        )
+        powers.append(power)
+        received.append(
+            [
+                lax.all_to_all(block, "feed", split_axis=0, concat_axis=0, tiled=True)
+                for block in blocks
+            ]
+        )
+    power = jnp.sum(received[-1][0][:, middle])
+    mean_power = power / (NIN * SPEC * kept)
+    factor = jnp.reshape(1.0 / (SPEC * mean_power), (1,))
+    full = [(blocks[0], 0) for blocks in received[:-1]]
+    first = correlate_call(
+        full + [(received[-1][0], 0)], 0, middle, capacity, used, factor, None, in_local
+    )
+    return correlate_call(
+        full + [(received[-1][1], middle)], middle, capacity, capacity, used, factor, first, in_local
+    )
+
+
 def solution(mesh):
+    in_local = NIN // mesh.shape["feed"]
+    blocks = in_local * 4 == LANES
     return jax.shard_map(
-        local,
+        local_blocks if blocks else local_plain,
         mesh=mesh,
         in_specs=(P("feed", "grp", None), P(), P(), P("grp")),
         out_specs=P(("grp", "feed"), None, None, None),

time: 665 us -> 302 us (0.45)
  the two profiles are of different devices: /device:TPU:0 before, /device:TPU:13 now
where the time goes in v1:
time: 302 us; the launch traced here: 297 us
  Pallas kernels  145 us (48%)
  blocking collectives  109 us (36%)
  local copies, waits for them, and re-layouts  30.8 us (10%)
  starting transfers between devices  5.05 us (2%)
  other arithmetic  4.63 us (2%)
    pallas_call x3, Pallas kernels, spectra_call(): pl.pallas_call(functools.partial(spectra_kernel, parts, len(before), capa...  122 us
    all_to_all x3, blocking collectives, local_blocks(): lax.all_to_all(block, 'feed', split_axis=0, concat_axis=0, tiled=True)  109 us
    unnamed x9, local copies, waits for them, and re-layouts  30.7 us
    pallas_call x2, Pallas kernels, correlate_call(): pl.pallas_call(functools.partial(correlate_kernel, len(arrays), in_local)...  23.6 us
  transfers between devices with their start and end apart: 1, of which 1 were waited for; matrix products, arithmetic and copies ran while one was open for 1% of the time, Pallas kernels for 4%

profile of v1, /device:TPU:13, one launch (start us, length us, event | category | flops | bytes accessed | tf_op | source)
XLA Modules:
  0.0 297.3 jit_solution(17195159245464870111)
XLA Ops:
  0.0 0.7 fusion.1
  0.7 0.9 convert_reduce_fusion
  1.7 0.7 multiply_add_fusion.refs_0_
  2.4 26.2 %copy.27.refs_4_.refs_5_.refs_6_.refs_7_ = bf16[32,51,8192]{2,1,0:T(8,128)(2,1)} copy(bf16[32,51,8192]{2,0,1:T(8,128)(2,1)} %param.5) | data formatting | bytes 53477376 | tf_op args[0]
  28.6 0.0 copy-done.1
  28.6 0.0 copy-start
  28.6 3.4 %copy-done = bf16[4,256,4096]{2,1,0:T(8,128)(2,1)S(1)} copy-done((bf16[4,256,4096]{2,1,0:T(8,128)(2,1)S(1)}, bf16[4,256,4096]{2,1,0:T(8,128)(2,1)}, u32[]{:S(2)}) %copy-start) | copy-done | bytes 8388632
  31.9 39.8 %spectra.3 = (f32[16,24,8,128]{3,2,1,0:T(8,128)S(1)}, f32[8,128]{1,0:T(8,128)S(1)}) custom-call(s32[256]{0:T(256)S(1)} %multiply_add_fusion.refs_0_, s32[256]{0:T(256)S(1)} %get-tuple-element.19.refs_1_, f32[4,8192]{1,0:T(4,128)S(1)} %copy-done.1, f32[4,8192]{1,0:T(4,128)S(1)} %copy-done.1, bf16[32,51,8192]{2,1,0:T(8,128)(2,1)} %copy.27.refs_4_.refs_5_.refs_6_.refs_7_, ...), custom_call_target="tpu_custom_call" | custom-call | flops 6442450944 | bytes 31457280 | tf_op jit(solution)/shard_map/spectra/pallas_call | solution.py:265
  71.8 39.8 %spectra.4 = (f32[16,24,8,128]{3,2,1,0:T(8,128)S(1)}, f32[8,128]{1,0:T(8,128)S(1)}) custom-call(s32[256]{0:T(256)S(1)} %multiply_add_fusion.refs_0_, s32[256]{0:T(256)S(1)} %get-tuple-element.19.refs_1_, f32[4,8192]{1,0:T(4,128)S(1)} %copy-done.1, f32[4,8192]{1,0:T(4,128)S(1)} %copy-done.1, bf16[32,51,8192]{2,1,0:T(8,128)(2,1)} %copy.27.refs_4_.refs_5_.refs_6_.refs_7_, ...), custom_call_target="tpu_custom_call" | custom-call | flops 6442450944 | bytes 31457280 | tf_op jit(solution)/shard_map/spectra/pallas_call | solution.py:265
  111.6 41.9 %spectra.5 = (f32[16,13,8,128]{3,2,1,0:T(8,128)S(1)}, f32[16,12,8,128]{3,2,1,0:T(8,128)S(1)}, f32[8,128]{1,0:T(8,128)}) custom-call(s32[256]{0:T(256)S(1)} %multiply_add_fusion.refs_0_, s32[256]{0:T(256)S(1)} %get-tuple-element.19.refs_1_, f32[4,8192]{1,0:T(4,128)S(1)} %copy-done.1, f32[4,8192]{1,0:T(4,128)S(1)} %copy-done.1, ...), custom_call_target="tpu_custom_call" | custom-call | flops 6442450944 | bytes 31457280 | tf_op jit(solution)/shard_map/spectra/pallas_call | solution.py:265
  153.6 27.1 %all_to_all.20.refs_4_ = f32[16,13,8,128]{3,2,1,0:T(8,128)} all-to-all(f32[16,13,8,128]{3,2,1,0:T(8,128)S(1)} %get-tuple-element.13), channel_id=1, replica_groups=mesh['grp'=2,'feed'=16] {'feed'}, dimensions={0} | all-to-all | bytes 1703936 | tf_op jit(solution)/shard_map/all_to_all | solution.py:432
  180.6 40.9 %all_to_all.21.refs_2_ = f32[16,24,8,128]{3,2,1,0:T(8,128)S(1)} all-to-all(f32[16,24,8,128]{3,2,1,0:T(8,128)S(1)} %get-tuple-element.14), channel_id=1, replica_groups=mesh['grp'=2,'feed'=16] {'feed'}, dimensions={0} | all-to-all | bytes 3145728 | tf_op jit(solution)/shard_map/all_to_all | solution.py:432
  221.5 40.9 %all_to_all.22.refs_3_ = f32[16,24,8,128]{3,2,1,0:T(8,128)S(1)} all-to-all(f32[16,24,8,128]{3,2,1,0:T(8,128)S(1)} %get-tuple-element.15), channel_id=1, replica_groups=mesh['grp'=2,'feed'=16] {'feed'}, dimensions={0} | all-to-all | bytes 3145728 | tf_op jit(solution)/shard_map/all_to_all | solution.py:432
  262.4 0.0 copy-done.3
  262.4 5.0 %all-to-all-start.3 = ((f32[16,12,8,128]{3,2,1,0:T(8,128)}), f32[16,12,8,128]{3,2,1,0:T(8,128)}, u32[]{:S(2)}, u32[]{:S(2)}) async-start(f32[16,12,8,128]{3,2,1,0:T(8,128)} %copy-done.3), calls=%async_computation.3 | async-start | bytes 1572864 | tf_op jit(solution)/shard_map/all_to_all | solution.py:432
  267.4 0.2 and_reduce_fusion
  267.6 0.6 convert_reduce_fusion.1
  268.9 0.1 fusion.2
  269.0 1.5 slice_reduce_fusion
  271.1 0.0 copy-start.2
  271.1 1.1 copy-done.2
  272.3 13.2 %correlate.2.refs_5_ = bf16[24,2,512,512]{3,2,1,0:T(8,128)(2,1)} custom-call(s32[12]{0:T(128)S(1)} %get-tuple-element.17.refs_0_, f32[1]{0:T(128)} %bitcast.1.refs_1_, f32[16,24,8,128]{3,2,1,0:T(8,128)S(1)} %all_to_all.21.refs_2_, f32[16,24,8,128]{3,2,1,0:T(8,128)S(1)} %all_to_all.22.refs_3_, f32[16,13,8,128]{3,2,1,0:T(8,128)S(1)} %copy-done.2), custom_call_target="tpu_custom_call" | custom-call | flops 6442450944 | bytes 14942208 | tf_op jit(solution)/shard_map/correlate/pallas_call | solution.py:372
  285.4 1.3 all-to-all-done.3.refs_4_
  286.8 10.5 %correlate.3 = bf16[24,2,512,512]{3,2,1,0:T(8,128)(2,1)} custom-call(s32[12]{0:T(128)S(1)} %get-tuple-element.18.refs_0_, f32[1]{0:T(128)} %bitcast.1.refs_1_, f32[16,24,8,128]{3,2,1,0:T(8,128)S(1)} %all_to_all.21.refs_2_, f32[16,24,8,128]{3,2,1,0:T(8,128)S(1)} %all_to_all.22.refs_3_, ...), custom_call_target="tpu_custom_call", output_to_operand_aliasing={{}: (5, {})} | custom-call | flops 6442450944 | bytes 14942208 | tf_op jit(solution)/shard_map/correlate/pallas_call | solution.py:372
  (5 shorter events, 0.0 us)
Async XLA Ops:
  2.4 26.2 %copy-start.1 = (f32[4,8192]{1,0:T(4,128)S(1)}, f32[4,8192]{1,0:T(4,128)}, u32[]{:S(2)}) copy-start(f32[4,8192]{1,0:T(4,128)} %refs_3_.5) | copy-start | bytes 393220
  28.6 3.4 %copy-start = (bf16[4,256,4096]{2,1,0:T(8,128)(2,1)S(1)}, bf16[4,256,4096]{2,1,0:T(8,128)(2,1)}, u32[]{:S(2)}) copy-start(bf16[4,256,4096]{2,1,0:T(8,128)(2,1)} %constant.8.clone.refs_8_) | copy-start | bytes 25165828
  153.6 108.8 %copy-start.3 = (f32[16,12,8,128]{3,2,1,0:T(8,128)}, f32[16,12,8,128]{3,2,1,0:T(8,128)S(1)}, u32[]{:S(2)}) copy-start(f32[16,12,8,128]{3,2,1,0:T(8,128)S(1)} %get-tuple-element.16) | copy-start | bytes 2359300
  262.4 24.4 %all-to-all-start.3 = ((f32[16,12,8,128]{3,2,1,0:T(8,128)}), f32[16,12,8,128]{3,2,1,0:T(8,128)}, u32[]{:S(2)}, u32[]{:S(2)}) async-start(f32[16,12,8,128]{3,2,1,0:T(8,128)} %copy-done.3), calls=%async_computation.3 | async-start | bytes 1572864 | tf_op jit(solution)/shard_map/all_to_all | solution.py:432
  271.1 1.2 copy-start.2

commit v2 on v1

--- a/solution.py
+++ b/solution.py
@@ -131,23 +131,13 @@
 
 
 def spectra_kernel(parts, carry_in, capacity, taps, in_local, *refs):
-    slot_ref, live_ref, taps_a, taps_b, main_a, halo_a, main_b, halo_b, table = refs[:9]
-    refs = refs[9:]
+    slot_ref, live_ref, taps_a, taps_b, frames_a, frames_b, table = refs[:7]
+    refs = refs[7:]
     before, refs = refs[:carry_in], refs[carry_in:]
     outs, refs = refs[: len(parts)], refs[len(parts) :]
-    power_out, frames, even_h, even_l, odd_h, odd_l, acc, flat = refs
+    power_out, even_h, even_l, odd_h, odd_l, acc, flat = refs
     step = pl.program_id(0)
     tiles = NB // LANES
-
-    for half, (main, halo) in enumerate(((main_a, halo_a), (main_b, halo_b))):
-        for tile in range(tiles):
-            lanes = slice(tile * LANES, (tile + 1) * LANES)
-            for i in range(in_local):
-                frames[half, tile, pl.ds(i, GROUP, stride=in_local), :] = main[i, :, lanes].astype(
-                    jnp.float32
-                )
-                tail = halo[i, :, lanes].astype(jnp.float32)[:8]
-                frames[half, tile, pl.ds(GROUP * in_local + i, 8, stride=in_local), :] = tail
 
     for tile in range(tiles):
         lanes = slice(tile * LANES, (tile + 1) * LANES)
@@ -156,7 +146,8 @@
         for first in range(0, in_local, 16):
 
             def load(half, f):
-                return frames[half, tile, pl.ds(f * in_local + first, 16), :]
+                ref = (frames_a, frames_b)[half]
+                return ref[f, first : first + 16, lanes].astype(jnp.float32)
 
             held_a = [load(0, f) for f in range(taps - 1)]
             held_b = [load(1, f) for f in range(taps - 1)]
@@ -220,13 +211,17 @@
 
 
 def spectra_call(group, parts, before, table, slot_of, live, fir_taps, samples, devices, capacity):
-    in_local, _, _ = samples.shape
+    _, in_local, _ = samples.shape
     taps = fir_taps.shape[0]
     steps = HALF // NB
     far = HALF // NB
 
-    def frames_spec(offset, block):
-        return pl.BlockSpec((in_local, GROUP, NB), lambda j, *_: (0, block, j + offset))
+    def frames_spec(offset):
+        count = GROUP + taps - 1
+        return pl.BlockSpec(
+            (pl.Element(count), pl.Element(in_local), pl.Element(NB)),
+            lambda j, *_: (group * GROUP, 0, pl.multiple_of((j + offset) * NB, NB)),
+        )
 
     def taps_spec(offset):
         return pl.BlockSpec((taps, NB), lambda j, *_: (0, j + offset))
@@ -244,16 +239,13 @@
         in_specs=[
             taps_spec(0),
             taps_spec(far),
-            frames_spec(0, group),
-            frames_spec(0, group + 1),
-            frames_spec(far, group),
-            frames_spec(far, group + 1),
+            frames_spec(0),
+            frames_spec(far),
             pl.BlockSpec((4, BAND, NB), lambda j, *_: (0, 0, j)),
         ]
         + [pl.BlockSpec((8, LANES), lambda j, *_: (0, 0))] * len(before),
         out_specs=[pl.BlockSpec(s.shape, lambda j, *_, n=len(s.shape): (0,) * n) for s in shapes],
         scratch_shapes=[
-            pltpu.VMEM((2, NB // LANES, (GROUP + 8) * in_local, LANES), jnp.float32),
             pltpu.VMEM((rows, NB), jnp.bfloat16),
             pltpu.VMEM((rows, NB), jnp.bfloat16),
             pltpu.VMEM((rows, NB), jnp.bfloat16),
@@ -266,7 +258,7 @@
         functools.partial(spectra_kernel, parts, len(before), capacity, taps, in_local),
         out_shape=shapes,
         grid_spec=grid_spec,
-        compiler_params=pltpu.CompilerParams(vmem_limit_bytes=40 * MIB),
+        compiler_params=pltpu.CompilerParams(vmem_limit_bytes=60 * MIB),
         cost_estimate=pl.CostEstimate(
             flops=3 * 2 * rows * HALF * 2 * BAND, bytes_accessed=30 * MIB, transcendentals=0
         ),
@@ -276,8 +268,6 @@
         live,
         fir_taps,
         fir_taps,
-        samples,
-        samples,
         samples,
         samples,
         table,
@@ -382,7 +372,7 @@
             pltpu.VMEM((LANES, nin), jnp.bfloat16),
         ],
         input_output_aliases=aliases,
-        compiler_params=pltpu.CompilerParams(vmem_limit_bytes=40 * MIB),
+        compiler_params=pltpu.CompilerParams(vmem_limit_bytes=60 * MIB),
         cost_estimate=pl.CostEstimate(
             flops=(high - low) * 8 * nin * nin * 256,
             bytes_accessed=(high - low) * (4 * nin * nin + 8 * nin * SPEC),
@@ -396,6 +386,7 @@
     devices = lax.axis_size("feed")
     capacity = BAND // devices + BAND // (2 * devices)
     in_local = samples.shape[0]
+    samples = jnp.transpose(samples, (1, 0, 2))
     owners = owner_map[:, 0]
     channels = jnp.arange(BAND, dtype=jnp.int32)
     same_owner = (owners[:, None] == owners[None, :]) & (channels[None, :] < channels[:, None])

time: 302 us -> 245 us (0.81)
  local copies, waits for them, and re-layouts: 30.8 us -> 1.53 us
  Pallas kernels: 145 us -> 118 us
    pallas_call x3, Pallas kernels: 122 us -> 90.9 us  [spectra_call(): pl.pallas_call(functools.partial(spectra_kernel, parts, len(before), capa...]
    unnamed x9 -> x8, local copies, waits for them, and re-layouts: 30.7 us -> 0.89 us
    pallas_call x2, Pallas kernels: 23.6 us -> 26.7 us  [correlate_call(): pl.pallas_call(functools.partial(correlate_kernel, len(arrays), in_local)...]
  transfers between devices with their start and end apart: 1 -> 1, of which waited for: 1 -> 1; matrix products, arithmetic and copies ran while one was open for 1% -> 1% of each run, Pallas kernels for 4% -> 6%
where the time goes in v2:
time: 245 us; the launch traced here: 242 us
  Pallas kernels  118 us (48%)
  blocking collectives  109 us (44%)
  starting transfers between devices  5.05 us (2%)
  other arithmetic  4.93 us (2%)
    all_to_all x3, blocking collectives, local_blocks(): lax.all_to_all(block, 'feed', split_axis=0, concat_axis=0, tiled=True)  109 us
    pallas_call x3, Pallas kernels, spectra_call(): pl.pallas_call(functools.partial(spectra_kernel, parts, len(before), capa...  90.9 us
    pallas_call x2, Pallas kernels, correlate_call(): pl.pallas_call(functools.partial(correlate_kernel, len(arrays), in_local)...  26.7 us
    all_to_all x1, starting transfers between devices, local_blocks(): lax.all_to_all(block, 'feed', split_axis=0, concat_axis=0, tiled=True)  5.05 us
  transfers between devices with their start and end apart: 1, of which 1 were waited for; matrix products, arithmetic and copies ran while one was open for 1% of the time, Pallas kernels for 6%

profile of v2, /device:TPU:13, one launch (start us, length us, event | category | flops | bytes accessed | tf_op | source)
XLA Modules:
  0.0 241.7 jit_solution(7356944352924507199)
XLA Ops:
  0.0 0.7 fusion.1
  0.7 0.9 convert_reduce_fusion
  1.7 1.3 multiply_add_fusion.refs_0_
  2.9 0.6 not_convert_fusion
  3.5 29.7 %spectra.3 = (f32[16,24,8,128]{3,2,1,0:T(8,128)}, f32[8,128]{1,0:T(8,128)}) custom-call(s32[256]{0:T(256)} %multiply_add_fusion.refs_0_, s32[256]{0:T(256)} %get-tuple-element.19.refs_1_, f32[4,8192]{1,0:T(4,128)} %refs_3_.5, f32[4,8192]{1,0:T(4,128)} %refs_3_.5, bf16[51,32,8192]{2,1,0:T(8,128)(2,1)} %bitcast.3, bf16[51,32,8192]{2,1,0:T(8,128)(2,1)} %bitcast.4, ...), custom_call_target="tpu_custom_call" | custom-call | flops 6442450944 | bytes 31457280 | tf_op jit(solution)/shard_map/spectra/pallas_call | solution.py:257
  33.2 29.8 %spectra.4 = (f32[16,24,8,128]{3,2,1,0:T(8,128)}, f32[8,128]{1,0:T(8,128)}) custom-call(s32[256]{0:T(256)} %multiply_add_fusion.refs_0_, s32[256]{0:T(256)} %get-tuple-element.19.refs_1_, f32[4,8192]{1,0:T(4,128)} %refs_3_.5, f32[4,8192]{1,0:T(4,128)} %refs_3_.5, bf16[51,32,8192]{2,1,0:T(8,128)(2,1)} %bitcast.5, bf16[51,32,8192]{2,1,0:T(8,128)(2,1)} %bitcast.6, ...), custom_call_target="tpu_custom_call" | custom-call | flops 6442450944 | bytes 31457280 | tf_op jit(solution)/shard_map/spectra/pallas_call | solution.py:257
  63.0 0.0 copy-start.2
  63.0 31.4 %spectra.5 = (f32[16,13,8,128]{3,2,1,0:T(8,128)}, f32[16,12,8,128]{3,2,1,0:T(8,128)}, f32[8,128]{1,0:T(8,128)}) custom-call(s32[256]{0:T(256)} %multiply_add_fusion.refs_0_, s32[256]{0:T(256)} %get-tuple-element.19.refs_1_, f32[4,8192]{1,0:T(4,128)} %refs_3_.5, f32[4,8192]{1,0:T(4,128)} %refs_3_.5, bf16[51,32,8192]{2,1,0:T(8,128)(2,1)} %bitcast.7, ...), custom_call_target="tpu_custom_call" | custom-call | flops 6442450944 | bytes 31457280 | tf_op jit(solution)/shard_map/spectra/pallas_call | solution.py:257
  94.4 0.0 copy-start.3
  94.4 27.2 %all_to_all.20.refs_4_ = f32[16,13,8,128]{3,2,1,0:T(8,128)S(1)} all-to-all(f32[16,13,8,128]{3,2,1,0:T(8,128)} %get-tuple-element.13), channel_id=1, replica_groups=mesh['grp'=2,'feed'=16] {'feed'}, dimensions={0} | all-to-all | bytes 1703936 | tf_op jit(solution)/shard_map/all_to_all | solution.py:423
  121.6 0.0 copy-done.2
  121.6 41.0 %all_to_all.21.refs_2_ = f32[16,24,8,128]{3,2,1,0:T(8,128)} all-to-all(f32[16,24,8,128]{3,2,1,0:T(8,128)S(1)} %copy-done.2), channel_id=1, replica_groups=mesh['grp'=2,'feed'=16] {'feed'}, dimensions={0} | all-to-all | bytes 3145728 | tf_op jit(solution)/shard_map/all_to_all | solution.py:423
  162.6 41.2 %all_to_all.22.refs_3_ = f32[16,24,8,128]{3,2,1,0:T(8,128)} all-to-all(f32[16,24,8,128]{3,2,1,0:T(8,128)} %get-tuple-element.15), channel_id=1, replica_groups=mesh['grp'=2,'feed'=16] {'feed'}, dimensions={0} | all-to-all | bytes 3145728 | tf_op jit(solution)/shard_map/all_to_all | solution.py:423
  203.8 5.0 %all-to-all-start.3 = ((f32[16,12,8,128]{3,2,1,0:T(8,128)}), f32[16,12,8,128]{3,2,1,0:T(8,128)S(1)}, u32[]{:S(2)}, u32[]{:S(2)}) async-start(f32[16,12,8,128]{3,2,1,0:T(8,128)} %get-tuple-element.16), calls=%async_computation.3 | async-start | bytes 1572864 | tf_op jit(solution)/shard_map/all_to_all | solution.py:423
  208.9 0.0 copy-done.3
  208.9 0.2 and_reduce_fusion
  209.1 0.6 convert_reduce_fusion.1
  210.3 0.6 fusion.2
  211.0 0.6 slice_reduce_fusion
  212.3 0.0 copy-done
  212.3 14.0 %correlate.2.refs_5_ = bf16[24,2,512,512]{3,2,1,0:T(8,128)(2,1)} custom-call(s32[12]{0:T(128)} %get-tuple-element.17.refs_0_, f32[1]{0:T(128)} %bitcast.2.refs_1_, f32[16,24,8,128]{3,2,1,0:T(8,128)} %all_to_all.21.refs_2_, f32[16,24,8,128]{3,2,1,0:T(8,128)} %all_to_all.22.refs_3_, f32[16,13,8,128]{3,2,1,0:T(8,128)} %copy-done), custom_call_target="tpu_custom_call" | custom-call | flops 6442450944 | bytes 14942208 | tf_op jit(solution)/shard_map/correlate/pallas_call | solution.py:362
  226.3 1.8 all-to-all-done.3.refs_4_
  228.1 0.9 copy-done.1
  229.0 12.7 %correlate.3 = bf16[24,2,512,512]{3,2,1,0:T(8,128)(2,1)} custom-call(s32[12]{0:T(128)} %get-tuple-element.18.refs_0_, f32[1]{0:T(128)} %bitcast.2.refs_1_, f32[16,24,8,128]{3,2,1,0:T(8,128)} %all_to_all.21.refs_2_, f32[16,24,8,128]{3,2,1,0:T(8,128)} %all_to_all.22.refs_3_, f32[16,12,8,128]{3,2,1,0:T(8,128)} %copy-done.1, ...), custom_call_target="tpu_custom_call", output_to_operand_aliasing={{}: (5, {})} | custom-call | flops 6442450944 | bytes 14942208 | tf_op jit(solution)/shard_map/correlate/pallas_call | solution.py:362
  (4 shorter events, 0.0 us)
Async XLA Ops:
  63.0 58.6 %copy-start.2 = (f32[16,24,8,128]{3,2,1,0:T(8,128)S(1)}, f32[16,24,8,128]{3,2,1,0:T(8,128)}, u32[]{:S(2)}) copy-start(f32[16,24,8,128]{3,2,1,0:T(8,128)} %get-tuple-element.14) | copy-start | bytes 4718596
  94.4 114.4 %copy-start.3 = (s32[256]{0:T(256)S(1)}, s32[256]{0:T(256)}, u32[]{:S(2)}) copy-start(s32[256]{0:T(256)} %multiply_add_fusion.refs_0_) | copy-start | bytes 3076
  121.6 90.7 %copy-start = (f32[16,13,8,128]{3,2,1,0:T(8,128)}, f32[16,13,8,128]{3,2,1,0:T(8,128)S(1)}, u32[]{:S(2)}) copy-start(f32[16,13,8,128]{3,2,1,0:T(8,128)S(1)} %all_to_all.20.refs_4_) | copy-start | bytes 2555908
  203.8 24.3 %all-to-all-start.3 = ((f32[16,12,8,128]{3,2,1,0:T(8,128)}), f32[16,12,8,128]{3,2,1,0:T(8,128)S(1)}, u32[]{:S(2)}, u32[]{:S(2)}) async-start(f32[16,12,8,128]{3,2,1,0:T(8,128)} %get-tuple-element.16), calls=%async_computation.3 | async-start | bytes 1572864 | tf_op jit(solution)/shard_map/all_to_all | solution.py:423
  228.1 0.9 copy-start.1

commit v3 on v0

--- a/solution.py
+++ b/solution.py
@@ -1,15 +1,25 @@
+import functools
 import math
 
 import jax
 import jax.numpy as jnp
+import ml_dtypes
+import numpy as np
 from jax import lax
+from jax.experimental import pallas as pl
+from jax.experimental.pallas import tpu as pltpu
 from jax.sharding import PartitionSpec as P
 
 NIN = 512
 NFFT = 8192
+HALF = NFFT // 2
 BAND = 256
 BAND_START = 1536
 SPEC = 48
+FIRST = 16
+KB = 256
+LANES = 128
+MIB = 1 << 20
 
 
 def dft_table(length, first, width):
@@ -18,6 +28,19 @@
     phase_int = row_ids * chan_ids % length
     angles = phase_int.astype(jnp.float32) * (2.0 * math.pi / length)
     return jnp.concatenate([jnp.cos(angles), -jnp.sin(angles)], axis=1)
+
+
+def folded_table():
+    n = np.arange(HALF, dtype=np.int64)
+    tables = []
+    for parity in range(2):
+        chans = BAND_START + 2 * np.arange(BAND // 2, dtype=np.int64) + parity
+        angles = (n[:, None] * chans[None, :] % NFFT) * (2.0 * math.pi / NFFT)
+        full = np.concatenate([np.cos(angles), -np.sin(angles)], axis=1) / math.sqrt(NFFT)
+        high = full.astype(np.float32).astype(ml_dtypes.bfloat16)
+        low = (full - high.astype(np.float64)).astype(np.float32).astype(ml_dtypes.bfloat16)
+        tables.append(np.stack([high, low]))
+    return np.stack(tables)
 
 
 def slot_tables(owner_map, dropped_channels, capacity, slot_total):
@@ -66,7 +89,7 @@
     return jnp.stack([real_vis, imag_vis], axis=1)
 
 
-def local(samples, fir_taps, owner_map, dropped_channels):
+def local_plain(samples, fir_taps, owner_map, dropped_channels):
     devices = lax.axis_size("feed")
     capacity = BAND // devices + BAND // (2 * devices)
     slot_total = devices * capacity
@@ -96,9 +119,354 @@
     return (raw_vis * factor).astype(jnp.bfloat16)
 
 
+def split(value):
+    high = value.astype(jnp.bfloat16)
+    return high, (value - high.astype(jnp.float32)).astype(jnp.bfloat16)
+
+
+def spectra_kernel(count, parts, carry_in, taps, in_local, *refs):
+    row_ref, live_ref, taps_a, taps_b, frames_a, frames_b, table_a, table_b, table_last = refs[:9]
+    refs = refs[9:]
+    before, refs = refs[:carry_in], refs[carry_in:]
+    outs, refs = refs[: len(parts)], refs[len(parts) :]
+    power_out, even_0, odd_0, even_1, odd_1, acc, flat = refs
+    step = pl.program_id(0)
+    rows = count * in_local
+
+    def windowed(block, even, odd):
+        for tile in range(KB // LANES):
+            own = slice(tile * LANES, (tile + 1) * LANES)
+            lanes = slice(block * KB + tile * LANES, block * KB + (tile + 1) * LANES)
+            coef_a = [taps_a[t : t + 1, lanes] for t in range(taps)]
+            coef_b = [taps_b[t : t + 1, lanes] for t in range(taps)]
+            for first in range(0, in_local, 16):
+
+                def load(ref, f):
+                    return ref[f, first : first + 16, lanes].astype(jnp.float32)
+
+                held_a = [load(frames_a, f) for f in range(taps - 1)]
+                held_b = [load(frames_b, f) for f in range(taps - 1)]
+                for s in range(count):
+                    held_a.append(load(frames_a, s + taps - 1))
+                    held_b.append(load(frames_b, s + taps - 1))
+                    near = sum(c * x for c, x in zip(coef_a[1:], held_a[1:])) + coef_a[0] * held_a[0]
+                    far = sum(c * x for c, x in zip(coef_b[1:], held_b[1:])) + coef_b[0] * held_b[0]
+                    at = slice(s * in_local + first, s * in_local + first + 16)
+                    for ref, value in ((even, near + far), (odd, near - far)):
+                        high, low = split(value)
+                        ref[at, tile * LANES : (tile + 1) * LANES] = high
+                        ref[at, KB + tile * LANES : KB + (tile + 1) * LANES] = low
+                    held_a, held_b = held_a[1:], held_b[1:]
+
+    def multiply(table, even, odd):
+        for parity, ref in enumerate((even, odd)):
+            cols = slice(parity * BAND, (parity + 1) * BAND)
+            right = jnp.concatenate([table[parity, 0], table[parity, 0], table[parity, 1]], axis=0)
+            for start in range(0, rows, 256):
+                at = slice(start, start + 256)
+                left = jnp.concatenate([ref[at, :], ref[at, :KB]], axis=1)
+                acc[at, cols] += jnp.dot(left, right, preferred_element_type=jnp.float32)
+
+    @pl.when(step == 0)
+    def _():
+        even_1[...] = jnp.zeros_like(even_1)
+        odd_1[...] = jnp.zeros_like(odd_1)
+        acc[...] = jnp.zeros_like(acc)
+
+    multiply(table_b, even_1, odd_1)
+    windowed(0, even_0, odd_0)
+    multiply(table_a, even_0, odd_0)
+    windowed(1, even_1, odd_1)
+
+    @pl.when(step == pl.num_programs(0) - 1)
+    def _():
+        multiply(table_last, even_1, odd_1)
+        width = rows // LANES
+        for parity in range(2):
+            for part in range(2):
+                cols = slice(parity * BAND + part * LANES, parity * BAND + (part + 1) * LANES)
+                for g in range(width):
+                    turned = acc[g * LANES : (g + 1) * LANES, cols].T
+                    row = (parity * 2 + part) * width + g
+                    flat[pl.ds(row, LANES, stride=4 * width), :] = turned
+        size = 2 * width
+
+        def place(c, total):
+            value = flat[pl.ds(pl.multiple_of(c * size, size), size), :]
+            for p, out in enumerate(outs):
+                row = row_ref[p, c]
+
+                @pl.when(row >= 0)
+                def _(out=out, row=row):
+                    out[row] = value
+
+            square = sum(value[start : start + 8] ** 2 for start in range(0, size, 8))
+            return total + live_ref[c].astype(jnp.float32) * square
+
+        total = lax.fori_loop(0, BAND, place, jnp.zeros((8, LANES), jnp.float32), unroll=8)
+        for ref in before:
+            total = total + ref[...]
+        power_out[...] = total
+        for out, (low, high, extra) in zip(outs, parts):
+            if extra:
+                for d in range(out.shape[0] // (high - low + extra)):
+                    out[(d + 1) * (high - low + extra) - 1, :8] = total
+
+
+def spectra_call(first, count, parts, before, table, place, live, fir_taps, samples, devices):
+    _, in_local, _ = samples.shape
+    taps = fir_taps.shape[0]
+    step_size = 2 * KB
+    steps = HALF // step_size
+    owners, ranks = place
+    rows_of = [
+        jnp.where((ranks >= low) & (ranks < high), owners * (high - low + extra) + ranks - low, -1)
+        for low, high, extra in parts
+    ]
+
+    def frames_spec(offset):
+        return pl.BlockSpec(
+            (pl.Element(count + taps - 1), pl.Element(in_local), pl.Element(step_size)),
+            lambda j, *_: (first, 0, pl.multiple_of((j + offset) * step_size, step_size)),
+        )
+
+    def taps_spec(offset):
+        return pl.BlockSpec((taps, step_size), lambda j, *_: (0, j + offset))
+
+    def table_spec(index):
+        return pl.BlockSpec((2, 2, KB, BAND), lambda j, *_: (0, 0, index(j), 0))
+
+    rows = count * in_local
+    width = 2 * rows // LANES
+    shapes = [
+        jax.ShapeDtypeStruct((devices * (high - low + extra), width, LANES), jnp.float32)
+        for low, high, extra in parts
+    ]
+    shapes.append(jax.ShapeDtypeStruct((8, LANES), jnp.float32))
+    grid_spec = pltpu.PrefetchScalarGridSpec(
+        num_scalar_prefetch=2,
+        grid=(steps,),
+        in_specs=[
+            taps_spec(0),
+            taps_spec(steps),
+            frames_spec(0),
+            frames_spec(steps),
+            table_spec(lambda j: 2 * j),
+            table_spec(lambda j: jnp.maximum(2 * j - 1, 0)),
+            table_spec(lambda j: 2 * steps - 1),
+        ]
+        + [pl.BlockSpec((8, LANES), lambda j, *_: (0, 0))] * len(before),
+        out_specs=[pl.BlockSpec(s.shape, lambda j, *_, n=len(s.shape): (0,) * n) for s in shapes],
+        scratch_shapes=[pltpu.VMEM((rows, 2 * KB), jnp.bfloat16)] * 4
+        + [
+            pltpu.VMEM((rows, 2 * BAND), jnp.float32),
+            pltpu.VMEM((BAND * width, LANES), jnp.float32),
+        ],
+    )
+    *blocks, power = pl.pallas_call(
+        functools.partial(spectra_kernel, count, parts, len(before), taps, in_local),
+        out_shape=shapes,
+        grid_spec=grid_spec,
+        compiler_params=pltpu.CompilerParams(vmem_limit_bytes=60 * MIB),
+        cost_estimate=pl.CostEstimate(
+            flops=3 * 2 * rows * HALF * 2 * BAND, bytes_accessed=30 * MIB, transcendentals=0
+        ),
+        name="spectra",
+    )(
+        jnp.stack(rows_of),
+        live,
+        fir_taps,
+        fir_taps,
+        samples,
+        samples,
+        table,
+        table,
+        table,
+        *before,
+    )
+    return [block.reshape(devices, -1, width, LANES) for block in blocks], power
+
+
+def exchange_lanes(values, in_local):
+    count = len(values)
+    lane = lax.broadcasted_iota(jnp.int32, values[0].shape, 1) // in_local
+    values = list(values)
+    distance = count // 2
+    while distance:
+        upper = (lane & distance) != 0
+        shift = distance * in_local
+        for a in range(count):
+            if a & distance:
+                continue
+            x, y = values[a], values[a + distance]
+            values[a] = jnp.where(upper, pltpu.roll(y, shift, 1), x)
+            values[a + distance] = jnp.where(upper, y, pltpu.roll(x, LANES - shift, 1))
+        distance //= 2
+    return values
+
+
+def correlate_kernel(counts, slots, in_local, *refs):
+    factor_ref, used_ref = refs[:2]
+    groups = refs[2 : 2 + counts]
+    out = refs[-1 - 2 * slots]
+    scratch = refs[-2 * slots :]
+    per_tile = LANES // in_local
+    sources = groups[0].shape[0]
+    factor = factor_ref[0]
+    upper = lax.broadcasted_iota(jnp.int32, (8, LANES), 0) >= 4
+
+    def prepare(slot, left, right):
+        for block in range(sources // per_tile):
+            lanes = slice(block * LANES, (block + 1) * LANES)
+            straight, turned = [], []
+            for ref in groups:
+                width = ref.shape[2]
+                tiles = []
+                for start in range(0, width, 8):
+                    mixed = [
+                        ref[block * per_tile + a, slot, start : start + 8] for a in range(per_tile)
+                    ]
+                    tiles.append(exchange_lanes(mixed, in_local))
+                for q in range(per_tile):
+                    column = [t[q] for t in tiles]
+                    straight += column
+                    if len(column) == 1:
+                        swapped = pltpu.roll(column[0], 4, 0)
+                        turned.append(jnp.where(upper, -swapped, swapped))
+                    else:
+                        half = len(column) // 2
+                        turned += column[half:] + [-t for t in column[:half]]
+            pad = [jnp.zeros((LANES - 8 * len(straight), LANES), jnp.float32)]
+            columns = jnp.concatenate(straight + pad, axis=0)
+            rotated = jnp.concatenate(turned + pad, axis=0)
+            high, low = split(columns)
+            right[:LANES, lanes] = high
+            right[LANES : 2 * LANES, lanes] = high
+            right[2 * LANES :, lanes] = low
+            for part, value in enumerate((columns, rotated)):
+                high, low = split(value.T)
+                at = slice((part * sources // per_tile + block) * LANES, (part * sources // per_tile + block + 1) * LANES)
+                left[at, :LANES] = high
+                left[at, LANES : 2 * LANES] = low
+                left[at, 2 * LANES :] = high
+
+    def multiply(slot, left, right):
+        used = used_ref[pl.program_id(0) * slots + slot] != 0
+        nin = sources * in_local
+        for part in range(2):
+            for start in range(0, nin, 256):
+                total = jnp.dot(
+                    left[part * nin + start : part * nin + start + 256, :],
+                    right[...],
+                    preferred_element_type=jnp.float32,
+                )
+                total = jnp.where(used, total * factor, 0.0)
+                out[slot, part, start : start + 256, :] = total.astype(jnp.bfloat16)
+
+    for slot in range(slots):
+        prepare(slot, scratch[2 * slot], scratch[2 * slot + 1])
+        if slot:
+            multiply(slot - 1, scratch[2 * slot - 2], scratch[2 * slot - 1])
+    multiply(slots - 1, scratch[2 * slots - 2], scratch[2 * slots - 1])
+
+
+def correlate_call(received, low, high, capacity, used, factor, total, in_local, slots):
+    arrays = [r for r, _ in received]
+    sources = arrays[0].shape[0]
+    nin = sources * in_local
+    aliases = {}
+    extra, extra_specs = [], []
+    if total is not None:
+        extra, extra_specs = [total], [pl.BlockSpec(memory_space=pl.ANY)]
+        aliases = {2 + len(arrays): 0}
+    in_specs = [
+        pl.BlockSpec(memory_space=pltpu.SMEM),
+        pl.BlockSpec(memory_space=pltpu.SMEM),
+    ] + [
+        pl.BlockSpec(
+            (sources, slots, r.shape[2], LANES),
+            lambda s, d=(low - first) // slots: (0, s + d, 0, 0),
+        )
+        for r, first in received
+    ]
+    return pl.pallas_call(
+        functools.partial(correlate_kernel, len(arrays), slots, in_local),
+        out_shape=jax.ShapeDtypeStruct((capacity, 2, nin, nin), jnp.bfloat16),
+        grid=((high - low) // slots,),
+        in_specs=in_specs + extra_specs,
+        out_specs=pl.BlockSpec((slots, 2, nin, nin), lambda s: (s + low // slots, 0, 0, 0)),
+        scratch_shapes=[
+            pltpu.VMEM((2 * nin, 3 * LANES), jnp.bfloat16),
+            pltpu.VMEM((3 * LANES, nin), jnp.bfloat16),
+        ]
+        * slots,
+        input_output_aliases=aliases,
+        compiler_params=pltpu.CompilerParams(vmem_limit_bytes=60 * MIB),
+        cost_estimate=pl.CostEstimate(
+            flops=(high - low) * 8 * nin * nin * 256,
+            bytes_accessed=(high - low) * (4 * nin * nin + 8 * nin * SPEC),
+            transcendentals=0,
+        ),
+        name="correlate",
+    )(factor, used[low:high], *arrays, *extra)
+
+
+def exchange(block):
+    return lax.all_to_all(block, "feed", split_axis=0, concat_axis=0, tiled=True)
+
+
+def local_blocks(samples, fir_taps, owner_map, dropped_channels):
+    devices = lax.axis_size("feed")
+    capacity = BAND // devices + BAND // (2 * devices)
+    in_local = samples.shape[0]
+    frames = jnp.transpose(samples, (1, 0, 2))
+    owners = owner_map[:, 0]
+    channels = jnp.arange(BAND, dtype=jnp.int32)
+    same_owner = (owners[:, None] == owners[None, :]) & (channels[None, :] < channels[:, None])
+    ranks = jnp.sum(same_owner.astype(jnp.int32), axis=1)
+    live = jnp.logical_not(jnp.any(dropped_channels[None, :] == channels[:, None], axis=1))
+    kept = jnp.sum(live.astype(jnp.float32))
+    mine = (owners == lax.axis_index("feed")) & live
+    slots = jnp.arange(capacity, dtype=jnp.int32)
+    used = jnp.any((ranks[None, :] == slots[:, None]) & mine[None, :], axis=1).astype(jnp.int32)
+
+    table = jnp.asarray(folded_table())
+    middle = capacity * 3 // 4
+    live_flags = live.astype(jnp.int32)
+    call = functools.partial(
+        spectra_call,
+        table=table,
+        place=(owners, ranks),
+        live=live_flags,
+        fir_taps=fir_taps,
+        samples=frames,
+        devices=devices,
+    )
+    (block_a,), power = call(0, FIRST, ((0, capacity, 0),), [])
+    received_a = exchange(block_a)
+    (block_b, block_c), _ = call(
+        FIRST, SPEC - FIRST, ((0, middle, 1), (middle, capacity, 0)), [power]
+    )
+    block_b, received_a = lax.optimization_barrier((block_b, received_a))
+    received_b = exchange(block_b)
+    block_c, received_b = lax.optimization_barrier((block_c, received_b))
+    received_c = exchange(block_c)
+
+    power = jnp.sum(received_b[:, middle, :8])
+    mean_power = power / (NIN * SPEC * kept)
+    factor = jnp.reshape(1.0 / (SPEC * mean_power), (1,))
+    run = functools.partial(
+        correlate_call, capacity=capacity, used=used, factor=factor, in_local=in_local, slots=2
+    )
+    first = run([(received_a, 0), (received_b, 0)], 0, middle, total=None)
+    return run([(received_a, 0), (received_c, middle)], middle, capacity, total=first)
+
+
 def solution(mesh):
+    in_local = NIN // mesh.shape["feed"]
+    blocks = in_local * 4 == LANES
     return jax.shard_map(
-        local,
+        local_blocks if blocks else local_plain,
         mesh=mesh,
         in_specs=(P("feed", "grp", None), P(), P(), P("grp")),
         out_specs=P(("grp", "feed"), None, None, None),

time: 665 us -> 164 us (0.25)
  the two profiles are of different devices: /device:TPU:0 before, /device:TPU:13 now
where the time goes in v3:
time: 164 us; the launch traced here: 163 us
  Pallas kernels  79.5 us (48%)
  blocking collectives  61.9 us (38%)
  starting transfers between devices  11.7 us (7%)
  other arithmetic  6.94 us (4%)
    all_to_all x1, blocking collectives, exchange(): lax.all_to_all(block, 'feed', split_axis=0, concat_axis=0, tiled=True)  61.9 us
    pallas_call x2, Pallas kernels, spectra_call(): pl.pallas_call(functools.partial(spectra_kernel, count, parts, len(before...  56.3 us
    pallas_call x2, Pallas kernels, correlate_call(): pl.pallas_call(functools.partial(correlate_kernel, len(arrays), slots, in...  23.2 us
    all_to_all x2, starting transfers between devices, exchange(): lax.all_to_all(block, 'feed', split_axis=0, concat_axis=0, tiled=True)  11.7 us
  transfers between devices with their start and end apart: 2, of which 0 were waited for; matrix products, arithmetic and copies ran while one was open for 2% of the time, Pallas kernels for 32%

profile of v3, /device:TPU:13, one launch (start us, length us, event | category | flops | bytes accessed | tf_op | source)
XLA Modules:
  0.0 163.0 jit_solution(12312637173250685685)
XLA Ops:
  0.0 0.7 fusion.1
  0.7 0.9 convert_reduce_fusion
  1.7 1.3 and_select_fusion
  2.9 1.3 compare_and_fusion
  4.2 20.0 %spectra.2 = (f32[384,8,128]{2,1,0:T(8,128)}, f32[8,128]{1,0:T(8,128)}) custom-call(s32[1,256]{1,0:T(1,128)} %get-tuple-element.21.refs_0_, s32[256]{0:T(256)} %get-tuple-element.25.refs_1_, f32[4,8192]{1,0:T(4,128)} %refs_3_.3, f32[4,8192]{1,0:T(4,128)} %refs_3_.3, bf16[51,32,8192]{2,1,0:T(8,128)(2,1)} %bitcast.22, bf16[51,32,8192]{2,1,0:T(8,128)(2,1)} %bitcast.23, ...), custom_call_target="tpu_custom_call" | custom-call | flops 6442450944 | bytes 31457280 | tf_op jit(solution)/shard_map/spectra/pallas_call | solution.py:266
  24.2 6.6 %all-to-all-start = ((f32[16,24,8,128]{3,2,1,0:T(8,128)}), f32[16,24,8,128]{3,2,1,0:T(8,128)S(1)}, u32[]{:S(2)}, u32[]{:S(2)}) async-start(f32[16,24,8,128]{3,2,1,0:T(8,128)} %bitcast.27), calls=%async_computation | async-start | bytes 3145728 | tf_op jit(solution)/shard_map/all_to_all | solution.py:415
  30.8 0.6 pad_add_fusion.refs_0_
  31.4 36.3 %spectra.3 = (f32[304,16,128]{2,1,0:T(8,128)}, f32[96,16,128]{2,1,0:T(8,128)}, f32[8,128]{1,0:T(8,128)}) custom-call(s32[2,256]{1,0:T(2,128)} %pad_add_fusion.refs_0_, s32[256]{0:T(256)} %get-tuple-element.25.refs_1_, f32[4,8192]{1,0:T(4,128)} %refs_3_.3, f32[4,8192]{1,0:T(4,128)} %refs_3_.3, bf16[51,32,8192]{2,1,0:T(8,128)(2,1)} %bitcast.24, ...), custom_call_target="tpu_custom_call" | custom-call | flops 12884901888 | bytes 31457280 | tf_op jit(solution)/shard_map/spectra/pallas_call | solution.py:266
  67.6 0.0 all-to-all-done.refs_2_
  67.7 0.0 copy-start
  67.7 61.9 %all_to_all.15.refs_3_ = f32[16,19,16,128]{3,2,1,0:T(8,128)} all-to-all(f32[16,19,16,128]{3,2,1,0:T(8,128)} %bitcast.26), channel_id=1, replica_groups=mesh['grp'=2,'feed'=16] {'feed'}, dimensions={0} | all-to-all | bytes 4980736 | tf_op jit(solution)/shard_map/all_to_all | solution.py:415
  129.5 0.0 copy-done
  129.5 5.2 %all-to-all-start.2 = ((f32[16,6,16,128]{3,2,1,0:T(8,128)}), f32[16,6,16,128]{3,2,1,0:T(8,128)S(1)}, u32[]{:S(2)}, u32[]{:S(2)}) async-start(f32[16,6,16,128]{3,2,1,0:T(8,128)} %bitcast.6), calls=%async_computation.2 | async-start | bytes 1572864 | tf_op jit(solution)/shard_map/all_to_all | solution.py:415
  134.7 0.1 fusion.3
  134.8 0.0 copy-start.2
  134.8 0.7 slice.10.refs_1_
  135.5 0.6 convert_reduce_fusion.1
  136.7 1.5 slice_reduce_fusion
  138.9 0.0 copy-done.2
  138.9 16.2 %correlate.2.refs_4_ = bf16[24,2,512,512]{3,2,1,0:T(8,128)(2,1)} custom-call(f32[1]{0:T(128)} %bitcast.9.refs_0_, s32[18]{0:T(128)} %bitcast.31, f32[16,24,8,128]{3,2,1,0:T(8,128)} %copy-done, f32[16,19,16,128]{3,2,1,0:T(8,128)} %all_to_all.15.refs_3_), custom_call_target="tpu_custom_call" | custom-call | flops 9663676416 | bytes 22413312 | tf_op jit(solution)/shard_map/correlate/pallas_call | solution.py:392
  155.1 0.0 all-to-all-done.2.refs_3_
  155.1 0.0 copy-start.1
  155.1 0.9 copy-done.1
  156.0 7.0 %correlate.3 = bf16[24,2,512,512]{3,2,1,0:T(8,128)(2,1)} custom-call(f32[1]{0:T(128)} %bitcast.9.refs_0_, s32[6]{0:T(128)} %slice.10.refs_1_, f32[16,24,8,128]{3,2,1,0:T(8,128)} %copy-done, f32[16,6,16,128]{3,2,1,0:T(8,128)} %copy-done.1, bf16[24,2,512,512]{3,2,1,0:T(8,128)(2,1)} %correlate.2.refs_4_), custom_call_target="tpu_custom_call", output_to_operand_aliasing={{}: (4, {})} | custom-call | flops 3221225472 | bytes 7471104 | tf_op jit(solution)/shard_map/correlate/pallas_call | solution.py:392
  (1 shorter events, 0.0 us)
Async XLA Ops:
  24.2 43.4 %all-to-all-start = ((f32[16,24,8,128]{3,2,1,0:T(8,128)}), f32[16,24,8,128]{3,2,1,0:T(8,128)S(1)}, u32[]{:S(2)}, u32[]{:S(2)}) async-start(f32[16,24,8,128]{3,2,1,0:T(8,128)} %bitcast.27), calls=%async_computation | async-start | bytes 3145728 | tf_op jit(solution)/shard_map/all_to_all | solution.py:415
  67.7 61.9 %copy-start = (f32[16,24,8,128]{3,2,1,0:T(8,128)}, f32[16,24,8,128]{3,2,1,0:T(8,128)S(1)}, u32[]{:S(2)}) copy-start(f32[16,24,8,128]{3,2,1,0:T(8,128)S(1)} %all-to-all-done.refs_2_) | copy-start | bytes 4718596
  129.5 25.6 %all-to-all-start.2 = ((f32[16,6,16,128]{3,2,1,0:T(8,128)}), f32[16,6,16,128]{3,2,1,0:T(8,128)S(1)}, u32[]{:S(2)}, u32[]{:S(2)}) async-start(f32[16,6,16,128]{3,2,1,0:T(8,128)} %bitcast.6), calls=%async_computation.2 | async-start | bytes 1572864 | tf_op jit(solution)/shard_map/all_to_all | solution.py:415
  134.8 4.1 %copy-start.2 = (s32[24]{0:T(128)}, s32[24]{0:T(128)S(1)}, u32[]{:S(2)}) copy-start(s32[24]{0:T(128)S(1)} %convert_element_type.15) | copy-start | bytes 292
  155.1 0.9 copy-start.1

commit v4 on v3

--- a/solution.py
+++ b/solution.py
@@ -124,12 +124,13 @@
     return high, (value - high.astype(jnp.float32)).astype(jnp.bfloat16)
 
 
-def spectra_kernel(count, parts, carry_in, taps, in_local, *refs):
-    row_ref, live_ref, taps_a, taps_b, frames_a, frames_b, table_a, table_b, table_last = refs[:9]
-    refs = refs[9:]
-    before, refs = refs[:carry_in], refs[carry_in:]
-    outs, refs = refs[: len(parts)], refs[len(parts) :]
-    power_out, even_0, odd_0, even_1, odd_1, acc, flat = refs
+def spectra_kernel(count, last, devices, message, taps, in_local, *refs):
+    row_ref, taps_a, taps_b, frames_a, frames_b, table_a, table_b, table_last = refs[:8]
+    if last:
+        before, out = refs[8:10]
+    else:
+        out, power_out = refs[8:10]
+    even_0, odd_0, even_1, odd_1, acc, flat = refs[10:]
     step = pl.program_id(0)
     rows = count * in_local
 
@@ -162,8 +163,8 @@
         for parity, ref in enumerate((even, odd)):
             cols = slice(parity * BAND, (parity + 1) * BAND)
             right = jnp.concatenate([table[parity, 0], table[parity, 0], table[parity, 1]], axis=0)
-            for start in range(0, rows, 256):
-                at = slice(start, start + 256)
+            for start in range(0, rows, 512):
+                at = slice(start, start + 512)
                 left = jnp.concatenate([ref[at, :], ref[at, :KB]], axis=1)
                 acc[at, cols] += jnp.dot(left, right, preferred_element_type=jnp.float32)
 
@@ -193,36 +194,35 @@
 
         def place(c, total):
             value = flat[pl.ds(pl.multiple_of(c * size, size), size), :]
-            for p, out in enumerate(outs):
-                row = row_ref[p, c]
-
-                @pl.when(row >= 0)
-                def _(out=out, row=row):
-                    out[row] = value
+            row = row_ref[c]
+
+            @pl.when(row >= 0)
+            def _():
+                out[pl.ds(pl.multiple_of(row * 8, 8), size), :] = value
 
             square = sum(value[start : start + 8] ** 2 for start in range(0, size, 8))
-            return total + live_ref[c].astype(jnp.float32) * square
+            return total + (row >= 0).astype(jnp.float32) * square
 
         total = lax.fori_loop(0, BAND, place, jnp.zeros((8, LANES), jnp.float32), unroll=8)
-        for ref in before:
-            total = total + ref[...]
-        power_out[...] = total
-        for out, (low, high, extra) in zip(outs, parts):
-            if extra:
-                for d in range(out.shape[0] // (high - low + extra)):
-                    out[(d + 1) * (high - low + extra) - 1, :8] = total
-
-
-def spectra_call(first, count, parts, before, table, place, live, fir_taps, samples, devices):
+        if last:
+            total = total + before[...]
+            for d in range(devices):
+                out[(d + 1) * message - 8 : (d + 1) * message, :] = total
+        else:
+            power_out[...] = total
+
+
+def spectra_call(first, count, before, table, owners, ranks, dead, fir_taps, samples, devices):
     _, in_local, _ = samples.shape
     taps = fir_taps.shape[0]
     step_size = 2 * KB
     steps = HALF // step_size
-    owners, ranks = place
-    rows_of = [
-        jnp.where((ranks >= low) & (ranks < high), owners * (high - low + extra) + ranks - low, -1)
-        for low, high, extra in parts
-    ]
+    last = before is not None
+    rows = count * in_local
+    width = 2 * rows // LANES
+    capacity = BAND // devices + BAND // (2 * devices)
+    message = capacity * width + 8 * last
+    row_of = jnp.where(dead, -1, owners * (message // 8) + ranks * (width // 8))
 
     def frames_spec(offset):
         return pl.BlockSpec(
@@ -236,15 +236,12 @@
     def table_spec(index):
         return pl.BlockSpec((2, 2, KB, BAND), lambda j, *_: (0, 0, index(j), 0))
 
-    rows = count * in_local
-    width = 2 * rows // LANES
-    shapes = [
-        jax.ShapeDtypeStruct((devices * (high - low + extra), width, LANES), jnp.float32)
-        for low, high, extra in parts
-    ]
-    shapes.append(jax.ShapeDtypeStruct((8, LANES), jnp.float32))
+    block = jax.ShapeDtypeStruct((devices * message, LANES), jnp.float32)
+    power = jax.ShapeDtypeStruct((8, LANES), jnp.float32)
+    whole = [pl.BlockSpec(block.shape, lambda j, *_: (0, 0))]
+    single = [pl.BlockSpec(power.shape, lambda j, *_: (0, 0))]
     grid_spec = pltpu.PrefetchScalarGridSpec(
-        num_scalar_prefetch=2,
+        num_scalar_prefetch=1,
         grid=(steps,),
         in_specs=[
             taps_spec(0),
@@ -255,17 +252,17 @@
             table_spec(lambda j: jnp.maximum(2 * j - 1, 0)),
             table_spec(lambda j: 2 * steps - 1),
         ]
-        + [pl.BlockSpec((8, LANES), lambda j, *_: (0, 0))] * len(before),
-        out_specs=[pl.BlockSpec(s.shape, lambda j, *_, n=len(s.shape): (0,) * n) for s in shapes],
+        + (single if last else []),
+        out_specs=whole + ([] if last else single),
         scratch_shapes=[pltpu.VMEM((rows, 2 * KB), jnp.bfloat16)] * 4
         + [
             pltpu.VMEM((rows, 2 * BAND), jnp.float32),
             pltpu.VMEM((BAND * width, LANES), jnp.float32),
         ],
     )
-    *blocks, power = pl.pallas_call(
-        functools.partial(spectra_kernel, count, parts, len(before), taps, in_local),
-        out_shape=shapes,
+    sent, *rest = pl.pallas_call(
+        functools.partial(spectra_kernel, count, last, devices, message, taps, in_local),
+        out_shape=[block] + ([] if last else [power]),
         grid_spec=grid_spec,
         compiler_params=pltpu.CompilerParams(vmem_limit_bytes=60 * MIB),
         cost_estimate=pl.CostEstimate(
@@ -273,8 +270,7 @@
         ),
         name="spectra",
     )(
-        jnp.stack(rows_of),
-        live,
+        row_of,
         fir_taps,
         fir_taps,
         samples,
@@ -282,9 +278,9 @@
         table,
         table,
         table,
-        *before,
-    )
-    return [block.reshape(devices, -1, width, LANES) for block in blocks], power
+        *([before] if last else []),
+    )
+    return [sent.reshape(devices, message, LANES)] + rest
 
 
 def exchange_lanes(values, in_local):
@@ -305,11 +301,10 @@
     return values
 
 
-def correlate_kernel(counts, slots, in_local, *refs):
-    factor_ref, used_ref = refs[:2]
-    groups = refs[2 : 2 + counts]
-    out = refs[-1 - 2 * slots]
-    scratch = refs[-2 * slots :]
+def correlate_kernel(widths, slots, in_local, factor_ref, used_ref, *refs):
+    groups = refs[: len(widths)]
+    out = refs[len(widths)]
+    scratch = refs[len(widths) + 1 :]
     per_tile = LANES // in_local
     sources = groups[0].shape[0]
     factor = factor_ref[0]
@@ -319,12 +314,11 @@
         for block in range(sources // per_tile):
             lanes = slice(block * LANES, (block + 1) * LANES)
             straight, turned = [], []
-            for ref in groups:
-                width = ref.shape[2]
+            for ref, width in zip(groups, widths):
                 tiles = []
-                for start in range(0, width, 8):
+                for start in range(slot * width, (slot + 1) * width, 8):
                     mixed = [
-                        ref[block * per_tile + a, slot, start : start + 8] for a in range(per_tile)
+                        ref[block * per_tile + a, start : start + 8] for a in range(per_tile)
                     ]
                     tiles.append(exchange_lanes(mixed, in_local))
                 for q in range(per_tile):
@@ -354,14 +348,13 @@
         used = used_ref[pl.program_id(0) * slots + slot] != 0
         nin = sources * in_local
         for part in range(2):
-            for start in range(0, nin, 256):
-                total = jnp.dot(
-                    left[part * nin + start : part * nin + start + 256, :],
-                    right[...],
-                    preferred_element_type=jnp.float32,
-                )
-                total = jnp.where(used, total * factor, 0.0)
-                out[slot, part, start : start + 256, :] = total.astype(jnp.bfloat16)
+            total = jnp.dot(
+                left[part * nin : (part + 1) * nin, :],
+                right[...],
+                preferred_element_type=jnp.float32,
+            )
+            total = jnp.where(used, total * factor, 0.0)
+            out[slot, part] = total.astype(jnp.bfloat16)
 
     for slot in range(slots):
         prepare(slot, scratch[2 * slot], scratch[2 * slot + 1])
@@ -370,96 +363,80 @@
     multiply(slots - 1, scratch[2 * slots - 2], scratch[2 * slots - 1])
 
 
-def correlate_call(received, low, high, capacity, used, factor, total, in_local, slots):
-    arrays = [r for r, _ in received]
-    sources = arrays[0].shape[0]
+def correlate_call(received, widths, capacity, used, factor, in_local, slots):
+    sources = received[0].shape[0]
     nin = sources * in_local
-    aliases = {}
-    extra, extra_specs = [], []
-    if total is not None:
-        extra, extra_specs = [total], [pl.BlockSpec(memory_space=pl.ANY)]
-        aliases = {2 + len(arrays): 0}
     in_specs = [
         pl.BlockSpec(memory_space=pltpu.SMEM),
         pl.BlockSpec(memory_space=pltpu.SMEM),
-    ] + [
-        pl.BlockSpec(
-            (sources, slots, r.shape[2], LANES),
-            lambda s, d=(low - first) // slots: (0, s + d, 0, 0),
-        )
-        for r, first in received
-    ]
+    ] + [pl.BlockSpec((sources, slots * width, LANES), lambda s: (0, s, 0)) for width in widths]
     return pl.pallas_call(
-        functools.partial(correlate_kernel, len(arrays), slots, in_local),
+        functools.partial(correlate_kernel, widths, slots, in_local),
         out_shape=jax.ShapeDtypeStruct((capacity, 2, nin, nin), jnp.bfloat16),
-        grid=((high - low) // slots,),
-        in_specs=in_specs + extra_specs,
-        out_specs=pl.BlockSpec((slots, 2, nin, nin), lambda s: (s + low // slots, 0, 0, 0)),
+        grid=(capacity // slots,),
+        in_specs=in_specs,
+        out_specs=pl.BlockSpec((slots, 2, nin, nin), lambda s: (s, 0, 0, 0)),
         scratch_shapes=[
             pltpu.VMEM((2 * nin, 3 * LANES), jnp.bfloat16),
             pltpu.VMEM((3 * LANES, nin), jnp.bfloat16),
         ]
         * slots,
-        input_output_aliases=aliases,
         compiler_params=pltpu.CompilerParams(vmem_limit_bytes=60 * MIB),
         cost_estimate=pl.CostEstimate(
-            flops=(high - low) * 8 * nin * nin * 256,
-            bytes_accessed=(high - low) * (4 * nin * nin + 8 * nin * SPEC),
+            flops=capacity * 8 * nin * nin * 256,
+            bytes_accessed=capacity * (4 * nin * nin + 8 * nin * SPEC),
             transcendentals=0,
         ),
         name="correlate",
-    )(factor, used[low:high], *arrays, *extra)
+    )(factor, used, *received)
 
 
 def exchange(block):
     return lax.all_to_all(block, "feed", split_axis=0, concat_axis=0, tiled=True)
+
+
+def channel_tables(owners, dropped_channels):
+    channels = jnp.arange(BAND, dtype=jnp.int32)[:, None]
+    names = jnp.concatenate([owners, dropped_channels])[None, :]
+    entry = jnp.arange(names.shape[1], dtype=jnp.int32)[None, :]
+    earlier = (entry < channels) & (names == owners[:, None])
+    flagged = (entry >= BAND) & (names == channels)
+    total = jnp.sum(jnp.where(flagged, BAND, earlier.astype(jnp.int32)), axis=1)
+    return total % BAND, total >= BAND
 
 
 def local_blocks(samples, fir_taps, owner_map, dropped_channels):
     devices = lax.axis_size("feed")
     capacity = BAND // devices + BAND // (2 * devices)
     in_local = samples.shape[0]
-    frames = jnp.transpose(samples, (1, 0, 2))
     owners = owner_map[:, 0]
-    channels = jnp.arange(BAND, dtype=jnp.int32)
-    same_owner = (owners[:, None] == owners[None, :]) & (channels[None, :] < channels[:, None])
-    ranks = jnp.sum(same_owner.astype(jnp.int32), axis=1)
-    live = jnp.logical_not(jnp.any(dropped_channels[None, :] == channels[:, None], axis=1))
-    kept = jnp.sum(live.astype(jnp.float32))
-    mine = (owners == lax.axis_index("feed")) & live
+    ranks, dead = channel_tables(owners, dropped_channels)
+    call = functools.partial(
+        spectra_call,
+        table=jnp.asarray(folded_table()),
+        owners=owners,
+        ranks=ranks,
+        dead=dead,
+        fir_taps=fir_taps,
+        samples=jnp.transpose(samples, (1, 0, 2)),
+        devices=devices,
+    )
+    block_a, power = call(0, FIRST, None)
+    received_a = exchange(block_a)
+    (block_b,) = call(FIRST, SPEC - FIRST, power)
+    block_b, received_a = lax.optimization_barrier((block_b, received_a))
+    received_b = exchange(block_b)
+
+    kept = jnp.sum(jnp.logical_not(dead).astype(jnp.float32))
+    mine = (owners == lax.axis_index("feed")) & jnp.logical_not(dead)
     slots = jnp.arange(capacity, dtype=jnp.int32)
     used = jnp.any((ranks[None, :] == slots[:, None]) & mine[None, :], axis=1).astype(jnp.int32)
-
-    table = jnp.asarray(folded_table())
-    middle = capacity * 3 // 4
-    live_flags = live.astype(jnp.int32)
-    call = functools.partial(
-        spectra_call,
-        table=table,
-        place=(owners, ranks),
-        live=live_flags,
-        fir_taps=fir_taps,
-        samples=frames,
-        devices=devices,
-    )
-    (block_a,), power = call(0, FIRST, ((0, capacity, 0),), [])
-    received_a = exchange(block_a)
-    (block_b, block_c), _ = call(
-        FIRST, SPEC - FIRST, ((0, middle, 1), (middle, capacity, 0)), [power]
-    )
-    block_b, received_a = lax.optimization_barrier((block_b, received_a))
-    received_b = exchange(block_b)
-    block_c, received_b = lax.optimization_barrier((block_c, received_b))
-    received_c = exchange(block_c)
-
-    power = jnp.sum(received_b[:, middle, :8])
-    mean_power = power / (NIN * SPEC * kept)
+    mean_power = jnp.sum(received_b[:, -8:]) / (NIN * SPEC * kept)
     factor = jnp.reshape(1.0 / (SPEC * mean_power), (1,))
-    run = functools.partial(
-        correlate_call, capacity=capacity, used=used, factor=factor, in_local=in_local, slots=2
-    )
-    first = run([(received_a, 0), (received_b, 0)], 0, middle, total=None)
-    return run([(received_a, 0), (received_c, middle)], middle, capacity, total=first)
+    widths = [block.shape[1] // capacity for block in (block_a, block_b)]
+    return correlate_call(
+        [received_a, received_b], widths, capacity, used, factor, in_local, slots=2
+    )
 
 
 def solution(mesh):

time: 164 us -> 167 us (1.018)
  waiting for transfers between devices: 0.01 us -> 70.6 us
  blocking collectives: 61.9 us -> 0 us
  Pallas kernels: 79.5 us -> 75.4 us
    all_to_all x2, waiting for transfers between devices: 0.01 us -> 70.6 us  [exchange(): lax.all_to_all(block, 'feed', split_axis=0, concat_axis=0, tiled=True)]
    all_to_all x1 -> x0, blocking collectives: 61.9 us -> none  [exchange(): lax.all_to_all(block, 'feed', split_axis=0, concat_axis=0, tiled=True)]
    pallas_call x4 -> x3, Pallas kernels: 79.5 us -> 75.4 us  [the longest x2 54.6 us: spectra_call(): pl.pallas_call(functools.partial(spectra_kernel, count, last, devices, me...]
  transfers between devices with their start and end apart: 2 -> 2, of which waited for: 0 -> 2; matrix products, arithmetic and copies ran while one was open for 2% -> 1% of each run, Pallas kernels for 32% -> 21%
where the time goes in v4:
time: 167 us; the launch traced here: 166 us
  Pallas kernels  75.4 us (45%)
  waiting for transfers between devices  70.6 us (42%)
  starting transfers between devices  11.5 us (7%)
  other arithmetic  6.15 us (4%)
    all_to_all x2, waiting for transfers between devices, exchange(): lax.all_to_all(block, 'feed', split_axis=0, concat_axis=0, tiled=True)  70.6 us
    pallas_call x2, Pallas kernels, spectra_call(): pl.pallas_call(functools.partial(spectra_kernel, count, last, devices, me...  54.6 us
    pallas_call x1, Pallas kernels, correlate_call(): pl.pallas_call(functools.partial(correlate_kernel, widths, slots, in_loca...  20.8 us
    all_to_all x2, starting transfers between devices, exchange(): lax.all_to_all(block, 'feed', split_axis=0, concat_axis=0, tiled=True)  11.5 us
  transfers between devices with their start and end apart: 2, of which 2 were waited for; matrix products, arithmetic and copies ran while one was open for 1% of the time, Pallas kernels for 21%

profile of v4, /device:TPU:13, one launch (start us, length us, event | category | flops | bytes accessed | tf_op | source)
XLA Modules:
  0.0 166.4 jit_solution(17600288713530258666)
XLA Ops:
  0.0 0.7 pad_add_fusion
  0.7 0.8 select_reduce_fusion
  1.5 0.7 compare_and_fusion
  2.2 1.2 add_select_fusion
  3.5 0.0 copy-start.2
  3.5 20.4 %spectra.2 = (f32[3072,128]{1,0:T(8,128)}, f32[8,128]{1,0:T(8,128)}) custom-call(s32[256]{0:T(256)} %get-tuple-element.15.refs_0_, f32[4,8192]{1,0:T(4,128)} %refs_2_.3, f32[4,8192]{1,0:T(4,128)} %refs_2_.3, bf16[51,32,8192]{2,1,0:T(8,128)(2,1)} %bitcast.5, bf16[51,32,8192]{2,1,0:T(8,128)(2,1)} %bitcast.6, ...), custom_call_target="tpu_custom_call" | custom-call | flops 6442450944 | bytes 31457280 | tf_op jit(solution)/shard_map/spectra/pallas_call | solution.py:263
  23.9 6.6 %all-to-all-start = ((f32[16,192,128]{2,1,0:T(8,128)}), f32[16,192,128]{2,1,0:T(8,128)S(1)}, u32[]{:S(2)}, u32[]{:S(2)}) async-start(f32[16,192,128]{2,1,0:T(8,128)} %bitcast.10), calls=%async_computation | async-start | bytes 3145728 | tf_op jit(solution)/shard_map/all_to_all | solution.py:395
  30.5 0.0 copy-done.2
  30.5 0.6 add_select_fusion.1.refs_0_
  31.0 34.2 %spectra.3 = f32[6272,128]{1,0:T(8,128)} custom-call(s32[256]{0:T(256)} %add_select_fusion.1.refs_0_, f32[4,8192]{1,0:T(4,128)} %refs_2_.3, f32[4,8192]{1,0:T(4,128)} %refs_2_.3, bf16[51,32,8192]{2,1,0:T(8,128)(2,1)} %bitcast.7, bf16[51,32,8192]{2,1,0:T(8,128)(2,1)} %bitcast.8, bf16[2,2,4096,256]{3,2,1,0:T(8,128)(2,1)} %constant.44.clone.refs_5_.refs_6_.refs_7_, ...), custom_call_target="tpu_custom_call" | custom-call | flops 12884901888 | bytes 31457280 | tf_op jit(solution)/shard_map/spectra/pallas_call | solution.py:263
  65.2 1.4 all-to-all-done.refs_0_
  66.6 0.0 copy-start.1
  66.6 1.1 copy-done.1
  67.8 4.9 %all-to-all-start.1 = ((f32[16,392,128]{2,1,0:T(8,128)}), f32[16,392,128]{2,1,0:T(8,128)S(1)}, u32[]{:S(2)}, u32[]{:S(2)}) async-start(f32[16,392,128]{2,1,0:T(8,128)} %bitcast.9), calls=%async_computation.1 | async-start | bytes 6422528 | tf_op jit(solution)/shard_map/all_to_all | solution.py:395
  72.7 0.1 fusion.3
  72.8 0.6 convert_element_type.11.used_ref
  73.4 0.7 fusion.4
  74.8 69.2 %all-to-all-done.1.refs_1_ = f32[16,392,128]{2,1,0:T(8,128)S(1)} async-done(((f32[16,392,128]{2,1,0:T(8,128)}), f32[16,392,128]{2,1,0:T(8,128)S(1)}, u32[]{:S(2)}, u32[]{:S(2)}) %all-to-all-start.1) | async-done | bytes 3211296 | tf_op jit(solution)/shard_map/all_to_all | solution.py:395
  144.0 0.0 copy-start
  144.0 0.7 slice_reduce_fusion
  145.5 0.2 copy-done
  145.7 20.8 %correlate.1 = bf16[24,2,512,512]{3,2,1,0:T(8,128)(2,1)} custom-call(f32[1]{0:T(128)} %bitcast.4.factor_ref, s32[24]{0:T(128)} %convert_element_type.11.used_ref, f32[16,192,128]{2,1,0:T(8,128)} %copy-done.1, f32[16,392,128]{2,1,0:T(8,128)} %copy-done), custom_call_target="tpu_custom_call" | custom-call | flops 12884901888 | bytes 29884416 | tf_op jit(solution)/shard_map/correlate/pallas_call | solution.py:373
  (1 shorter events, 0.0 us)
Async XLA Ops:
  3.5 27.0 %copy-start.2 = (s32[256,1]{0,1:T(1,128)S(1)}, s32[256,1]{0,1:T(1,128)}, u32[]{:S(2)}) copy-start(s32[256,1]{0,1:T(1,128)} %param.7) | copy-start | bytes 3076
  23.9 42.7 %all-to-all-start = ((f32[16,192,128]{2,1,0:T(8,128)}), f32[16,192,128]{2,1,0:T(8,128)S(1)}, u32[]{:S(2)}, u32[]{:S(2)}) async-start(f32[16,192,128]{2,1,0:T(8,128)} %bitcast.10), calls=%async_computation | async-start | bytes 3145728 | tf_op jit(solution)/shard_map/all_to_all | solution.py:395
  66.6 1.2 copy-start.1
  67.8 76.2 %all-to-all-start.1 = ((f32[16,392,128]{2,1,0:T(8,128)}), f32[16,392,128]{2,1,0:T(8,128)S(1)}, u32[]{:S(2)}, u32[]{:S(2)}) async-start(f32[16,392,128]{2,1,0:T(8,128)} %bitcast.9), calls=%async_computation.1 | async-start | bytes 6422528 | tf_op jit(solution)/shard_map/all_to_all | solution.py:395
  144.0 1.7 %copy-start = (f32[16,392,128]{2,1,0:T(8,128)}, f32[16,392,128]{2,1,0:T(8,128)S(1)}, u32[]{:S(2)}) copy-start(f32[16,392,128]{2,1,0:T(8,128)S(1)} %all-to-all-done.1.refs_1_) | copy-start | bytes 9633796

commit v5 on v4

--- a/solution.py
+++ b/solution.py
@@ -134,9 +134,7 @@
     step = pl.program_id(0)
     rows = count * in_local
 
-    def windowed(block, even, odd):
-        for tile in range(KB // LANES):
-            own = slice(tile * LANES, (tile + 1) * LANES)
+    def window_piece(block, tile, begin, even, odd):
             lanes = slice(block * KB + tile * LANES, block * KB + (tile + 1) * LANES)
             coef_a = [taps_a[t : t + 1, lanes] for t in range(taps)]
             coef_b = [taps_b[t : t + 1, lanes] for t in range(taps)]
@@ -145,9 +143,9 @@
                 def load(ref, f):
                     return ref[f, first : first + 16, lanes].astype(jnp.float32)
 
-                held_a = [load(frames_a, f) for f in range(taps - 1)]
-                held_b = [load(frames_b, f) for f in range(taps - 1)]
-                for s in range(count):
+                held_a = [load(frames_a, begin + f) for f in range(taps - 1)]
+                held_b = [load(frames_b, begin + f) for f in range(taps - 1)]
+                for s in range(begin, begin + 8):
                     held_a.append(load(frames_a, s + taps - 1))
                     held_b.append(load(frames_b, s + taps - 1))
                     near = sum(c * x for c, x in zip(coef_a[1:], held_a[1:])) + coef_a[0] * held_a[0]
@@ -159,14 +157,31 @@
                         ref[at, KB + tile * LANES : KB + (tile + 1) * LANES] = low
                     held_a, held_b = held_a[1:], held_b[1:]
 
-    def multiply(table, even, odd):
-        for parity, ref in enumerate((even, odd)):
-            cols = slice(parity * BAND, (parity + 1) * BAND)
-            right = jnp.concatenate([table[parity, 0], table[parity, 0], table[parity, 1]], axis=0)
-            for start in range(0, rows, 512):
-                at = slice(start, start + 512)
-                left = jnp.concatenate([ref[at, :], ref[at, :KB]], axis=1)
-                acc[at, cols] += jnp.dot(left, right, preferred_element_type=jnp.float32)
+    def matmul_piece(table, parity, start, ref):
+        cols = slice(parity * BAND, (parity + 1) * BAND)
+        at = slice(start, start + 256)
+        right = jnp.concatenate([table[parity, 0], table[parity, 0], table[parity, 1]], axis=0)
+        left = jnp.concatenate([ref[at, :], ref[at, :KB]], axis=1)
+        acc[at, cols] += jnp.dot(left, right, preferred_element_type=jnp.float32)
+
+    def matmul_pieces(table, even, odd):
+        return [
+            functools.partial(matmul_piece, table, parity, start, ref)
+            for parity, ref in enumerate((even, odd))
+            for start in range(0, rows, 256)
+        ]
+
+    def window_pieces(block, even, odd):
+        return [
+            functools.partial(window_piece, block, tile, begin, even, odd)
+            for tile in range(KB // LANES)
+            for begin in range(0, count, 8)
+        ]
+
+    def alternate(left, right):
+        for one, other in zip(left, right, strict=True):
+            one()
+            other()
 
     @pl.when(step == 0)
     def _():
@@ -174,14 +189,13 @@
         odd_1[...] = jnp.zeros_like(odd_1)
         acc[...] = jnp.zeros_like(acc)
 
-    multiply(table_b, even_1, odd_1)
-    windowed(0, even_0, odd_0)
-    multiply(table_a, even_0, odd_0)
-    windowed(1, even_1, odd_1)
+    alternate(matmul_pieces(table_b, even_1, odd_1), window_pieces(0, even_0, odd_0))
+    alternate(matmul_pieces(table_a, even_0, odd_0), window_pieces(1, even_1, odd_1))
 
     @pl.when(step == pl.num_programs(0) - 1)
     def _():
-        multiply(table_last, even_1, odd_1)
+        for piece in matmul_pieces(table_last, even_1, odd_1):
+            piece()
         width = rows // LANES
         for parity in range(2):
             for part in range(2):
@@ -301,86 +315,113 @@
     return values
 
 
-def correlate_kernel(widths, slots, in_local, factor_ref, used_ref, *refs):
+def correlate_kernel(widths, in_local, factor_ref, used_ref, *refs):
     groups = refs[: len(widths)]
-    out = refs[len(widths)]
-    scratch = refs[len(widths) + 1 :]
+    out, left_0, right_0, left_1, right_1, staged, sems = refs[len(widths) :]
+    step, last = pl.program_id(0), pl.num_programs(0) - 1
     per_tile = LANES // in_local
-    sources = groups[0].shape[0]
+    blocks = groups[0].shape[0] // per_tile
+    nin = groups[0].shape[0] * in_local
     factor = factor_ref[0]
     upper = lax.broadcasted_iota(jnp.int32, (8, LANES), 0) >= 4
 
-    def prepare(slot, left, right):
-        for block in range(sources // per_tile):
-            lanes = slice(block * LANES, (block + 1) * LANES)
-            straight, turned = [], []
-            for ref, width in zip(groups, widths):
-                tiles = []
-                for start in range(slot * width, (slot + 1) * width, 8):
-                    mixed = [
-                        ref[block * per_tile + a, start : start + 8] for a in range(per_tile)
-                    ]
-                    tiles.append(exchange_lanes(mixed, in_local))
-                for q in range(per_tile):
-                    column = [t[q] for t in tiles]
-                    straight += column
-                    if len(column) == 1:
-                        swapped = pltpu.roll(column[0], 4, 0)
-                        turned.append(jnp.where(upper, -swapped, swapped))
-                    else:
-                        half = len(column) // 2
-                        turned += column[half:] + [-t for t in column[:half]]
-            pad = [jnp.zeros((LANES - 8 * len(straight), LANES), jnp.float32)]
-            columns = jnp.concatenate(straight + pad, axis=0)
-            rotated = jnp.concatenate(turned + pad, axis=0)
-            high, low = split(columns)
+    def prepare(slot, left, right, block):
+        used = used_ref[2 * step + slot] != 0
+        straight, turned = [], []
+        for ref, width in zip(groups, widths):
+            tiles = []
+            for start in range(slot * width, (slot + 1) * width, 8):
+                mixed = [
+                    jnp.where(used, ref[block * per_tile + a, start : start + 8], 0.0)
+                    for a in range(per_tile)
+                ]
+                tiles.append(exchange_lanes(mixed, in_local))
+            for q in range(per_tile):
+                column = [t[q] for t in tiles]
+                straight += column
+                if len(column) == 1:
+                    swapped = pltpu.roll(column[0], 4, 0)
+                    turned.append(jnp.where(upper, swapped, -swapped))
+                else:
+                    half = len(column) // 2
+                    turned += [-t for t in column[half:]] + column[:half]
+        pad = [jnp.zeros((LANES - 8 * len(straight), LANES), jnp.float32)]
+        columns = jnp.concatenate(straight + pad, axis=0)
+        for part, value in enumerate((columns, jnp.concatenate(turned + pad, axis=0))):
+            high, low = split(value)
+            lanes = slice(part * nin + block * LANES, part * nin + (block + 1) * LANES)
             right[:LANES, lanes] = high
             right[LANES : 2 * LANES, lanes] = high
             right[2 * LANES :, lanes] = low
-            for part, value in enumerate((columns, rotated)):
-                high, low = split(value.T)
-                at = slice((part * sources // per_tile + block) * LANES, (part * sources // per_tile + block + 1) * LANES)
-                left[at, :LANES] = high
-                left[at, LANES : 2 * LANES] = low
-                left[at, 2 * LANES :] = high
-
-    def multiply(slot, left, right):
-        used = used_ref[pl.program_id(0) * slots + slot] != 0
-        nin = sources * in_local
-        for part in range(2):
-            total = jnp.dot(
-                left[part * nin : (part + 1) * nin, :],
-                right[...],
-                preferred_element_type=jnp.float32,
-            )
-            total = jnp.where(used, total * factor, 0.0)
-            out[slot, part] = total.astype(jnp.bfloat16)
-
-    for slot in range(slots):
-        prepare(slot, scratch[2 * slot], scratch[2 * slot + 1])
-        if slot:
-            multiply(slot - 1, scratch[2 * slot - 2], scratch[2 * slot - 1])
-    multiply(slots - 1, scratch[2 * slots - 2], scratch[2 * slots - 1])
-
-
-def correlate_call(received, widths, capacity, used, factor, in_local, slots):
+        high, low = split(columns.T)
+        at = slice(block * LANES, (block + 1) * LANES)
+        left[at, :LANES] = high
+        left[at, LANES : 2 * LANES] = low
+        left[at, 2 * LANES :] = high
+
+    def multiply(slot, left, right, block):
+        size = 2 * nin // blocks
+        total = jnp.dot(
+            left[...],
+            right[:, block * size : (block + 1) * size],
+            preferred_element_type=jnp.float32,
+        )
+        start = block * size % nin
+        staged[slot, block * size // nin, :, start : start + size] = (total * factor).astype(
+            jnp.bfloat16
+        )
+
+    def copy(slot, index):
+        return pltpu.make_async_copy(staged.at[slot], out.at[index], sems.at[slot])
+
+    @pl.when(step >= 2)
+    def _():
+        copy(1, 2 * step - 3).wait()
+
+    for block in range(blocks):
+        multiply(1, left_1, right_1, block)
+        prepare(0, left_0, right_0, block)
+
+    @pl.when(step >= 1)
+    def _():
+        copy(1, 2 * step - 1).start()
+        copy(0, 2 * step - 2).wait()
+
+    for block in range(blocks):
+        multiply(0, left_0, right_0, block)
+        prepare(1, left_1, right_1, block)
+
+    copy(0, 2 * step).start()
+
+    @pl.when(step == last)
+    def _():
+        copy(1, 2 * step - 1).wait()
+        for block in range(blocks):
+            multiply(1, left_1, right_1, block)
+        copy(1, 2 * step + 1).start()
+        copy(0, 2 * step).wait()
+        copy(1, 2 * step + 1).wait()
+
+
+def correlate_call(received, widths, capacity, used, factor, in_local):
     sources = received[0].shape[0]
     nin = sources * in_local
     in_specs = [
         pl.BlockSpec(memory_space=pltpu.SMEM),
         pl.BlockSpec(memory_space=pltpu.SMEM),
-    ] + [pl.BlockSpec((sources, slots * width, LANES), lambda s: (0, s, 0)) for width in widths]
+    ] + [pl.BlockSpec((sources, 2 * width, LANES), lambda s: (0, s, 0)) for width in widths]
     return pl.pallas_call(
-        functools.partial(correlate_kernel, widths, slots, in_local),
+        functools.partial(correlate_kernel, widths, in_local),
         out_shape=jax.ShapeDtypeStruct((capacity, 2, nin, nin), jnp.bfloat16),
-        grid=(capacity // slots,),
+        grid=(capacity // 2,),
         in_specs=in_specs,
-        out_specs=pl.BlockSpec((slots, 2, nin, nin), lambda s: (s, 0, 0, 0)),
+        out_specs=pl.BlockSpec(memory_space=pl.ANY),
         scratch_shapes=[
-            pltpu.VMEM((2 * nin, 3 * LANES), jnp.bfloat16),
-            pltpu.VMEM((3 * LANES, nin), jnp.bfloat16),
+            pltpu.VMEM((nin, 3 * LANES), jnp.bfloat16),
+            pltpu.VMEM((3 * LANES, 2 * nin), jnp.bfloat16),
         ]
-        * slots,
+        * 2
+        + [pltpu.VMEM((2, 2, nin, nin), jnp.bfloat16), pltpu.SemaphoreType.DMA((2,))],
         compiler_params=pltpu.CompilerParams(vmem_limit_bytes=60 * MIB),
         cost_estimate=pl.CostEstimate(
             flops=capacity * 8 * nin * nin * 256,
@@ -435,7 +476,7 @@
     factor = jnp.reshape(1.0 / (SPEC * mean_power), (1,))
     widths = [block.shape[1] // capacity for block in (block_a, block_b)]
     return correlate_call(
-        [received_a, received_b], widths, capacity, used, factor, in_local, slots=2
+        [received_a, received_b], widths, capacity, used, factor, in_local
     )
 
 

time: 167 us -> 169 us (1.012)
    pallas_call x1, Pallas kernels: 20.8 us -> 23 us  [correlate_call(): pl.pallas_call(functools.partial(correlate_kernel, widths, in_local), out...]
  transfers between devices with their start and end apart: 2 -> 2, of which waited for: 2 -> 2; matrix products, arithmetic and copies ran while one was open for 1% -> 1% of each run, Pallas kernels for 21% -> 20%
where the time goes in v5:
time: 169 us; the launch traced here: 168 us
  Pallas kernels  77 us (46%)
  waiting for transfers between devices  71 us (42%)
  starting transfers between devices  11.5 us (7%)
  other arithmetic  6.15 us (4%)
    all_to_all x2, waiting for transfers between devices, exchange(): lax.all_to_all(block, 'feed', split_axis=0, concat_axis=0, tiled=True)  71 us
    pallas_call x2, Pallas kernels, spectra_call(): pl.pallas_call(functools.partial(spectra_kernel, count, last, devices, me...  54 us
    pallas_call x1, Pallas kernels, correlate_call(): pl.pallas_call(functools.partial(correlate_kernel, widths, in_local), out...  23 us
    all_to_all x2, starting transfers between devices, exchange(): lax.all_to_all(block, 'feed', split_axis=0, concat_axis=0, tiled=True)  11.5 us
  transfers between devices with their start and end apart: 2, of which 2 were waited for; matrix products, arithmetic and copies ran while one was open for 1% of the time, Pallas kernels for 20%

profile of v5, /device:TPU:13, one launch (start us, length us, event | category | flops | bytes accessed | tf_op | source)
XLA Modules:
  0.0 168.5 jit_solution(2643886768147717763)
XLA Ops:
  0.0 0.7 pad_add_fusion
  0.7 0.8 select_reduce_fusion
  1.5 0.7 compare_and_fusion
  2.2 1.2 add_select_fusion
  3.5 0.0 copy-start.2
  3.5 20.2 %spectra.2 = (f32[3072,128]{1,0:T(8,128)}, f32[8,128]{1,0:T(8,128)}) custom-call(s32[256]{0:T(256)} %get-tuple-element.15.refs_0_, f32[4,8192]{1,0:T(4,128)} %refs_2_.3, f32[4,8192]{1,0:T(4,128)} %refs_2_.3, bf16[51,32,8192]{2,1,0:T(8,128)(2,1)} %bitcast.5, bf16[51,32,8192]{2,1,0:T(8,128)(2,1)} %bitcast.6, ...), custom_call_target="tpu_custom_call" | custom-call | flops 6442450944 | bytes 31457280 | tf_op jit(solution)/shard_map/spectra/pallas_call | solution.py:277
  23.7 6.6 %all-to-all-start = ((f32[16,192,128]{2,1,0:T(8,128)}), f32[16,192,128]{2,1,0:T(8,128)S(1)}, u32[]{:S(2)}, u32[]{:S(2)}) async-start(f32[16,192,128]{2,1,0:T(8,128)} %bitcast.10), calls=%async_computation | async-start | bytes 3145728 | tf_op jit(solution)/shard_map/all_to_all | solution.py:436
  30.3 0.0 copy-done.2
  30.3 0.6 add_select_fusion.1.refs_0_
  30.9 33.8 %spectra.3 = f32[6272,128]{1,0:T(8,128)} custom-call(s32[256]{0:T(256)} %add_select_fusion.1.refs_0_, f32[4,8192]{1,0:T(4,128)} %refs_2_.3, f32[4,8192]{1,0:T(4,128)} %refs_2_.3, bf16[51,32,8192]{2,1,0:T(8,128)(2,1)} %bitcast.7, bf16[51,32,8192]{2,1,0:T(8,128)(2,1)} %bitcast.8, bf16[2,2,4096,256]{3,2,1,0:T(8,128)(2,1)} %constant.44.clone.refs_5_.refs_6_.refs_7_, ...), custom_call_target="tpu_custom_call" | custom-call | flops 12884901888 | bytes 31457280 | tf_op jit(solution)/shard_map/spectra/pallas_call | solution.py:277
  64.7 1.8 %all-to-all-done.refs_0_ = f32[16,192,128]{2,1,0:T(8,128)S(1)} async-done(((f32[16,192,128]{2,1,0:T(8,128)}), f32[16,192,128]{2,1,0:T(8,128)S(1)}, u32[]{:S(2)}, u32[]{:S(2)}) %all-to-all-start) | async-done | bytes 1572896 | tf_op jit(solution)/shard_map/all_to_all | solution.py:436
  66.4 0.0 copy-start.1
  66.4 1.1 copy-done.1
  67.6 4.9 %all-to-all-start.1 = ((f32[16,392,128]{2,1,0:T(8,128)}), f32[16,392,128]{2,1,0:T(8,128)S(1)}, u32[]{:S(2)}, u32[]{:S(2)}) async-start(f32[16,392,128]{2,1,0:T(8,128)} %bitcast.9), calls=%async_computation.1 | async-start | bytes 6422528 | tf_op jit(solution)/shard_map/all_to_all | solution.py:436
  72.5 0.1 fusion.3
  72.6 0.6 convert_element_type.11.used_ref
  73.2 0.7 fusion.4
  74.6 69.2 %all-to-all-done.1.refs_1_ = f32[16,392,128]{2,1,0:T(8,128)S(1)} async-done(((f32[16,392,128]{2,1,0:T(8,128)}), f32[16,392,128]{2,1,0:T(8,128)S(1)}, u32[]{:S(2)}, u32[]{:S(2)}) %all-to-all-start.1) | async-done | bytes 3211296 | tf_op jit(solution)/shard_map/all_to_all | solution.py:436
  143.8 0.0 copy-start
  143.8 0.7 slice_reduce_fusion
  145.3 0.2 copy-done
  145.5 23.0 %correlate.1 = bf16[24,2,512,512]{3,2,1,0:T(8,128)(2,1)} custom-call(f32[1]{0:T(128)} %bitcast.4.factor_ref, s32[24]{0:T(128)} %convert_element_type.11.used_ref, f32[16,192,128]{2,1,0:T(8,128)} %copy-done.1, f32[16,392,128]{2,1,0:T(8,128)} %copy-done), custom_call_target="tpu_custom_call" | custom-call | flops 12884901888 | bytes 29884416 | tf_op jit(solution)/shard_map/correlate/pallas_call | solution.py:413
  (1 shorter events, 0.0 us)
Async XLA Ops:
  3.5 26.8 %copy-start.2 = (s32[256,1]{0,1:T(1,128)S(1)}, s32[256,1]{0,1:T(1,128)}, u32[]{:S(2)}) copy-start(s32[256,1]{0,1:T(1,128)} %param.7) | copy-start | bytes 3076
  23.7 42.7 %all-to-all-start = ((f32[16,192,128]{2,1,0:T(8,128)}), f32[16,192,128]{2,1,0:T(8,128)S(1)}, u32[]{:S(2)}, u32[]{:S(2)}) async-start(f32[16,192,128]{2,1,0:T(8,128)} %bitcast.10), calls=%async_computation | async-start | bytes 3145728 | tf_op jit(solution)/shard_map/all_to_all | solution.py:436
  66.4 1.2 copy-start.1
  67.6 76.2 %all-to-all-start.1 = ((f32[16,392,128]{2,1,0:T(8,128)}), f32[16,392,128]{2,1,0:T(8,128)S(1)}, u32[]{:S(2)}, u32[]{:S(2)}) async-start(f32[16,392,128]{2,1,0:T(8,128)} %bitcast.9), calls=%async_computation.1 | async-start | bytes 6422528 | tf_op jit(solution)/shard_map/all_to_all | solution.py:436
  143.8 1.7 copy-start

commit v6 on v5

--- a/solution.py
+++ b/solution.py
@@ -36,7 +36,7 @@
     for parity in range(2):
         chans = BAND_START + 2 * np.arange(BAND // 2, dtype=np.int64) + parity
         angles = (n[:, None] * chans[None, :] % NFFT) * (2.0 * math.pi / NFFT)
-        full = np.concatenate([np.cos(angles), -np.sin(angles)], axis=1) / math.sqrt(NFFT)
+        full = np.stack([np.cos(angles), -np.sin(angles)]) / math.sqrt(NFFT)
         high = full.astype(np.float32).astype(ml_dtypes.bfloat16)
         low = (full - high.astype(np.float64)).astype(np.float32).astype(ml_dtypes.bfloat16)
         tables.append(np.stack([high, low]))
@@ -152,16 +152,19 @@
                     far = sum(c * x for c, x in zip(coef_b[1:], held_b[1:])) + coef_b[0] * held_b[0]
                     at = slice(s * in_local + first, s * in_local + first + 16)
                     for ref, value in ((even, near + far), (odd, near - far)):
-                        high, low = split(value)
-                        ref[at, tile * LANES : (tile + 1) * LANES] = high
-                        ref[at, KB + tile * LANES : KB + (tile + 1) * LANES] = low
+                        ref[0, tile, at, :], ref[1, tile, at, :] = split(value)
                     held_a, held_b = held_a[1:], held_b[1:]
 
     def matmul_piece(table, parity, start, ref):
         cols = slice(parity * BAND, (parity + 1) * BAND)
         at = slice(start, start + 256)
-        right = jnp.concatenate([table[parity, 0], table[parity, 0], table[parity, 1]], axis=0)
-        left = jnp.concatenate([ref[at, :], ref[at, :KB]], axis=1)
+        tall = [
+            jnp.concatenate([table[parity, part, 0], table[parity, part, 1]], axis=1)
+            for part in range(2)
+        ]
+        right = jnp.concatenate([tall[0], tall[0], tall[1]], axis=0)
+        wide = [ref[part, tile, at, :] for part in (0, 1, 0) for tile in range(KB // LANES)]
+        left = jnp.concatenate(wide, axis=1)
         acc[at, cols] += jnp.dot(left, right, preferred_element_type=jnp.float32)
 
     def matmul_pieces(table, even, odd):
@@ -248,7 +251,7 @@
         return pl.BlockSpec((taps, step_size), lambda j, *_: (0, j + offset))
 
     def table_spec(index):
-        return pl.BlockSpec((2, 2, KB, BAND), lambda j, *_: (0, 0, index(j), 0))
+        return pl.BlockSpec((2, 2, 2, KB, LANES), lambda j, *_: (0, 0, 0, index(j), 0))
 
     block = jax.ShapeDtypeStruct((devices * message, LANES), jnp.float32)
     power = jax.ShapeDtypeStruct((8, LANES), jnp.float32)
@@ -268,7 +271,7 @@
         ]
         + (single if last else []),
         out_specs=whole + ([] if last else single),
-        scratch_shapes=[pltpu.VMEM((rows, 2 * KB), jnp.bfloat16)] * 4
+        scratch_shapes=[pltpu.VMEM((2, KB // LANES, rows, LANES), jnp.bfloat16)] * 4
         + [
             pltpu.VMEM((rows, 2 * BAND), jnp.float32),
             pltpu.VMEM((BAND * width, LANES), jnp.float32),
@@ -348,28 +351,21 @@
         pad = [jnp.zeros((LANES - 8 * len(straight), LANES), jnp.float32)]
         columns = jnp.concatenate(straight + pad, axis=0)
         for part, value in enumerate((columns, jnp.concatenate(turned + pad, axis=0))):
-            high, low = split(value)
-            lanes = slice(part * nin + block * LANES, part * nin + (block + 1) * LANES)
-            right[:LANES, lanes] = high
-            right[LANES : 2 * LANES, lanes] = high
-            right[2 * LANES :, lanes] = low
-        high, low = split(columns.T)
+            right[0, part * blocks + block], right[1, part * blocks + block] = split(value)
         at = slice(block * LANES, (block + 1) * LANES)
-        left[at, :LANES] = high
-        left[at, LANES : 2 * LANES] = low
-        left[at, 2 * LANES :] = high
-
-    def multiply(slot, left, right, block):
-        size = 2 * nin // blocks
+        left[0, at, :], left[1, at, :] = split(columns.T)
+
+    def multiply(slot, left, right, part):
+        wide = [
+            jnp.concatenate([right[k, part * blocks + b] for b in range(blocks)], axis=1)
+            for k in range(2)
+        ]
         total = jnp.dot(
-            left[...],
-            right[:, block * size : (block + 1) * size],
+            jnp.concatenate([left[0], left[1], left[0]], axis=1),
+            jnp.concatenate([wide[0], wide[0], wide[1]], axis=0),
             preferred_element_type=jnp.float32,
         )
-        start = block * size % nin
-        staged[slot, block * size // nin, :, start : start + size] = (total * factor).astype(
-            jnp.bfloat16
-        )
+        staged[slot, part] = (total * factor).astype(jnp.bfloat16)
 
     def copy(slot, index):
         return pltpu.make_async_copy(staged.at[slot], out.at[index], sems.at[slot])
@@ -378,26 +374,28 @@
     def _():
         copy(1, 2 * step - 3).wait()
 
-    for block in range(blocks):
-        multiply(1, left_1, right_1, block)
-        prepare(0, left_0, right_0, block)
+    for part in range(2):
+        multiply(1, left_1, right_1, part)
+        for block in range(part * blocks // 2, (part + 1) * blocks // 2):
+            prepare(0, left_0, right_0, block)
 
     @pl.when(step >= 1)
     def _():
         copy(1, 2 * step - 1).start()
         copy(0, 2 * step - 2).wait()
 
-    for block in range(blocks):
-        multiply(0, left_0, right_0, block)
-        prepare(1, left_1, right_1, block)
+    for part in range(2):
+        multiply(0, left_0, right_0, part)
+        for block in range(part * blocks // 2, (part + 1) * blocks // 2):
+            prepare(1, left_1, right_1, block)
 
     copy(0, 2 * step).start()
 
     @pl.when(step == last)
     def _():
         copy(1, 2 * step - 1).wait()
-        for block in range(blocks):
-            multiply(1, left_1, right_1, block)
+        for part in range(2):
+            multiply(1, left_1, right_1, part)
         copy(1, 2 * step + 1).start()
         copy(0, 2 * step).wait()
         copy(1, 2 * step + 1).wait()
@@ -417,8 +415,8 @@
         in_specs=in_specs,
         out_specs=pl.BlockSpec(memory_space=pl.ANY),
         scratch_shapes=[
-            pltpu.VMEM((nin, 3 * LANES), jnp.bfloat16),
-            pltpu.VMEM((3 * LANES, 2 * nin), jnp.bfloat16),
+            pltpu.VMEM((2, nin, LANES), jnp.bfloat16),
+            pltpu.VMEM((2, 2 * nin // LANES, LANES, LANES), jnp.bfloat16),
         ]
         * 2
         + [pltpu.VMEM((2, 2, nin, nin), jnp.bfloat16), pltpu.SemaphoreType.DMA((2,))],

time: 169 us -> 168 us (level)
  Pallas kernels: 77 us -> 74.6 us
  waiting for transfers between devices: 71 us -> 72.7 us
    pallas_call x2, Pallas kernels: 54 us -> 51.8 us  [spectra_call(): pl.pallas_call(functools.partial(spectra_kernel, count, last, devices, me...]
    all_to_all x2, waiting for transfers between devices: 71 us -> 72.7 us  [exchange(): lax.all_to_all(block, 'feed', split_axis=0, concat_axis=0, tiled=True)]
  transfers between devices with their start and end apart: 2 -> 2, of which waited for: 2 -> 2; matrix products, arithmetic and copies ran while one was open for 1% -> 1% of each run, Pallas kernels for 20% -> 19%
where the time goes in v6:
time: 168 us
  Pallas kernels  74.6 us (44%)
  waiting for transfers between devices  72.7 us (43%)
  starting transfers between devices  11.5 us (7%)
  other arithmetic  6.15 us (4%)
    all_to_all x2, waiting for transfers between devices, exchange(): lax.all_to_all(block, 'feed', split_axis=0, concat_axis=0, tiled=True)  72.7 us
    pallas_call x2, Pallas kernels, spectra_call(): pl.pallas_call(functools.partial(spectra_kernel, count, last, devices, me...  51.8 us
    pallas_call x1, Pallas kernels, correlate_call(): pl.pallas_call(functools.partial(correlate_kernel, widths, in_local), out...  22.7 us
    all_to_all x2, starting transfers between devices, exchange(): lax.all_to_all(block, 'feed', split_axis=0, concat_axis=0, tiled=True)  11.5 us
  transfers between devices with their start and end apart: 2, of which 2 were waited for; matrix products, arithmetic and copies ran while one was open for 1% of the time, Pallas kernels for 19%

profile of v6, /device:TPU:13, one launch (start us, length us, event | category | flops | bytes accessed | tf_op | source)
XLA Modules:
  0.0 167.7 jit_solution(18356559120690001131)
XLA Ops:
  0.0 0.7 pad_add_fusion
  0.7 0.8 select_reduce_fusion
  1.5 0.7 compare_and_fusion
  2.2 1.2 add_select_fusion
  3.5 0.0 copy-start.2
  3.5 19.7 %spectra.2 = (f32[3072,128]{1,0:T(8,128)}, f32[8,128]{1,0:T(8,128)}) custom-call(s32[256]{0:T(256)} %get-tuple-element.15.refs_0_, f32[4,8192]{1,0:T(4,128)} %refs_2_.3, f32[4,8192]{1,0:T(4,128)} %refs_2_.3, bf16[51,32,8192]{2,1,0:T(8,128)(2,1)} %bitcast.5, bf16[51,32,8192]{2,1,0:T(8,128)(2,1)} %bitcast.6, ...), custom_call_target="tpu_custom_call" | custom-call | flops 6442450944 | bytes 31457280 | tf_op jit(solution)/shard_map/spectra/pallas_call | solution.py:280
  23.2 6.6 %all-to-all-start = ((f32[16,192,128]{2,1,0:T(8,128)}), f32[16,192,128]{2,1,0:T(8,128)S(1)}, u32[]{:S(2)}, u32[]{:S(2)}) async-start(f32[16,192,128]{2,1,0:T(8,128)} %bitcast.10), calls=%async_computation | async-start | bytes 3145728 | tf_op jit(solution)/shard_map/all_to_all | solution.py:434
  29.8 0.0 copy-done.2
  29.8 0.6 add_select_fusion.1.refs_0_
  30.3 32.1 %spectra.3 = f32[6272,128]{1,0:T(8,128)} custom-call(s32[256]{0:T(256)} %add_select_fusion.1.refs_0_, f32[4,8192]{1,0:T(4,128)} %refs_2_.3, f32[4,8192]{1,0:T(4,128)} %refs_2_.3, bf16[51,32,8192]{2,1,0:T(8,128)(2,1)} %bitcast.7, bf16[51,32,8192]{2,1,0:T(8,128)(2,1)} %bitcast.8, bf16[2,2,2,4096,128]{4,3,2,1,0:T(8,128)(2,1)} %constant.44.clone.refs_5_.refs_6_.refs_7_, ...), custom_call_target="tpu_custom_call" | custom-call | flops 12884901888 | bytes 31457280 | tf_op jit(solution)/shard_map/spectra/pallas_call | solution.py:280
  62.5 3.5 %all-to-all-done.refs_0_ = f32[16,192,128]{2,1,0:T(8,128)S(1)} async-done(((f32[16,192,128]{2,1,0:T(8,128)}), f32[16,192,128]{2,1,0:T(8,128)S(1)}, u32[]{:S(2)}, u32[]{:S(2)}) %all-to-all-start) | async-done | bytes 1572896 | tf_op jit(solution)/shard_map/all_to_all | solution.py:434
  65.9 0.0 copy-start.1
  65.9 1.1 copy-done.1
  67.1 4.9 %all-to-all-start.1 = ((f32[16,392,128]{2,1,0:T(8,128)}), f32[16,392,128]{2,1,0:T(8,128)S(1)}, u32[]{:S(2)}, u32[]{:S(2)}) async-start(f32[16,392,128]{2,1,0:T(8,128)} %bitcast.9), calls=%async_computation.1 | async-start | bytes 6422528 | tf_op jit(solution)/shard_map/all_to_all | solution.py:434
  72.0 0.1 fusion.3
  72.1 0.6 convert_element_type.11.used_ref
  72.7 0.7 fusion.4
  74.1 69.2 %all-to-all-done.1.refs_1_ = f32[16,392,128]{2,1,0:T(8,128)S(1)} async-done(((f32[16,392,128]{2,1,0:T(8,128)}), f32[16,392,128]{2,1,0:T(8,128)S(1)}, u32[]{:S(2)}, u32[]{:S(2)}) %all-to-all-start.1) | async-done | bytes 3211296 | tf_op jit(solution)/shard_map/all_to_all | solution.py:434
  143.3 0.0 copy-start
  143.3 0.7 slice_reduce_fusion
  144.8 0.2 copy-done
  145.0 22.7 %correlate.1 = bf16[24,2,512,512]{3,2,1,0:T(8,128)(2,1)} custom-call(f32[1]{0:T(128)} %bitcast.4.factor_ref, s32[24]{0:T(128)} %convert_element_type.11.used_ref, f32[16,192,128]{2,1,0:T(8,128)} %copy-done.1, f32[16,392,128]{2,1,0:T(8,128)} %copy-done), custom_call_target="tpu_custom_call" | custom-call | flops 12884901888 | bytes 29884416 | tf_op jit(solution)/shard_map/correlate/pallas_call | solution.py:411
  (1 shorter events, 0.0 us)
Async XLA Ops:
  3.5 26.3 %copy-start.2 = (s32[256,1]{0,1:T(1,128)S(1)}, s32[256,1]{0,1:T(1,128)}, u32[]{:S(2)}) copy-start(s32[256,1]{0,1:T(1,128)} %param.7) | copy-start | bytes 3076
  23.2 42.7 %all-to-all-start = ((f32[16,192,128]{2,1,0:T(8,128)}), f32[16,192,128]{2,1,0:T(8,128)S(1)}, u32[]{:S(2)}, u32[]{:S(2)}) async-start(f32[16,192,128]{2,1,0:T(8,128)} %bitcast.10), calls=%async_computation | async-start | bytes 3145728 | tf_op jit(solution)/shard_map/all_to_all | solution.py:434
  65.9 1.2 copy-start.1
  67.1 76.2 %all-to-all-start.1 = ((f32[16,392,128]{2,1,0:T(8,128)}), f32[16,392,128]{2,1,0:T(8,128)S(1)}, u32[]{:S(2)}, u32[]{:S(2)}) async-start(f32[16,392,128]{2,1,0:T(8,128)} %bitcast.9), calls=%async_computation.1 | async-start | bytes 6422528 | tf_op jit(solution)/shard_map/all_to_all | solution.py:434
  143.3 1.7 copy-start

commit v7 on v6

--- a/solution.py
+++ b/solution.py
@@ -19,6 +19,7 @@
 FIRST = 16
 KB = 256
 LANES = 128
+STAGES = 4
 MIB = 1 << 20
 
 
@@ -124,36 +125,48 @@
     return high, (value - high.astype(jnp.float32)).astype(jnp.bfloat16)
 
 
-def spectra_kernel(count, last, devices, message, taps, in_local, *refs):
+def spectra_kernel(count, last, devices, blocks, taps, in_local, *refs):
     row_ref, taps_a, taps_b, frames_a, frames_b, table_a, table_b, table_last = refs[:8]
+    refs = refs[8:]
     if last:
-        before, out = refs[8:10]
-    else:
-        out, power_out = refs[8:10]
-    even_0, odd_0, even_1, odd_1, acc, flat = refs[10:]
+        before, refs = refs[0], refs[1:]
+    outs, refs = refs[:blocks], refs[blocks:]
+    if not last:
+        power_out, refs = refs[0], refs[1:]
+    even_0, odd_0, even_1, odd_1, acc, flat = refs
     step = pl.program_id(0)
     rows = count * in_local
 
-    def window_piece(block, tile, begin, even, odd):
-            lanes = slice(block * KB + tile * LANES, block * KB + (tile + 1) * LANES)
-            coef_a = [taps_a[t : t + 1, lanes] for t in range(taps)]
-            coef_b = [taps_b[t : t + 1, lanes] for t in range(taps)]
-            for first in range(0, in_local, 16):
-
-                def load(ref, f):
-                    return ref[f, first : first + 16, lanes].astype(jnp.float32)
-
-                held_a = [load(frames_a, begin + f) for f in range(taps - 1)]
-                held_b = [load(frames_b, begin + f) for f in range(taps - 1)]
-                for s in range(begin, begin + 8):
-                    held_a.append(load(frames_a, s + taps - 1))
-                    held_b.append(load(frames_b, s + taps - 1))
-                    near = sum(c * x for c, x in zip(coef_a[1:], held_a[1:])) + coef_a[0] * held_a[0]
-                    far = sum(c * x for c, x in zip(coef_b[1:], held_b[1:])) + coef_b[0] * held_b[0]
-                    at = slice(s * in_local + first, s * in_local + first + 16)
-                    for ref, value in ((even, near + far), (odd, near - far)):
-                        ref[0, tile, at, :], ref[1, tile, at, :] = split(value)
-                    held_a, held_b = held_a[1:], held_b[1:]
+    def window_piece(block, first, begin, even, odd):
+        lanes = slice(block * KB, (block + 1) * KB)
+        coef_a = [taps_a[t : t + 1, lanes] for t in range(taps)]
+        coef_b = [taps_b[t : t + 1, lanes] for t in range(taps)]
+
+        def load(ref, f):
+            return ref[f, first : first + 8, lanes].astype(jnp.float32)
+
+        held_a = [load(frames_a, begin + f) for f in range(taps - 1)]
+        held_b = [load(frames_b, begin + f) for f in range(taps - 1)]
+        for s in range(begin, begin + 8, 2):
+            pair = []
+            for f in (s, s + 1):
+                held_a.append(load(frames_a, f + taps - 1))
+                held_b.append(load(frames_b, f + taps - 1))
+                near = sum(c * x for c, x in zip(coef_a[1:], held_a[1:])) + coef_a[0] * held_a[0]
+                far = sum(c * x for c, x in zip(coef_b[1:], held_b[1:])) + coef_b[0] * held_b[0]
+                pair.append((near + far, near - far))
+                held_a, held_b = held_a[1:], held_b[1:]
+            start = row_of(s, first)
+            for ref, values in zip((even, odd), zip(*pair)):
+                for tile in range(KB // LANES):
+                    own = slice(tile * LANES, (tile + 1) * LANES)
+                    value = jnp.concatenate([v[:, own] for v in values], axis=0)
+                    ref[0, tile, start : start + 16, :], ref[1, tile, start : start + 16, :] = split(
+                        value
+                    )
+
+    def row_of(s, i):
+        return s // 2 * 2 * in_local + i // 8 * 16 + s % 2 * 8
 
     def matmul_piece(table, parity, start, ref):
         cols = slice(parity * BAND, (parity + 1) * BAND)
@@ -176,15 +189,17 @@
 
     def window_pieces(block, even, odd):
         return [
-            functools.partial(window_piece, block, tile, begin, even, odd)
-            for tile in range(KB // LANES)
+            functools.partial(window_piece, block, first, begin, even, odd)
+            for first in range(0, in_local, 8)
             for begin in range(0, count, 8)
         ]
 
     def alternate(left, right):
-        for one, other in zip(left, right, strict=True):
-            one()
-            other()
+        share = len(right) // len(left)
+        for k, piece in enumerate(left):
+            piece()
+            for other in right[k * share : (k + 1) * share]:
+                other()
 
     @pl.when(step == 0)
     def _():
@@ -204,32 +219,41 @@
             for part in range(2):
                 cols = slice(parity * BAND + part * LANES, parity * BAND + (part + 1) * LANES)
                 for g in range(width):
-                    turned = acc[g * LANES : (g + 1) * LANES, cols].T
+                    starts = [
+                        row_of(s, i)
+                        for s in range(g * LANES // in_local, (g + 1) * LANES // in_local)
+                        for i in range(0, in_local, 8)
+                    ]
+                    turned = jnp.concatenate([acc[r : r + 8, cols] for r in starts], axis=0).T
                     row = (parity * 2 + part) * width + g
                     flat[pl.ds(row, LANES, stride=4 * width), :] = turned
         size = 2 * width
 
         def place(c, total):
             value = flat[pl.ds(pl.multiple_of(c * size, size), size), :]
-            row = row_ref[c]
-
-            @pl.when(row >= 0)
-            def _():
-                out[pl.ds(pl.multiple_of(row * 8, 8), size), :] = value
+            live = jnp.int32(-1)
+            for p, out in enumerate(outs):
+                row = row_ref[p, c]
+                live = jnp.maximum(live, row)
+
+                @pl.when(row >= 0)
+                def _(out=out, row=row):
+                    out[pl.ds(pl.multiple_of(row * 8, 8), size), :] = value
 
             square = sum(value[start : start + 8] ** 2 for start in range(0, size, 8))
-            return total + (row >= 0).astype(jnp.float32) * square
+            return total + (live >= 0).astype(jnp.float32) * square
 
         total = lax.fori_loop(0, BAND, place, jnp.zeros((8, LANES), jnp.float32), unroll=8)
         if last:
             total = total + before[...]
+            message = outs[0].shape[0] // devices
             for d in range(devices):
-                out[(d + 1) * message - 8 : (d + 1) * message, :] = total
+                outs[0][(d + 1) * message - 8 : (d + 1) * message, :] = total
         else:
             power_out[...] = total
 
 
-def spectra_call(first, count, before, table, owners, ranks, dead, fir_taps, samples, devices):
+def spectra_call(first, count, parts, before, table, owners, ranks, dead, fir_taps, samples, devices):
     _, in_local, _ = samples.shape
     taps = fir_taps.shape[0]
     step_size = 2 * KB
@@ -237,9 +261,17 @@
     last = before is not None
     rows = count * in_local
     width = 2 * rows // LANES
-    capacity = BAND // devices + BAND // (2 * devices)
-    message = capacity * width + 8 * last
-    row_of = jnp.where(dead, -1, owners * (message // 8) + ranks * (width // 8))
+    messages = [
+        (high - low) * width + 8 * (last and p == 0) for p, (low, high) in enumerate(parts)
+    ]
+    rows_of = [
+        jnp.where(
+            dead | (ranks < low) | (ranks >= high),
+            -1,
+            owners * (message // 8) + (ranks - low) * (width // 8),
+        )
+        for (low, high), message in zip(parts, messages)
+    ]
 
     def frames_spec(offset):
         return pl.BlockSpec(
@@ -253,9 +285,9 @@
     def table_spec(index):
         return pl.BlockSpec((2, 2, 2, KB, LANES), lambda j, *_: (0, 0, 0, index(j), 0))
 
-    block = jax.ShapeDtypeStruct((devices * message, LANES), jnp.float32)
+    blocks = [jax.ShapeDtypeStruct((devices * m, LANES), jnp.float32) for m in messages]
     power = jax.ShapeDtypeStruct((8, LANES), jnp.float32)
-    whole = [pl.BlockSpec(block.shape, lambda j, *_: (0, 0))]
+    whole = [pl.BlockSpec(block.shape, lambda j, *_: (0, 0)) for block in blocks]
     single = [pl.BlockSpec(power.shape, lambda j, *_: (0, 0))]
     grid_spec = pltpu.PrefetchScalarGridSpec(
         num_scalar_prefetch=1,
@@ -277,9 +309,9 @@
             pltpu.VMEM((BAND * width, LANES), jnp.float32),
         ],
     )
-    sent, *rest = pl.pallas_call(
-        functools.partial(spectra_kernel, count, last, devices, message, taps, in_local),
-        out_shape=[block] + ([] if last else [power]),
+    results = pl.pallas_call(
+        functools.partial(spectra_kernel, count, last, devices, len(parts), taps, in_local),
+        out_shape=blocks + ([] if last else [power]),
         grid_spec=grid_spec,
         compiler_params=pltpu.CompilerParams(vmem_limit_bytes=60 * MIB),
         cost_estimate=pl.CostEstimate(
@@ -287,7 +319,7 @@
         ),
         name="spectra",
     )(
-        row_of,
+        jnp.stack(rows_of),
         fir_taps,
         fir_taps,
         samples,
@@ -297,7 +329,8 @@
         table,
         *([before] if last else []),
     )
-    return [sent.reshape(devices, message, LANES)] + rest
+    sent = [r.reshape(devices, m, LANES) for r, m in zip(results, messages)]
+    return sent + list(results[len(parts) :])
 
 
 def exchange_lanes(values, in_local):
@@ -318,10 +351,10 @@
     return values
 
 
-def correlate_kernel(widths, in_local, factor_ref, used_ref, *refs):
+def correlate_kernel(widths, low, count, in_local, factor_ref, used_ref, *refs):
     groups = refs[: len(widths)]
-    out, left_0, right_0, left_1, right_1, staged, sems = refs[len(widths) :]
-    step, last = pl.program_id(0), pl.num_programs(0) - 1
+    out, left_0, right_0, left_1, right_1, staged, sems = refs[-7:]
+    step, last = pl.program_id(0), count // 2 - 1
     per_tile = LANES // in_local
     blocks = groups[0].shape[0] // per_tile
     nin = groups[0].shape[0] * in_local
@@ -355,7 +388,7 @@
         at = slice(block * LANES, (block + 1) * LANES)
         left[0, at, :], left[1, at, :] = split(columns.T)
 
-    def multiply(slot, left, right, part):
+    def multiply(index, left, right, part):
         wide = [
             jnp.concatenate([right[k, part * blocks + b] for b in range(blocks)], axis=1)
             for k in range(2)
@@ -365,53 +398,87 @@
             jnp.concatenate([wide[0], wide[0], wide[1]], axis=0),
             preferred_element_type=jnp.float32,
         )
-        staged[slot, part] = (total * factor).astype(jnp.bfloat16)
-
-    def copy(slot, index):
-        return pltpu.make_async_copy(staged.at[slot], out.at[index], sems.at[slot])
-
-    @pl.when(step >= 2)
+        staged[lax.rem(index + STAGES, STAGES), part] = (total * factor).astype(jnp.bfloat16)
+
+    def copies(index):
+        buffer = lax.rem(index, STAGES)
+        return [
+            pltpu.make_async_copy(
+                staged.at[buffer, part, pl.ds(half * nin // 2, nin // 2)],
+                out.at[low + index, part, pl.ds(half * nin // 2, nin // 2)],
+                sems.at[buffer, 2 * part + half],
+            )
+            for part in range(2)
+            for half in range(2)
+        ]
+
+    def start(index):
+        for copy in copies(index):
+            copy.start()
+
+    def wait(index):
+        for copy in copies(index):
+            copy.wait()
+
+    odd, even = 2 * step - 1, 2 * step
+
+    @pl.when(odd >= STAGES)
     def _():
-        copy(1, 2 * step - 3).wait()
+        wait(odd - STAGES)
 
     for part in range(2):
-        multiply(1, left_1, right_1, part)
+        multiply(odd, left_1, right_1, part)
         for block in range(part * blocks // 2, (part + 1) * blocks // 2):
             prepare(0, left_0, right_0, block)
 
     @pl.when(step >= 1)
     def _():
-        copy(1, 2 * step - 1).start()
-        copy(0, 2 * step - 2).wait()
+        start(odd)
+
+    @pl.when(even >= STAGES)
+    def _():
+        wait(even - STAGES)
 
     for part in range(2):
-        multiply(0, left_0, right_0, part)
+        multiply(even, left_0, right_0, part)
         for block in range(part * blocks // 2, (part + 1) * blocks // 2):
             prepare(1, left_1, right_1, block)
 
-    copy(0, 2 * step).start()
+    start(even)
 
     @pl.when(step == last)
     def _():
-        copy(1, 2 * step - 1).wait()
+        if count > STAGES:
+            wait(jnp.int32(count - 1 - STAGES))
         for part in range(2):
-            multiply(1, left_1, right_1, part)
-        copy(1, 2 * step + 1).start()
-        copy(0, 2 * step).wait()
-        copy(1, 2 * step + 1).wait()
-
-
-def correlate_call(received, widths, capacity, used, factor, in_local):
-    sources = received[0].shape[0]
-    nin = sources * in_local
+            multiply(even + 1, left_1, right_1, part)
+        start(even + 1)
+        for index in range(count - min(STAGES, count), count):
+            wait(jnp.int32(index))
+
+
+def correlate_call(received, widths, low, high, capacity, used, factor, before, in_local):
+    arrays = [r for r, _ in received]
+    nin = arrays[0].shape[0] * in_local
+    count = high - low
     in_specs = [
         pl.BlockSpec(memory_space=pltpu.SMEM),
         pl.BlockSpec(memory_space=pltpu.SMEM),
-    ] + [pl.BlockSpec((sources, 2 * width, LANES), lambda s: (0, s, 0)) for width in widths]
+    ] + [
+        pl.BlockSpec(
+            (r.shape[0], 2 * width, LANES), lambda s, d=(low - first) // 2: (0, s + d, 0)
+        )
+        for (r, first), width in zip(received, widths)
+    ]
+    aliases = {}
+    if before is not None:
+        in_specs.append(pl.BlockSpec(memory_space=pl.ANY))
+        aliases = {2 + len(arrays): 0}
+        arrays.append(before)
     return pl.pallas_call(
-        functools.partial(correlate_kernel, widths, in_local),
+        functools.partial(correlate_kernel, widths, low, count, in_local),
         out_shape=jax.ShapeDtypeStruct((capacity, 2, nin, nin), jnp.bfloat16),
-        grid=(capacity // 2,),
+        grid=(count // 2,),
         in_specs=in_specs,
         out_specs=pl.BlockSpec(memory_space=pl.ANY),
         scratch_shapes=[
@@ -419,15 +486,19 @@
             pltpu.VMEM((2, 2 * nin // LANES, LANES, LANES), jnp.bfloat16),
         ]
         * 2
-        + [pltpu.VMEM((2, 2, nin, nin), jnp.bfloat16), pltpu.SemaphoreType.DMA((2,))],
+        + [
+            pltpu.VMEM((STAGES, 2, nin, nin), jnp.bfloat16),
+            pltpu.SemaphoreType.DMA((STAGES, 4)),
+        ],
+        input_output_aliases=aliases,
         compiler_params=pltpu.CompilerParams(vmem_limit_bytes=60 * MIB),
         cost_estimate=pl.CostEstimate(
-            flops=capacity * 8 * nin * nin * 256,
-            bytes_accessed=capacity * (4 * nin * nin + 8 * nin * SPEC),
+            flops=count * 8 * nin * nin * 256,
+            bytes_accessed=count * (4 * nin * nin + 8 * nin * SPEC),
             transcendentals=0,
         ),
         name="correlate",
-    )(factor, used, *received)
+    )(factor, used[low:high], *arrays)
 
 
 def exchange(block):
@@ -460,11 +531,14 @@
         samples=jnp.transpose(samples, (1, 0, 2)),
         devices=devices,
     )
-    block_a, power = call(0, FIRST, None)
+    middle = capacity - 4
+    block_a, power = call(0, FIRST, [(0, capacity)], None)
     received_a = exchange(block_a)
-    (block_b,) = call(FIRST, SPEC - FIRST, power)
+    block_b, block_c = call(FIRST, SPEC - FIRST, [(0, middle), (middle, capacity)], power)
     block_b, received_a = lax.optimization_barrier((block_b, received_a))
     received_b = exchange(block_b)
+    block_c, received_b = lax.optimization_barrier((block_c, received_b))
+    received_c = exchange(block_c)
 
     kept = jnp.sum(jnp.logical_not(dead).astype(jnp.float32))
     mine = (owners == lax.axis_index("feed")) & jnp.logical_not(dead)
@@ -472,9 +546,17 @@
     used = jnp.any((ranks[None, :] == slots[:, None]) & mine[None, :], axis=1).astype(jnp.int32)
     mean_power = jnp.sum(received_b[:, -8:]) / (NIN * SPEC * kept)
     factor = jnp.reshape(1.0 / (SPEC * mean_power), (1,))
-    widths = [block.shape[1] // capacity for block in (block_a, block_b)]
-    return correlate_call(
-        [received_a, received_b], widths, capacity, used, factor, in_local
+    run = functools.partial(
+        correlate_call,
+        widths=[2 * n * in_local // LANES for n in (FIRST, SPEC - FIRST)],
+        capacity=capacity,
+        used=used,
+        factor=factor,
+        in_local=in_local,
+    )
+    first = run([(received_a, 0), (received_b, 0)], low=0, high=middle, before=None)
+    return run(
+        [(received_a, 0), (received_c, middle)], low=middle, high=capacity, before=first
     )
 
 

time: 168 us -> 164 us (0.976)
  waiting for transfers between devices: 72.7 us -> 58.6 us
  starting transfers between devices: 11.5 us -> 16.9 us
  Pallas kernels: 74.6 us -> 77.8 us
    all_to_all x2 -> x3, waiting for transfers between devices: 72.7 us -> 58.6 us  [exchange(): lax.all_to_all(block, 'feed', split_axis=0, concat_axis=0, tiled=True)]
    all_to_all x2 -> x3, starting transfers between devices: 11.5 us -> 16.9 us  [exchange(): lax.all_to_all(block, 'feed', split_axis=0, concat_axis=0, tiled=True)]
    pallas_call x3 -> x4, Pallas kernels: 74.6 us -> 77.8 us  [the longest x2 54.4 us: spectra_call(): pl.pallas_call(functools.partial(spectra_kernel, count, last, devices, le...]
  transfers between devices with their start and end apart: 2 -> 3, of which waited for: 2 -> 2; matrix products, arithmetic and copies ran while one was open for 1% -> 1% of each run, Pallas kernels for 19% -> 32%
where the time goes in v7:
time: 164 us; the launch traced here: 163 us
  Pallas kernels  77.8 us (47%)
  waiting for transfers between devices  58.6 us (36%)
  starting transfers between devices  16.9 us (10%)
  other arithmetic  5.67 us (3%)
  local copies, waits for them, and re-layouts  2.59 us (2%)
    all_to_all x3, waiting for transfers between devices, exchange(): lax.all_to_all(block, 'feed', split_axis=0, concat_axis=0, tiled=True)  58.6 us
    pallas_call x2, Pallas kernels, spectra_call(): pl.pallas_call(functools.partial(spectra_kernel, count, last, devices, le...  54.4 us
    pallas_call x2, Pallas kernels, correlate_call(): pl.pallas_call(functools.partial(correlate_kernel, widths, low, count, in...  23.4 us
    all_to_all x3, starting transfers between devices, exchange(): lax.all_to_all(block, 'feed', split_axis=0, concat_axis=0, tiled=True)  16.9 us
  transfers between devices with their start and end apart: 3, of which 2 were waited for; matrix products, arithmetic and copies ran while one was open for 1% of the time, Pallas kernels for 32%

profile of v7, /device:TPU:13, one launch (start us, length us, event | category | flops | bytes accessed | tf_op | source)
XLA Modules:
  0.0 163.0 jit_solution(15537081115147930920)
XLA Ops:
  0.0 0.7 pad_add_fusion
  0.7 0.8 select_reduce_fusion
  1.5 1.3 or_select_fusion
  2.8 19.4 %spectra.2 = (f32[3072,128]{1,0:T(8,128)}, f32[8,128]{1,0:T(8,128)}) custom-call(s32[1,256]{1,0:T(1,128)} %get-tuple-element.21.refs_0_, f32[4,8192]{1,0:T(4,128)} %refs_2_.3, f32[4,8192]{1,0:T(4,128)} %refs_2_.3, bf16[51,32,8192]{2,1,0:T(8,128)(2,1)} %bitcast.20, bf16[51,32,8192]{2,1,0:T(8,128)(2,1)} %bitcast.21, ...), custom_call_target="tpu_custom_call" | custom-call | flops 6442450944 | bytes 31457280 | tf_op jit(solution)/shard_map/spectra/pallas_call | solution.py:312
  22.2 6.6 %all-to-all-start = ((f32[16,192,128]{2,1,0:T(8,128)}), f32[16,192,128]{2,1,0:T(8,128)S(1)}, u32[]{:S(2)}, u32[]{:S(2)}) async-start(f32[16,192,128]{2,1,0:T(8,128)} %bitcast.25), calls=%async_computation | async-start | bytes 3145728 | tf_op jit(solution)/shard_map/all_to_all | solution.py:505
  28.8 0.0 copy-done.2
  28.8 0.6 pad_add_fusion.1.refs_0_
  29.4 34.9 %spectra.3 = (f32[5248,128]{1,0:T(8,128)}, f32[1024,128]{1,0:T(8,128)}) custom-call(s32[2,256]{1,0:T(2,128)} %pad_add_fusion.1.refs_0_, f32[4,8192]{1,0:T(4,128)} %refs_2_.3, f32[4,8192]{1,0:T(4,128)} %refs_2_.3, bf16[51,32,8192]{2,1,0:T(8,128)(2,1)} %bitcast.22, bf16[51,32,8192]{2,1,0:T(8,128)(2,1)} %bitcast.23, ...), custom_call_target="tpu_custom_call" | custom-call | flops 12884901888 | bytes 31457280 | tf_op jit(solution)/shard_map/spectra/pallas_call | solution.py:312
  64.3 0.6 all-to-all-done.refs_0_
  65.0 1.1 copy-done
  66.1 5.4 %all-to-all-start.1 = ((f32[16,328,128]{2,1,0:T(8,128)}), f32[16,328,128]{2,1,0:T(8,128)}, u32[]{:S(2)}, u32[]{:S(2)}) async-start(f32[16,328,128]{2,1,0:T(8,128)} %bitcast.24), calls=%async_computation.1 | async-start | bytes 5373952 | tf_op jit(solution)/shard_map/all_to_all | solution.py:505
  71.5 0.1 fusion.3
  71.7 0.0 copy-start.3
  71.7 0.6 slice.10.used_ref
  72.3 0.7 convert_reduce_fusion
  73.7 58.0 %all-to-all-done.1.refs_1_ = f32[16,328,128]{2,1,0:T(8,128)} async-done(((f32[16,328,128]{2,1,0:T(8,128)}), f32[16,328,128]{2,1,0:T(8,128)}, u32[]{:S(2)}, u32[]{:S(2)}) %all-to-all-start.1) | async-done | bytes 2687008 | tf_op jit(solution)/shard_map/all_to_all | solution.py:505
  131.7 1.5 slice_reduce_fusion
  133.1 4.9 %all-to-all-start.2 = ((f32[16,64,128]{2,1,0:T(8,128)}), f32[16,64,128]{2,1,0:T(8,128)S(1)}, u32[]{:S(2)}, u32[]{:S(2)}) async-start(f32[16,64,128]{2,1,0:T(8,128)} %bitcast.6), calls=%async_computation.2 | async-start | bytes 1048576 | tf_op jit(solution)/shard_map/all_to_all | solution.py:505
  138.7 0.0 copy-done.3
  138.8 17.7 %correlate.2.refs_2_ = bf16[24,2,512,512]{3,2,1,0:T(8,128)(2,1)} custom-call(f32[1]{0:T(128)} %bitcast.9.factor_ref, s32[20]{0:T(128)} %bitcast.31, f32[16,192,128]{2,1,0:T(8,128)} %copy-done, f32[16,328,128]{2,1,0:T(8,128)} %all-to-all-done.1.refs_1_), custom_call_target="tpu_custom_call" | custom-call | flops 10737418240 | bytes 24903680 | tf_op jit(solution)/shard_map/correlate/pallas_call | solution.py:478
  156.4 0.0 all-to-all-done.2.refs_1_
  156.5 0.0 copy-start.1
  156.5 0.8 copy-done.1
  157.3 5.7 %correlate.3 = bf16[24,2,512,512]{3,2,1,0:T(8,128)(2,1)} custom-call(f32[1]{0:T(128)} %bitcast.9.factor_ref, s32[4]{0:T(128)} %slice.10.used_ref, f32[16,192,128]{2,1,0:T(8,128)} %copy-done, f32[16,64,128]{2,1,0:T(8,128)} %copy-done.1, bf16[24,2,512,512]{3,2,1,0:T(8,128)(2,1)} %correlate.2.refs_2_), custom_call_target="tpu_custom_call", output_to_operand_aliasing={{}: (4, {})} | custom-call | flops 2147483648 | bytes 4980736 | tf_op jit(solution)/shard_map/correlate/pallas_call | solution.py:478
  (7 shorter events, 0.0 us)
Async XLA Ops:
  22.2 6.6 %copy-start.2 = (s32[256,1]{0,1:T(1,128)S(1)}, s32[256,1]{0,1:T(1,128)}, u32[]{:S(2)}) copy-start(s32[256,1]{0,1:T(1,128)} %param.7) | copy-start | bytes 3076
  22.2 42.8 %all-to-all-start = ((f32[16,192,128]{2,1,0:T(8,128)}), f32[16,192,128]{2,1,0:T(8,128)S(1)}, u32[]{:S(2)}, u32[]{:S(2)}) async-start(f32[16,192,128]{2,1,0:T(8,128)} %bitcast.25), calls=%async_computation | async-start | bytes 3145728 | tf_op jit(solution)/shard_map/all_to_all | solution.py:505
  65.0 1.1 copy-start
  66.1 65.6 %all-to-all-start.1 = ((f32[16,328,128]{2,1,0:T(8,128)}), f32[16,328,128]{2,1,0:T(8,128)}, u32[]{:S(2)}, u32[]{:S(2)}) async-start(f32[16,328,128]{2,1,0:T(8,128)} %bitcast.24), calls=%async_computation.1 | async-start | bytes 5373952 | tf_op jit(solution)/shard_map/all_to_all | solution.py:505
  71.7 67.1 %copy-start.3 = (s32[24]{0:T(128)}, s32[24]{0:T(128)S(1)}, u32[]{:S(2)}) copy-start(s32[24]{0:T(128)S(1)} %convert_element_type.11) | copy-start | bytes 292
  133.1 23.3 %all-to-all-start.2 = ((f32[16,64,128]{2,1,0:T(8,128)}), f32[16,64,128]{2,1,0:T(8,128)S(1)}, u32[]{:S(2)}, u32[]{:S(2)}) async-start(f32[16,64,128]{2,1,0:T(8,128)} %bitcast.6), calls=%async_computation.2 | async-start | bytes 1048576 | tf_op jit(solution)/shard_map/all_to_all | solution.py:505
  156.5 0.8 copy-start.1

commit v8 on v7

--- a/solution.py
+++ b/solution.py
@@ -120,12 +120,19 @@
     return (raw_vis * factor).astype(jnp.bfloat16)
 
 
+def weighted(coefs, values):
+    terms = [c * v for c, v in zip(coefs, values)]
+    while len(terms) > 1:
+        terms = [sum(terms[k + 1 : k + 2], terms[k]) for k in range(0, len(terms), 2)]
+    return terms[0]
+
+
 def split(value):
     high = value.astype(jnp.bfloat16)
     return high, (value - high.astype(jnp.float32)).astype(jnp.bfloat16)
 
 
-def spectra_kernel(count, last, devices, blocks, taps, in_local, *refs):
+def spectra_kernel(count, last, devices, message, blocks, taps, in_local, *refs):
     row_ref, taps_a, taps_b, frames_a, frames_b, table_a, table_b, table_last = refs[:8]
     refs = refs[8:]
     if last:
@@ -133,44 +140,34 @@
     outs, refs = refs[:blocks], refs[blocks:]
     if not last:
         power_out, refs = refs[0], refs[1:]
-    even_0, odd_0, even_1, odd_1, acc, flat = refs
+    even_0, odd_0, even_1, odd_1, acc, flat, staged, sems = refs
     step = pl.program_id(0)
     rows = count * in_local
 
-    def window_piece(block, first, begin, even, odd):
-        lanes = slice(block * KB, (block + 1) * KB)
-        coef_a = [taps_a[t : t + 1, lanes] for t in range(taps)]
-        coef_b = [taps_b[t : t + 1, lanes] for t in range(taps)]
-
-        def load(ref, f):
-            return ref[f, first : first + 8, lanes].astype(jnp.float32)
-
-        held_a = [load(frames_a, begin + f) for f in range(taps - 1)]
-        held_b = [load(frames_b, begin + f) for f in range(taps - 1)]
-        for s in range(begin, begin + 8, 2):
-            pair = []
-            for f in (s, s + 1):
-                held_a.append(load(frames_a, f + taps - 1))
-                held_b.append(load(frames_b, f + taps - 1))
-                near = sum(c * x for c, x in zip(coef_a[1:], held_a[1:])) + coef_a[0] * held_a[0]
-                far = sum(c * x for c, x in zip(coef_b[1:], held_b[1:])) + coef_b[0] * held_b[0]
-                pair.append((near + far, near - far))
+    def window_piece(block, tile, begin, even, odd):
+        lanes = slice(block * KB + tile * LANES, block * KB + (tile + 1) * LANES)
+        coef_a = [jnp.broadcast_to(taps_a[t : t + 1, lanes], (16, LANES)) for t in range(taps)]
+        coef_b = [jnp.broadcast_to(taps_b[t : t + 1, lanes], (16, LANES)) for t in range(taps)]
+        for first in range(0, in_local, 16):
+
+            def load(ref, f):
+                return ref[f, first : first + 16, lanes].astype(jnp.float32)
+
+            held_a = [load(frames_a, begin + f) for f in range(taps - 1)]
+            held_b = [load(frames_b, begin + f) for f in range(taps - 1)]
+            for s in range(begin, begin + 8):
+                held_a.append(load(frames_a, s + taps - 1))
+                held_b.append(load(frames_b, s + taps - 1))
+                near = weighted(coef_a, held_a)
+                far = weighted(coef_b, held_b)
+                at = slice(s * in_local + first, s * in_local + first + 16)
+                for ref, value in ((even, near + far), (odd, near - far)):
+                    ref[0, tile, at, :], ref[1, tile, at, :] = split(value)
                 held_a, held_b = held_a[1:], held_b[1:]
-            start = row_of(s, first)
-            for ref, values in zip((even, odd), zip(*pair)):
-                for tile in range(KB // LANES):
-                    own = slice(tile * LANES, (tile + 1) * LANES)
-                    value = jnp.concatenate([v[:, own] for v in values], axis=0)
-                    ref[0, tile, start : start + 16, :], ref[1, tile, start : start + 16, :] = split(
-                        value
-                    )
-
-    def row_of(s, i):
-        return s // 2 * 2 * in_local + i // 8 * 16 + s % 2 * 8
 
     def matmul_piece(table, parity, start, ref):
         cols = slice(parity * BAND, (parity + 1) * BAND)
-        at = slice(start, start + 256)
+        at = slice(start, start + 512)
         tall = [
             jnp.concatenate([table[parity, part, 0], table[parity, part, 1]], axis=1)
             for part in range(2)
@@ -184,13 +181,13 @@
         return [
             functools.partial(matmul_piece, table, parity, start, ref)
             for parity, ref in enumerate((even, odd))
-            for start in range(0, rows, 256)
+            for start in range(0, rows, 512)
         ]
 
     def window_pieces(block, even, odd):
         return [
-            functools.partial(window_piece, block, first, begin, even, odd)
-            for first in range(0, in_local, 8)
+            functools.partial(window_piece, block, tile, begin, even, odd)
+            for tile in range(KB // LANES)
             for begin in range(0, count, 8)
         ]
 
@@ -219,41 +216,45 @@
             for part in range(2):
                 cols = slice(parity * BAND + part * LANES, parity * BAND + (part + 1) * LANES)
                 for g in range(width):
-                    starts = [
-                        row_of(s, i)
-                        for s in range(g * LANES // in_local, (g + 1) * LANES // in_local)
-                        for i in range(0, in_local, 8)
-                    ]
-                    turned = jnp.concatenate([acc[r : r + 8, cols] for r in starts], axis=0).T
+                    turned = acc[g * LANES : (g + 1) * LANES, cols].T
                     row = (parity * 2 + part) * width + g
                     flat[pl.ds(row, LANES, stride=4 * width), :] = turned
         size = 2 * width
 
         def place(c, total):
             value = flat[pl.ds(pl.multiple_of(c * size, size), size), :]
-            live = jnp.int32(-1)
-            for p, out in enumerate(outs):
-                row = row_ref[p, c]
-                live = jnp.maximum(live, row)
-
-                @pl.when(row >= 0)
-                def _(out=out, row=row):
-                    out[pl.ds(pl.multiple_of(row * 8, 8), size), :] = value
-
-            square = sum(value[start : start + 8] ** 2 for start in range(0, size, 8))
-            return total + (live >= 0).astype(jnp.float32) * square
+            row = row_ref[c]
+
+            @pl.when(row >= 0)
+            def _():
+                staged[pl.ds(pl.multiple_of(row * 8, 8), size), :] = value
+
+            square = value[:8] * value[:8]
+            for start in range(8, size, 8):
+                square += value[start : start + 8] * value[start : start + 8]
+            return total + (row >= 0).astype(jnp.float32) * square
 
         total = lax.fori_loop(0, BAND, place, jnp.zeros((8, LANES), jnp.float32), unroll=8)
         if last:
             total = total + before[...]
-            message = outs[0].shape[0] // devices
             for d in range(devices):
-                outs[0][(d + 1) * message - 8 : (d + 1) * message, :] = total
+                staged[(d + 1) * message - 8 : (d + 1) * message, :] = total
         else:
             power_out[...] = total
-
-
-def spectra_call(first, count, parts, before, table, owners, ranks, dead, fir_taps, samples, devices):
+        copies, row = [], 0
+        for k, out in enumerate(outs):
+            count_rows = out.shape[0]
+            copies.append(
+                pltpu.make_async_copy(staged.at[pl.ds(row, count_rows)], out, sems.at[k])
+            )
+            row += count_rows
+        for copy in copies:
+            copy.start()
+        for copy in copies:
+            copy.wait()
+
+
+def spectra_call(first, count, parts, place, before, table, ranks, dead, fir_taps, samples):
     _, in_local, _ = samples.shape
     taps = fir_taps.shape[0]
     step_size = 2 * KB
@@ -261,17 +262,10 @@
     last = before is not None
     rows = count * in_local
     width = 2 * rows // LANES
-    messages = [
-        (high - low) * width + 8 * (last and p == 0) for p, (low, high) in enumerate(parts)
-    ]
-    rows_of = [
-        jnp.where(
-            dead | (ranks < low) | (ranks >= high),
-            -1,
-            owners * (message // 8) + (ranks - low) * (width // 8),
-        )
-        for (low, high), message in zip(parts, messages)
-    ]
+    devices = sum(parts)
+    capacity = BAND // devices + BAND // (2 * devices)
+    message = capacity * width + 8 * last
+    row_of = jnp.where(dead, -1, place * (message // 8) + ranks * (width // 8))
 
     def frames_spec(offset):
         return pl.BlockSpec(
@@ -285,9 +279,9 @@
     def table_spec(index):
         return pl.BlockSpec((2, 2, 2, KB, LANES), lambda j, *_: (0, 0, 0, index(j), 0))
 
-    blocks = [jax.ShapeDtypeStruct((devices * m, LANES), jnp.float32) for m in messages]
+    blocks = [jax.ShapeDtypeStruct((n * message, LANES), jnp.float32) for n in parts]
     power = jax.ShapeDtypeStruct((8, LANES), jnp.float32)
-    whole = [pl.BlockSpec(block.shape, lambda j, *_: (0, 0)) for block in blocks]
+    whole = [pl.BlockSpec(memory_space=pl.ANY)] * len(parts)
     single = [pl.BlockSpec(power.shape, lambda j, *_: (0, 0))]
     grid_spec = pltpu.PrefetchScalarGridSpec(
         num_scalar_prefetch=1,
@@ -307,10 +301,12 @@
         + [
             pltpu.VMEM((rows, 2 * BAND), jnp.float32),
             pltpu.VMEM((BAND * width, LANES), jnp.float32),
+            pltpu.VMEM((devices * message, LANES), jnp.float32),
+            pltpu.SemaphoreType.DMA((len(parts),)),
         ],
     )
     results = pl.pallas_call(
-        functools.partial(spectra_kernel, count, last, devices, len(parts), taps, in_local),
+        functools.partial(spectra_kernel, count, last, devices, message, len(parts), taps, in_local),
         out_shape=blocks + ([] if last else [power]),
         grid_spec=grid_spec,
         compiler_params=pltpu.CompilerParams(vmem_limit_bytes=60 * MIB),
@@ -319,7 +315,7 @@
         ),
         name="spectra",
     )(
-        jnp.stack(rows_of),
+        row_of,
         fir_taps,
         fir_taps,
         samples,
@@ -329,7 +325,7 @@
         table,
         *([before] if last else []),
     )
-    sent = [r.reshape(devices, m, LANES) for r, m in zip(results, messages)]
+    sent = [r.reshape(n, message, LANES) for r, n in zip(results, parts)]
     return sent + list(results[len(parts) :])
 
 
@@ -351,26 +347,26 @@
     return values
 
 
-def correlate_kernel(widths, low, count, in_local, factor_ref, used_ref, *refs):
-    groups = refs[: len(widths)]
-    out, left_0, right_0, left_1, right_1, staged, sems = refs[-7:]
+def correlate_kernel(widths, count, in_local, factor_ref, used_ref, index_ref, *refs):
+    near_a, near_b, *far_b = refs[:-8]
+    out, left_0, right_0, left_1, right_1, second, staged, sems = refs[-8:]
     step, last = pl.program_id(0), count // 2 - 1
     per_tile = LANES // in_local
-    blocks = groups[0].shape[0] // per_tile
-    nin = groups[0].shape[0] * in_local
+    blocks = near_a.shape[0] // per_tile
+    nin = near_a.shape[0] * in_local
     factor = factor_ref[0]
     upper = lax.broadcasted_iota(jnp.int32, (8, LANES), 0) >= 4
 
     def prepare(slot, left, right, block):
         used = used_ref[2 * step + slot] != 0
         straight, turned = [], []
-        for ref, width in zip(groups, widths):
+        for group, (ref, width) in enumerate(zip((near_a, second), widths)):
             tiles = []
             for start in range(slot * width, (slot + 1) * width, 8):
-                mixed = [
-                    jnp.where(used, ref[block * per_tile + a, start : start + 8], 0.0)
-                    for a in range(per_tile)
-                ]
+                mixed = []
+                for source in range(block * per_tile, (block + 1) * per_tile):
+                    at = index_ref[source] if group else source
+                    mixed.append(jnp.where(used, ref[at, start : start + 8], 0.0))
                 tiles.append(exchange_lanes(mixed, in_local))
             for q in range(per_tile):
                 column = [t[q] for t in tiles]
@@ -405,7 +401,7 @@
         return [
             pltpu.make_async_copy(
                 staged.at[buffer, part, pl.ds(half * nin // 2, nin // 2)],
-                out.at[low + index, part, pl.ds(half * nin // 2, nin // 2)],
+                out.at[index, part, pl.ds(half * nin // 2, nin // 2)],
                 sems.at[buffer, 2 * part + half],
             )
             for part in range(2)
@@ -421,6 +417,9 @@
             copy.wait()
 
     odd, even = 2 * step - 1, 2 * step
+    second[: near_b.shape[0]] = near_b[...]
+    for k, ref in enumerate(far_b):
+        second[near_b.shape[0] + k] = ref[0]
 
     @pl.when(odd >= STAGES)
     def _():
@@ -457,26 +456,16 @@
             wait(jnp.int32(index))
 
 
-def correlate_call(received, widths, low, high, capacity, used, factor, before, in_local):
-    arrays = [r for r, _ in received]
-    nin = arrays[0].shape[0] * in_local
-    count = high - low
-    in_specs = [
-        pl.BlockSpec(memory_space=pltpu.SMEM),
-        pl.BlockSpec(memory_space=pltpu.SMEM),
-    ] + [
-        pl.BlockSpec(
-            (r.shape[0], 2 * width, LANES), lambda s, d=(low - first) // 2: (0, s + d, 0)
-        )
-        for (r, first), width in zip(received, widths)
+def correlate_call(received, widths, capacity, used, factor, index, in_local):
+    sources = received[0].shape[0]
+    nin = sources * in_local
+    count = capacity
+    in_specs = [pl.BlockSpec(memory_space=pltpu.SMEM)] * 3 + [
+        pl.BlockSpec((r.shape[0], 2 * width, LANES), lambda s: (0, s, 0))
+        for r, width in zip(received, widths[:1] + widths[1:] * len(received))
     ]
-    aliases = {}
-    if before is not None:
-        in_specs.append(pl.BlockSpec(memory_space=pl.ANY))
-        aliases = {2 + len(arrays): 0}
-        arrays.append(before)
     return pl.pallas_call(
-        functools.partial(correlate_kernel, widths, low, count, in_local),
+        functools.partial(correlate_kernel, widths, count, in_local),
         out_shape=jax.ShapeDtypeStruct((capacity, 2, nin, nin), jnp.bfloat16),
         grid=(count // 2,),
         in_specs=in_specs,
@@ -487,10 +476,10 @@
         ]
         * 2
         + [
+            pltpu.VMEM((sources, 2 * widths[1], LANES), jnp.float32),
             pltpu.VMEM((STAGES, 2, nin, nin), jnp.bfloat16),
             pltpu.SemaphoreType.DMA((STAGES, 4)),
         ],
-        input_output_aliases=aliases,
         compiler_params=pltpu.CompilerParams(vmem_limit_bytes=60 * MIB),
         cost_estimate=pl.CostEstimate(
             flops=count * 8 * nin * nin * 256,
@@ -498,11 +487,26 @@
             transcendentals=0,
         ),
         name="correlate",
-    )(factor, used[low:high], *arrays)
+    )(factor, used, index, *received)
 
 
 def exchange(block):
     return lax.all_to_all(block, "feed", split_axis=0, concat_axis=0, tiled=True)
+
+
+def exchange_halves(near, far, flight):
+    devices = 2 * near.shape[0]
+    half = near.shape[0]
+    groups = [list(range(half)), list(range(half, devices))]
+    close = lax.all_to_all(
+        near, "feed", split_axis=0, concat_axis=0, axis_index_groups=groups, tiled=True
+    )
+    arrived = []
+    for k, block in enumerate(far):
+        if k >= flight:
+            block, arrived[k - flight] = lax.optimization_barrier((block, arrived[k - flight]))
+        arrived.append(lax.ppermute(block, "feed", [(i, i ^ (half + k)) for i in range(devices)]))
+    return [close] + arrived
 
 
 def channel_tables(owners, dropped_channels):
@@ -524,39 +528,34 @@
     call = functools.partial(
         spectra_call,
         table=jnp.asarray(folded_table()),
-        owners=owners,
         ranks=ranks,
         dead=dead,
         fir_taps=fir_taps,
         samples=jnp.transpose(samples, (1, 0, 2)),
-        devices=devices,
-    )
-    middle = capacity - 4
-    block_a, power = call(0, FIRST, [(0, capacity)], None)
+    )
+    half = devices // 2
+    me = lax.axis_index("feed")
+
+    def place(device):
+        return jnp.where(device // half == me // half, device % half, half + (device ^ me) % half)
+
+    block_a, power = call(0, FIRST, [devices], owners, None)
     received_a = exchange(block_a)
-    block_b, block_c = call(FIRST, SPEC - FIRST, [(0, middle), (middle, capacity)], power)
-    block_b, received_a = lax.optimization_barrier((block_b, received_a))
-    received_b = exchange(block_b)
-    block_c, received_b = lax.optimization_barrier((block_c, received_b))
-    received_c = exchange(block_c)
+    near, *far = call(FIRST, SPEC - FIRST, [half] + [1] * half, place(owners), power)
+    near, received_a = lax.optimization_barrier((near, received_a))
+    received_b = exchange_halves(near, far, 3)
 
     kept = jnp.sum(jnp.logical_not(dead).astype(jnp.float32))
     mine = (owners == lax.axis_index("feed")) & jnp.logical_not(dead)
     slots = jnp.arange(capacity, dtype=jnp.int32)
     used = jnp.any((ranks[None, :] == slots[:, None]) & mine[None, :], axis=1).astype(jnp.int32)
-    mean_power = jnp.sum(received_b[:, -8:]) / (NIN * SPEC * kept)
+    powers = jnp.concatenate([block[:, -8:] for block in received_b])
+    mean_power = jnp.sum(powers) / (NIN * SPEC * kept)
     factor = jnp.reshape(1.0 / (SPEC * mean_power), (1,))
-    run = functools.partial(
-        correlate_call,
-        widths=[2 * n * in_local // LANES for n in (FIRST, SPEC - FIRST)],
-        capacity=capacity,
-        used=used,
-        factor=factor,
-        in_local=in_local,
-    )
-    first = run([(received_a, 0), (received_b, 0)], low=0, high=middle, before=None)
-    return run(
-        [(received_a, 0), (received_c, middle)], low=middle, high=capacity, before=first
+    widths = [2 * n * in_local // LANES for n in (FIRST, SPEC - FIRST)]
+    index = place(jnp.arange(devices, dtype=jnp.int32)).astype(jnp.int32)
+    return correlate_call(
+        [received_a] + received_b, widths, capacity, used, factor, index, in_local
     )
 
 

time: 164 us -> 178 us (1.085)
  other arithmetic: 5.67 us -> 11.6 us
  waiting for transfers between devices: 58.6 us -> 64.2 us
  between operations: 1.46 us -> 6.42 us
  Pallas kernels: 77.8 us -> 74 us
  starting transfers between devices: 16.9 us -> 18.9 us
    ppermute x0 -> x8, waiting for transfers between devices: none -> 61.6 us  [exchange_halves(): lax.ppermute(block, 'feed', [(i, i ^ half + k) for i in range(devices)])]
    all_to_all x3 -> x1, waiting for transfers between devices: 58.6 us -> 2.63 us  [exchange(): lax.all_to_all(block, 'feed', split_axis=0, concat_axis=0, tiled=True)]
    all_to_all x3 -> x1, starting transfers between devices: 16.9 us -> 6.57 us  [exchange(): lax.all_to_all(block, 'feed', split_axis=0, concat_axis=0, tiled=True)]
    ppermute x0 -> x8, starting transfers between devices: none -> 8.27 us  [exchange_halves(): lax.ppermute(block, 'feed', [(i, i ^ half + k) for i in range(devices)])]
    reduce_sum x1 -> x9, other arithmetic: 1.46 us -> 5.66 us  [local_blocks(): mean_power = jnp.sum(powers) / (NIN * SPEC * kept)]
    all_to_all x0 -> x1, starting transfers between devices: none -> 4.05 us  [exchange_halves(): lax.all_to_all(near, 'feed', split_axis=0, concat_axis=0, axis_index_grou...]
    pallas_call x4 -> x3, Pallas kernels: 77.8 us -> 74 us  [the longest x2 52.6 us: spectra_call(): pl.pallas_call(functools.partial(spectra_kernel, count, last, devices, me...]
  transfers between devices with their start and end apart: 3 -> 10, of which waited for: 2 -> 9; matrix products, arithmetic and copies ran while one was open for 1% -> 4% of each run, Pallas kernels for 32% -> 19%
where the time goes in v8:
time: 178 us; the launch traced here: 176 us
  Pallas kernels  74 us (42%)
  waiting for transfers between devices  64.2 us (36%)
  starting transfers between devices  18.9 us (11%)
  other arithmetic  11.6 us (7%)
  between operations  6.42 us (4%)
    ppermute x8, waiting for transfers between devices, exchange_halves(): lax.ppermute(block, 'feed', [(i, i ^ half + k) for i in range(devices)])  61.6 us
    pallas_call x2, Pallas kernels, spectra_call(): pl.pallas_call(functools.partial(spectra_kernel, count, last, devices, me...  52.6 us
    pallas_call x1, Pallas kernels, correlate_call(): pl.pallas_call(functools.partial(correlate_kernel, widths, count, in_loca...  21.4 us
    ppermute x8, starting transfers between devices, exchange_halves(): lax.ppermute(block, 'feed', [(i, i ^ half + k) for i in range(devices)])  8.27 us
    all_to_all x1, starting transfers between devices, exchange(): lax.all_to_all(block, 'feed', split_axis=0, concat_axis=0, tiled=True)  6.57 us
    reduce_sum x9, other arithmetic, local_blocks(): mean_power = jnp.sum(powers) / (NIN * SPEC * kept)  5.66 us
    all_to_all x1, starting transfers between devices, exchange_halves(): lax.all_to_all(near, 'feed', split_axis=0, concat_axis=0, axis_index_grou...  4.05 us
  transfers between devices with their start and end apart: 10, of which 9 were waited for; matrix products, arithmetic and copies ran while one was open for 4% of the time, Pallas kernels for 19%

profile of v8, /device:TPU:13, one launch (start us, length us, event | category | flops | bytes accessed | tf_op | source)
XLA Modules:
  0.0 176.4 jit_solution(14543065618556620044)
XLA Ops:
  0.0 0.7 pad_add_fusion
  0.7 0.8 select_reduce_fusion
  1.5 0.7 compare_and_fusion
  2.2 1.2 add_select_fusion
  3.5 19.7 %spectra.2 = (f32[3072,128]{1,0:T(8,128)}, f32[8,128]{1,0:T(8,128)}) custom-call(s32[256]{0:T(256)} %get-tuple-element.53.refs_0_, f32[4,8192]{1,0:T(4,128)} %refs_2_.3, f32[4,8192]{1,0:T(4,128)} %refs_2_.3, bf16[51,32,8192]{2,1,0:T(8,128)(2,1)} %bitcast.13, bf16[51,32,8192]{2,1,0:T(8,128)(2,1)} %bitcast.14, ...), custom_call_target="tpu_custom_call" | custom-call | flops 6442450944 | bytes 31457280 | tf_op jit(solution)/shard_map/spectra/pallas_call | solution.py:308
  23.2 6.6 %all-to-all-start = ((f32[16,192,128]{2,1,0:T(8,128)}), f32[16,192,128]{2,1,0:T(8,128)S(1)}, u32[]{:S(2)}, u32[]{:S(2)}) async-start(f32[16,192,128]{2,1,0:T(8,128)} %bitcast.18), calls=%async_computation | async-start | bytes 3145728 | tf_op jit(solution)/shard_map/all_to_all | solution.py:494
  30.3 32.9 %spectra.3 = (f32[3136,128]{1,0:T(8,128)}, f32[392,128]{1,0:T(8,128)}, f32[392,128]{1,0:T(8,128)}, f32[392,128]{1,0:T(8,128)}, f32[392,128]{1,0:T(8,128)}, /*ind...) custom-call(s32[256]{0:T(256)} %add_select_fusion.1.refs_0_, f32[4,8192]{1,0:T(4,128)} %refs_2_.3, ...), custom_call_target="tpu_custom_call" | custom-call | flops 12884901888 | bytes 31457280 | tf_op jit(solution)/shard_map/spectra/pallas_call | solution.py:308
  63.3 2.6 %all-to-all-done.refs_0_ = f32[16,192,128]{2,1,0:T(8,128)S(1)} async-done(((f32[16,192,128]{2,1,0:T(8,128)}), f32[16,192,128]{2,1,0:T(8,128)S(1)}, u32[]{:S(2)}, u32[]{:S(2)}) %all-to-all-start) | async-done | bytes 1572896 | tf_op jit(solution)/shard_map/all_to_all | solution.py:494
  65.9 1.1 copy-done.1
  67.1 4.0 %all-to-all-start.1 = ((f32[8,392,128]{2,1,0:T(8,128)}), f32[8,392,128]{2,1,0:T(8,128)S(1)}, u32[]{:S(2)}, u32[]{:S(2)}) async-start(f32[8,392,128]{2,1,0:T(8,128)} %bitcast.17), calls=%async_computation.1 | async-start | bytes 3211264 | tf_op jit(solution)/shard_map/all_to_all | solution.py:501
  71.1 2.3 %collective-permute-start = (f32[1,392,128]{2,1,0:T(8,128)}, f32[1,392,128]{2,1,0:T(8,128)S(1)}, u32[]{:S(2)}, u32[]{:S(2)}) collective-permute-start(f32[1,392,128]{2,1,0:T(8,128)} %bitcast.31), channel_id=1, source_target_pairs={{0,8},{1,9},{2,10},{3,11},{4,12},{5,13},{6,14},{7,15},{8,0},{9,1},... | collective-permute-start | bytes 602120 | tf_op jit(solution)/shard_map/ppermute | solution.py:508
  74.0 2.3 %collective-permute-start.2 = (f32[1,392,128]{2,1,0:T(8,128)}, f32[1,392,128]{2,1,0:T(8,128)S(1)}, u32[]{:S(2)}, u32[]{:S(2)}) collective-permute-start(f32[1,392,128]{2,1,0:T(8,128)} %bitcast.29), channel_id=1, source_target_pairs={{0,10},{1,11},{2,8},{3,9},{4,14},{5,15},{6,12},{7,13},{8,2},{9,3},... | collective-permute-start | bytes 602120 | tf_op jit(solution)/shard_map/ppermute | solution.py:508
  77.0 0.7 fusion.4
  78.9 17.0 %collective-permute-done.refs_2_ = f32[1,392,128]{2,1,0:T(8,128)S(1)} collective-permute-done((f32[1,392,128]{2,1,0:T(8,128)}, f32[1,392,128]{2,1,0:T(8,128)S(1)}, u32[]{:S(2)}, u32[]{:S(2)}) %collective-permute-start) | collective-permute-done | bytes 200736 | tf_op jit(solution)/shard_map/ppermute | solution.py:508
  96.5 4.7 %collective-permute-done.1.refs_3_ = f32[1,392,128]{2,1,0:T(8,128)S(1)} collective-permute-done((f32[1,392,128]{2,1,0:T(8,128)}, f32[1,392,128]{2,1,0:T(8,128)S(1)}, u32[]{:S(2)}, u32[]{:S(2)}) %collective-permute-start.1) | collective-permute-done | bytes 200736 | tf_op jit(solution)/shard_map/ppermute | solution.py:508
  101.2 3.3 %collective-permute-done.2.refs_4_ = f32[1,392,128]{2,1,0:T(8,128)S(1)} collective-permute-done((f32[1,392,128]{2,1,0:T(8,128)}, f32[1,392,128]{2,1,0:T(8,128)S(1)}, u32[]{:S(2)}, u32[]{:S(2)}) %collective-permute-start.2) | collective-permute-done | bytes 200736 | tf_op jit(solution)/shard_map/ppermute | solution.py:508
  106.5 12.7 %collective-permute-done.3.refs_5_ = f32[1,392,128]{2,1,0:T(8,128)S(1)} collective-permute-done((f32[1,392,128]{2,1,0:T(8,128)}, f32[1,392,128]{2,1,0:T(8,128)S(1)}, u32[]{:S(2)}, u32[]{:S(2)}) %collective-permute-start.3) | collective-permute-done | bytes 200736 | tf_op jit(solution)/shard_map/ppermute | solution.py:508
  119.2 2.5 %collective-permute-start.6 = (f32[1,392,128]{2,1,0:T(8,128)}, f32[1,392,128]{2,1,0:T(8,128)S(1)}, u32[]{:S(2)}, u32[]{:S(2)}) collective-permute-start(f32[1,392,128]{2,1,0:T(8,128)} %bitcast.25), channel_id=1, source_target_pairs={{0,14},{1,15},{2,12},{3,13},{4,10},{5,11},{6,8},{7,9},{8,6},{9,7},... | collective-permute-start | bytes 602120 | tf_op jit(solution)/shard_map/ppermute | solution.py:508
  121.6 4.8 %collective-permute-done.4.refs_6_ = f32[1,392,128]{2,1,0:T(8,128)S(1)} collective-permute-done((f32[1,392,128]{2,1,0:T(8,128)}, f32[1,392,128]{2,1,0:T(8,128)S(1)}, u32[]{:S(2)}, u32[]{:S(2)}) %collective-permute-start.4) | collective-permute-done | bytes 200736 | tf_op jit(solution)/shard_map/ppermute | solution.py:508
  127.7 11.8 %collective-permute-done.5.refs_7_ = f32[1,392,128]{2,1,0:T(8,128)S(1)} collective-permute-done((f32[1,392,128]{2,1,0:T(8,128)}, f32[1,392,128]{2,1,0:T(8,128)S(1)}, u32[]{:S(2)}, u32[]{:S(2)}) %collective-permute-start.5) | collective-permute-done | bytes 200736 | tf_op jit(solution)/shard_map/ppermute | solution.py:508
  140.2 3.5 %collective-permute-done.6.refs_8_ = f32[1,392,128]{2,1,0:T(8,128)S(1)} collective-permute-done((f32[1,392,128]{2,1,0:T(8,128)}, f32[1,392,128]{2,1,0:T(8,128)S(1)}, u32[]{:S(2)}, u32[]{:S(2)}) %collective-permute-start.6) | collective-permute-done | bytes 200736 | tf_op jit(solution)/shard_map/ppermute | solution.py:508
  144.3 3.7 %collective-permute-done.7.refs_9_ = f32[1,392,128]{2,1,0:T(8,128)S(1)} collective-permute-done((f32[1,392,128]{2,1,0:T(8,128)S(1)}, f32[1,392,128]{2,1,0:T(8,128)S(1)}, u32[]{:S(2)}, u32[]{:S(2)}) %collective-permute-start.7) | collective-permute-done | bytes 200736 | tf_op jit(solution)/shard_map/ppermute | solution.py:508
  148.6 0.7 slice_reduce_fusion
  155.0 21.4 %correlate.1 = bf16[24,2,512,512]{3,2,1,0:T(8,128)(2,1)} custom-call(f32[1]{0:T(128)} %bitcast.12.factor_ref, s32[24]{0:T(128)} %convert_element_type.11.used_ref, s32[16]{0:T(128)} %compare_select_fusion.6.index_ref, f32[16,192,128]{2,1,0:T(8,128)} %copy-done.1, f32[8,392,128]{2,1,0:T(8,128)} %copy-done, f32[1,392,128]{2,1,0:T(8,128)} %copy-done.3, ...), custom_call_target="tpu_custom_call" | custom-call | flops 12884901888 | bytes 29884416 | tf_op jit(solution)/shard_map/correlate/pallas_call | solution.py:467
  (42 shorter events, 7.9 us)
Async XLA Ops:
  23.2 6.6 %copy-start.2 = (s32[256,1]{0,1:T(1,128)S(1)}, s32[256,1]{0,1:T(1,128)}, u32[]{:S(2)}) copy-start(s32[256,1]{0,1:T(1,128)} %param.7) | copy-start | bytes 3076
  23.2 42.8 %all-to-all-start = ((f32[16,192,128]{2,1,0:T(8,128)}), f32[16,192,128]{2,1,0:T(8,128)S(1)}, u32[]{:S(2)}, u32[]{:S(2)}) async-start(f32[16,192,128]{2,1,0:T(8,128)} %bitcast.18), calls=%async_computation | async-start | bytes 3145728 | tf_op jit(solution)/shard_map/all_to_all | solution.py:494
  65.9 1.1 copy-start.1
  65.9 60.5 %copy-start.11 = (f32[392,128]{1,0:T(8,128)S(1)}, f32[392,128]{1,0:T(8,128)}, u32[]{:S(2)}) copy-start(f32[392,128]{1,0:T(8,128)} %get-tuple-element.44) | copy-start | bytes 602116
  67.1 81.5 %all-to-all-start.1 = ((f32[8,392,128]{2,1,0:T(8,128)}), f32[8,392,128]{2,1,0:T(8,128)S(1)}, u32[]{:S(2)}, u32[]{:S(2)}) async-start(f32[8,392,128]{2,1,0:T(8,128)} %bitcast.17), calls=%async_computation.1 | async-start | bytes 3211264 | tf_op jit(solution)/shard_map/all_to_all | solution.py:501
  71.1 24.8 %collective-permute-start = (f32[1,392,128]{2,1,0:T(8,128)}, f32[1,392,128]{2,1,0:T(8,128)S(1)}, u32[]{:S(2)}, u32[]{:S(2)}) collective-permute-start(f32[1,392,128]{2,1,0:T(8,128)} %bitcast.31), channel_id=1, source_target_pairs={{0,8},{1,9},{2,10},{3,11},{4,12},{5,13},{6,14},{7,15},{8,0},{9,1},... | collective-permute-start | bytes 602120 | tf_op jit(solution)/shard_map/ppermute | solution.py:508
  73.5 27.8 %collective-permute-start.1 = (f32[1,392,128]{2,1,0:T(8,128)}, f32[1,392,128]{2,1,0:T(8,128)S(1)}, u32[]{:S(2)}, u32[]{:S(2)}) collective-permute-start(f32[1,392,128]{2,1,0:T(8,128)} %bitcast.30), channel_id=1, source_target_pairs={{0,9},{1,8},{2,11},{3,10},{4,13},{5,12},{6,15},{7,14},{8,1},{9,0},... | collective-permute-start | bytes 602120 | tf_op jit(solution)/shard_map/ppermute | solution.py:508
  74.0 30.6 %collective-permute-start.2 = (f32[1,392,128]{2,1,0:T(8,128)}, f32[1,392,128]{2,1,0:T(8,128)S(1)}, u32[]{:S(2)}, u32[]{:S(2)}) collective-permute-start(f32[1,392,128]{2,1,0:T(8,128)} %bitcast.29), channel_id=1, source_target_pairs={{0,10},{1,11},{2,8},{3,9},{4,14},{5,15},{6,12},{7,13},{8,2},{9,3},... | collective-permute-start | bytes 602120 | tf_op jit(solution)/shard_map/ppermute | solution.py:508
  96.0 58.9 %copy-start.3 = (f32[1,392,128]{2,1,0:T(8,128)}, f32[1,392,128]{2,1,0:T(8,128)S(1)}, u32[]{:S(2)}) copy-start(f32[1,392,128]{2,1,0:T(8,128)S(1)} %collective-permute-done.refs_2_) | copy-start | bytes 602116
  96.0 23.2 %collective-permute-start.3 = (f32[1,392,128]{2,1,0:T(8,128)}, f32[1,392,128]{2,1,0:T(8,128)S(1)}, u32[]{:S(2)}, u32[]{:S(2)}) collective-permute-start(f32[1,392,128]{2,1,0:T(8,128)} %bitcast.28), channel_id=1, source_target_pairs={{0,11},{1,10},{2,9},{3,8},{4,15},{5,14},{6,13},{7,12},{8,3},{9,2},... | collective-permute-start | bytes 602120 | tf_op jit(solution)/shard_map/ppermute | solution.py:508
  101.2 53.6 %copy-start.4 = (f32[1,392,128]{2,1,0:T(8,128)}, f32[1,392,128]{2,1,0:T(8,128)S(1)}, u32[]{:S(2)}) copy-start(f32[1,392,128]{2,1,0:T(8,128)S(1)} %collective-permute-done.1.refs_3_) | copy-start | bytes 602116
  101.2 25.2 %collective-permute-start.4 = (f32[1,392,128]{2,1,0:T(8,128)}, f32[1,392,128]{2,1,0:T(8,128)S(1)}, u32[]{:S(2)}, u32[]{:S(2)}) collective-permute-start(f32[1,392,128]{2,1,0:T(8,128)} %bitcast.27), channel_id=1, source_target_pairs={{0,12},{1,13},{2,14},{3,15},{4,8},{5,9},{6,10},{7,11},{8,4},{9,5},... | collective-permute-start | bytes 602120 | tf_op jit(solution)/shard_map/ppermute | solution.py:508
  104.6 50.3 %copy-start.5 = (f32[1,392,128]{2,1,0:T(8,128)}, f32[1,392,128]{2,1,0:T(8,128)S(1)}, u32[]{:S(2)}) copy-start(f32[1,392,128]{2,1,0:T(8,128)S(1)} %collective-permute-done.2.refs_4_) | copy-start | bytes 602116
  104.6 34.9 %collective-permute-start.5 = (f32[1,392,128]{2,1,0:T(8,128)}, f32[1,392,128]{2,1,0:T(8,128)S(1)}, u32[]{:S(2)}, u32[]{:S(2)}) collective-permute-start(f32[1,392,128]{2,1,0:T(8,128)} %bitcast.26), channel_id=1, source_target_pairs={{0,13},{1,12},{2,15},{3,14},{4,9},{5,8},{6,11},{7,10},{8,5},{9,4},... | collective-permute-start | bytes 602120 | tf_op jit(solution)/shard_map/ppermute | solution.py:508
  119.2 35.7 %copy-start.6 = (f32[1,392,128]{2,1,0:T(8,128)}, f32[1,392,128]{2,1,0:T(8,128)S(1)}, u32[]{:S(2)}) copy-start(f32[1,392,128]{2,1,0:T(8,128)S(1)} %collective-permute-done.3.refs_5_) | copy-start | bytes 602116
  119.2 24.5 %collective-permute-start.6 = (f32[1,392,128]{2,1,0:T(8,128)}, f32[1,392,128]{2,1,0:T(8,128)S(1)}, u32[]{:S(2)}, u32[]{:S(2)}) collective-permute-start(f32[1,392,128]{2,1,0:T(8,128)} %bitcast.25), channel_id=1, source_target_pairs={{0,14},{1,15},{2,12},{3,13},{4,10},{5,11},{6,8},{7,9},{8,6},{9,7},... | collective-permute-start | bytes 602120 | tf_op jit(solution)/shard_map/ppermute | solution.py:508
  126.4 28.5 %copy-start.7 = (f32[1,392,128]{2,1,0:T(8,128)}, f32[1,392,128]{2,1,0:T(8,128)S(1)}, u32[]{:S(2)}) copy-start(f32[1,392,128]{2,1,0:T(8,128)S(1)} %collective-permute-done.4.refs_6_) | copy-start | bytes 602116
  126.4 21.5 %collective-permute-start.7 = (f32[1,392,128]{2,1,0:T(8,128)S(1)}, f32[1,392,128]{2,1,0:T(8,128)S(1)}, u32[]{:S(2)}, u32[]{:S(2)}) collective-permute-start(f32[1,392,128]{2,1,0:T(8,128)S(1)} %bitcast.24), channel_id=1, source_target_pairs={{0,15},{1,14},{2,13},{3,12},{4,11},{5,10},{6,9},{7,8},{8,7},{9,6},... | collective-permute-start | bytes 602120 | tf_op jit(solution)/shard_map/ppermute | solution.py:508
  139.5 15.4 %copy-start.8 = (f32[1,392,128]{2,1,0:T(8,128)}, f32[1,392,128]{2,1,0:T(8,128)S(1)}, u32[]{:S(2)}) copy-start(f32[1,392,128]{2,1,0:T(8,128)S(1)} %collective-permute-done.5.refs_7_) | copy-start | bytes 602116
  143.7 11.2 %copy-start.9 = (f32[1,392,128]{2,1,0:T(8,128)}, f32[1,392,128]{2,1,0:T(8,128)S(1)}, u32[]{:S(2)}) copy-start(f32[1,392,128]{2,1,0:T(8,128)S(1)} %collective-permute-done.6.refs_8_) | copy-start | bytes 602116
  148.0 7.0 %copy-start.10 = (f32[1,392,128]{2,1,0:T(8,128)}, f32[1,392,128]{2,1,0:T(8,128)S(1)}, u32[]{:S(2)}) copy-start(f32[1,392,128]{2,1,0:T(8,128)S(1)} %collective-permute-done.7.refs_9_) | copy-start | bytes 602116
  148.6 6.4 %copy-start = (f32[8,392,128]{2,1,0:T(8,128)}, f32[8,392,128]{2,1,0:T(8,128)S(1)}, u32[]{:S(2)}) copy-start(f32[8,392,128]{2,1,0:T(8,128)S(1)} %all-to-all-done.1.refs_1_) | copy-start | bytes 4816900

commit v9 on v8

--- a/solution.py
+++ b/solution.py
@@ -254,7 +254,7 @@
             copy.wait()
 
 
-def spectra_call(first, count, parts, place, before, table, ranks, dead, fir_taps, samples):
+def spectra_call(first, count, sizes, row_of, before, table, fir_taps, samples):
     _, in_local, _ = samples.shape
     taps = fir_taps.shape[0]
     step_size = 2 * KB
@@ -262,10 +262,9 @@
     last = before is not None
     rows = count * in_local
     width = 2 * rows // LANES
-    devices = sum(parts)
-    capacity = BAND // devices + BAND // (2 * devices)
-    message = capacity * width + 8 * last
-    row_of = jnp.where(dead, -1, place * (message // 8) + ranks * (width // 8))
+    total_rows = sum(n * r for n, r in sizes)
+    message = sizes[0][1]
+    devices = sum(n for n, r in sizes if r == message)
 
     def frames_spec(offset):
         return pl.BlockSpec(
@@ -279,9 +278,9 @@
     def table_spec(index):
         return pl.BlockSpec((2, 2, 2, KB, LANES), lambda j, *_: (0, 0, 0, index(j), 0))
 
-    blocks = [jax.ShapeDtypeStruct((n * message, LANES), jnp.float32) for n in parts]
+    blocks = [jax.ShapeDtypeStruct((n * r, LANES), jnp.float32) for n, r in sizes]
     power = jax.ShapeDtypeStruct((8, LANES), jnp.float32)
-    whole = [pl.BlockSpec(memory_space=pl.ANY)] * len(parts)
+    whole = [pl.BlockSpec(memory_space=pl.ANY)] * len(sizes)
     single = [pl.BlockSpec(power.shape, lambda j, *_: (0, 0))]
     grid_spec = pltpu.PrefetchScalarGridSpec(
         num_scalar_prefetch=1,
@@ -301,12 +300,12 @@
         + [
             pltpu.VMEM((rows, 2 * BAND), jnp.float32),
             pltpu.VMEM((BAND * width, LANES), jnp.float32),
-            pltpu.VMEM((devices * message, LANES), jnp.float32),
-            pltpu.SemaphoreType.DMA((len(parts),)),
+            pltpu.VMEM((total_rows, LANES), jnp.float32),
+            pltpu.SemaphoreType.DMA((len(sizes),)),
         ],
     )
     results = pl.pallas_call(
-        functools.partial(spectra_kernel, count, last, devices, message, len(parts), taps, in_local),
+        functools.partial(spectra_kernel, count, last, devices, message, len(sizes), taps, in_local),
         out_shape=blocks + ([] if last else [power]),
         grid_spec=grid_spec,
         compiler_params=pltpu.CompilerParams(vmem_limit_bytes=60 * MIB),
@@ -325,8 +324,8 @@
         table,
         *([before] if last else []),
     )
-    sent = [r.reshape(n, message, LANES) for r, n in zip(results, parts)]
-    return sent + list(results[len(parts) :])
+    sent = [r.reshape(*size, LANES) for r, size in zip(results, sizes)]
+    return sent + list(results[len(sizes) :])
 
 
 def exchange_lanes(values, in_local):
@@ -347,8 +346,8 @@
     return values
 
 
-def correlate_kernel(widths, count, in_local, factor_ref, used_ref, index_ref, *refs):
-    near_a, near_b, *far_b = refs[:-8]
+def correlate_kernel(widths, low, count, distant, in_local, factor_ref, used_ref, index_ref, *refs):
+    near_a, near_b, *far_b = refs[: 2 + distant]
     out, left_0, right_0, left_1, right_1, second, staged, sems = refs[-8:]
     step, last = pl.program_id(0), count // 2 - 1
     per_tile = LANES // in_local
@@ -401,7 +400,7 @@
         return [
             pltpu.make_async_copy(
                 staged.at[buffer, part, pl.ds(half * nin // 2, nin // 2)],
-                out.at[index, part, pl.ds(half * nin // 2, nin // 2)],
+                out.at[low + index, part, pl.ds(half * nin // 2, nin // 2)],
                 sems.at[buffer, 2 * part + half],
             )
             for part in range(2)
@@ -456,20 +455,33 @@
             wait(jnp.int32(index))
 
 
-def correlate_call(received, widths, capacity, used, factor, index, in_local):
-    sources = received[0].shape[0]
+def correlate_call(
+    first, rest, begin, widths, low, high, capacity, used, factor, index, before, in_local
+):
+    sources = first.shape[0]
     nin = sources * in_local
-    count = capacity
-    in_specs = [pl.BlockSpec(memory_space=pltpu.SMEM)] * 3 + [
-        pl.BlockSpec((r.shape[0], 2 * width, LANES), lambda s: (0, s, 0))
-        for r, width in zip(received, widths[:1] + widths[1:] * len(received))
-    ]
+    count = high - low
+
+    def spec(block, width, start):
+        return pl.BlockSpec(
+            (block.shape[0], 2 * width, LANES), lambda s: (0, s + (low - start) // 2, 0)
+        )
+
+    in_specs = [pl.BlockSpec(memory_space=pltpu.SMEM)] * 3 + [spec(first, widths[0], 0)]
+    in_specs += [spec(block, widths[1], begin) for block in rest]
+    arrays = [first] + rest
+    aliases = {}
+    if before is not None:
+        in_specs.append(pl.BlockSpec(memory_space=pl.ANY))
+        aliases = {3 + len(arrays): 0}
+        arrays.append(before)
     return pl.pallas_call(
-        functools.partial(correlate_kernel, widths, count, in_local),
+        functools.partial(correlate_kernel, widths, low, count, len(rest) - 1, in_local),
         out_shape=jax.ShapeDtypeStruct((capacity, 2, nin, nin), jnp.bfloat16),
         grid=(count // 2,),
         in_specs=in_specs,
         out_specs=pl.BlockSpec(memory_space=pl.ANY),
+        input_output_aliases=aliases,
         scratch_shapes=[
             pltpu.VMEM((2, nin, LANES), jnp.bfloat16),
             pltpu.VMEM((2, 2 * nin // LANES, LANES, LANES), jnp.bfloat16),
@@ -487,7 +499,7 @@
             transcendentals=0,
         ),
         name="correlate",
-    )(factor, used, index, *received)
+    )(factor, used[low:high], index, *arrays)
 
 
 def exchange(block):
@@ -498,15 +510,16 @@
     devices = 2 * near.shape[0]
     half = near.shape[0]
     groups = [list(range(half)), list(range(half, devices))]
-    close = lax.all_to_all(
-        near, "feed", split_axis=0, concat_axis=0, axis_index_groups=groups, tiled=True
-    )
     arrived = []
     for k, block in enumerate(far):
         if k >= flight:
             block, arrived[k - flight] = lax.optimization_barrier((block, arrived[k - flight]))
         arrived.append(lax.ppermute(block, "feed", [(i, i ^ (half + k)) for i in range(devices)]))
-    return [close] + arrived
+    near, arrived[0] = lax.optimization_barrier((near, arrived[0]))
+    close = lax.all_to_all(
+        near, "feed", split_axis=0, concat_axis=0, axis_index_groups=groups, tiled=True
+    )
+    return close, arrived
 
 
 def channel_tables(owners, dropped_channels):
@@ -528,22 +541,46 @@
     call = functools.partial(
         spectra_call,
         table=jnp.asarray(folded_table()),
-        ranks=ranks,
-        dead=dead,
         fir_taps=fir_taps,
         samples=jnp.transpose(samples, (1, 0, 2)),
     )
     half = devices // 2
+    middle = capacity - 4
     me = lax.axis_index("feed")
+    widths = [2 * n * in_local // LANES for n in (FIRST, SPEC - FIRST)]
 
     def place(device):
         return jnp.where(device // half == me // half, device % half, half + (device ^ me) % half)
 
-    block_a, power = call(0, FIRST, [devices], owners, None)
+    rows = widths[0] // 8
+    block_a, power = call(
+        0,
+        FIRST,
+        [(devices, capacity * widths[0])],
+        jnp.where(dead, -1, (owners * capacity + ranks) * rows),
+        None,
+    )
     received_a = exchange(block_a)
-    near, *far = call(FIRST, SPEC - FIRST, [half] + [1] * half, place(owners), power)
+    rows = widths[1] // 8
+    head, tail = middle * rows + 1, (capacity - middle) * rows
+    row_of = jnp.where(
+        ranks < middle,
+        place(owners) * head + ranks * rows,
+        devices * head + owners * tail + (ranks - middle) * rows,
+    )
+    near, *far, block_c = call(
+        FIRST,
+        SPEC - FIRST,
+        [(half, 8 * head)] + [(1, 8 * head)] * half + [(devices, 8 * tail)],
+        jnp.where(dead, -1, row_of),
+        power,
+    )
     near, received_a = lax.optimization_barrier((near, received_a))
-    received_b = exchange_halves(near, far, 3)
+    close, arrived = exchange_halves(near, far, 3)
+    late = half - 3
+    block_c, close, arrived[late] = lax.optimization_barrier((block_c, close, arrived[late]))
+    received_c = exchange(block_c)
+    received_b = [close] + arrived
 
     kept = jnp.sum(jnp.logical_not(dead).astype(jnp.float32))
     mine = (owners == lax.axis_index("feed")) & jnp.logical_not(dead)
@@ -552,10 +589,26 @@
     powers = jnp.concatenate([block[:, -8:] for block in received_b])
     mean_power = jnp.sum(powers) / (NIN * SPEC * kept)
     factor = jnp.reshape(1.0 / (SPEC * mean_power), (1,))
-    widths = [2 * n * in_local // LANES for n in (FIRST, SPEC - FIRST)]
-    index = place(jnp.arange(devices, dtype=jnp.int32)).astype(jnp.int32)
-    return correlate_call(
-        [received_a] + received_b, widths, capacity, used, factor, index, in_local
+    everyone = jnp.arange(devices, dtype=jnp.int32)
+    run = functools.partial(
+        correlate_call,
+        widths=widths,
+        capacity=capacity,
+        used=used,
+        factor=factor,
+        in_local=in_local,
+    )
+    vis = run(
+        received_a,
+        received_b,
+        begin=0,
+        low=0,
+        high=middle,
+        index=place(everyone).astype(jnp.int32),
+        before=None,
+    )
+    return run(
+        received_a, [received_c], begin=middle, low=middle, high=capacity, index=everyone, before=vis
     )
 
 

time: 178 us -> 176 us (0.989)
  waiting for transfers between devices: 64.2 us -> 54 us
  starting transfers between devices: 18.9 us -> 24.1 us
  Pallas kernels: 74 us -> 76.6 us
    ppermute x8, waiting for transfers between devices: 61.6 us -> 54 us  [exchange_halves(): lax.ppermute(block, 'feed', [(i, i ^ half + k) for i in range(devices)])]
    all_to_all x1 -> x2, starting transfers between devices: 6.57 us -> 10.8 us  [exchange(): lax.all_to_all(block, 'feed', split_axis=0, concat_axis=0, tiled=True)]
    pallas_call x1 -> x2, Pallas kernels: 21.4 us -> 24.1 us  [correlate_call(): pl.pallas_call(functools.partial(correlate_kernel, widths, low, count, le...]
    all_to_all x1 -> x2, waiting for transfers between devices: 2.63 us -> 0.01 us  [exchange(): lax.all_to_all(block, 'feed', split_axis=0, concat_axis=0, tiled=True)]
  transfers between devices with their start and end apart: 10 -> 11, of which waited for: 9 -> 7; matrix products, arithmetic and copies ran while one was open for 4% -> 4% of each run, Pallas kernels for 19% -> 29%
where the time goes in v9:
time: 176 us; the launch traced here: 175 us
  Pallas kernels  76.6 us (44%)
  waiting for transfers between devices  54 us (31%)
  starting transfers between devices  24.1 us (14%)
  other arithmetic  11.8 us (7%)
  between operations  6.75 us (4%)
    ppermute x8, waiting for transfers between devices, exchange_halves(): lax.ppermute(block, 'feed', [(i, i ^ half + k) for i in range(devices)])  54 us
    pallas_call x2, Pallas kernels, spectra_call(): pl.pallas_call(functools.partial(spectra_kernel, count, last, devices, me...  52.6 us
    pallas_call x2, Pallas kernels, correlate_call(): pl.pallas_call(functools.partial(correlate_kernel, widths, low, count, le...  24.1 us
    all_to_all x2, starting transfers between devices, exchange(): lax.all_to_all(block, 'feed', split_axis=0, concat_axis=0, tiled=True)  10.8 us
    ppermute x8, starting transfers between devices, exchange_halves(): lax.ppermute(block, 'feed', [(i, i ^ half + k) for i in range(devices)])  8.2 us
    reduce_sum x9, other arithmetic, local_blocks(): mean_power = jnp.sum(powers) / (NIN * SPEC * kept)  6.43 us
    all_to_all x1, starting transfers between devices, exchange_halves(): lax.all_to_all(near, 'feed', split_axis=0, concat_axis=0, axis_index_grou...  5.05 us
  transfers between devices with their start and end apart: 11, of which 7 were waited for; matrix products, arithmetic and copies ran while one was open for 4% of the time, Pallas kernels for 29%

profile of v9, /device:TPU:13, one launch (start us, length us, event | category | flops | bytes accessed | tf_op | source)
XLA Modules:
  0.0 174.7 jit_solution(5296039434914330569)
XLA Ops:
  0.0 0.7 pad_add_fusion
  0.7 0.8 select_reduce_fusion
  1.5 0.7 compare_and_fusion
  2.2 1.3 add_select_fusion
  3.5 19.7 %spectra.2 = (f32[3072,128]{1,0:T(8,128)}, f32[8,128]{1,0:T(8,128)}) custom-call(s32[256]{0:T(256)} %get-tuple-element.65.refs_0_, f32[4,8192]{1,0:T(4,128)} %refs_2_.3, f32[4,8192]{1,0:T(4,128)} %refs_2_.3, bf16[51,32,8192]{2,1,0:T(8,128)(2,1)} %bitcast.15, bf16[51,32,8192]{2,1,0:T(8,128)(2,1)} %bitcast.16, ...), custom_call_target="tpu_custom_call" | custom-call | flops 6442450944 | bytes 31457280 | tf_op jit(solution)/shard_map/spectra/pallas_call | solution.py:307
  23.2 6.6 %all-to-all-start = ((f32[16,192,128]{2,1,0:T(8,128)}), f32[16,192,128]{2,1,0:T(8,128)S(1)}, u32[]{:S(2)}, u32[]{:S(2)}) async-start(f32[16,192,128]{2,1,0:T(8,128)} %bitcast.19), calls=%async_computation | async-start | bytes 3145728 | tf_op jit(solution)/shard_map/all_to_all | solution.py:506
  30.3 32.9 %spectra.3 = (f32[2624,128]{1,0:T(8,128)}, f32[328,128]{1,0:T(8,128)}, f32[328,128]{1,0:T(8,128)}, f32[328,128]{1,0:T(8,128)}, f32[328,128]{1,0:T(8,128)}, /*ind...) custom-call(s32[256]{0:T(256)} %fusion.5.refs_0_, ...), custom_call_target="tpu_custom_call" | custom-call | flops 12884901888 | bytes 31457280 | tf_op jit(solution)/shard_map/spectra/pallas_call | solution.py:307
  63.3 2.2 %collective-permute-start = (f32[1,328,128]{2,1,0:T(8,128)}, f32[1,328,128]{2,1,0:T(8,128)S(1)}, u32[]{:S(2)}, u32[]{:S(2)}) collective-permute-start(f32[1,328,128]{2,1,0:T(8,128)} %bitcast.33), channel_id=1, source_target_pairs={{0,8},{1,9},{2,10},{3,11},{4,12},{5,13},{6,14},{7,15},{8,0},{9,1},... | collective-permute-start | bytes 503816 | tf_op jit(solution)/shard_map/ppermute | solution.py:517
  65.4 7.9 %collective-permute-done.refs_2_ = f32[1,328,128]{2,1,0:T(8,128)S(1)} collective-permute-done((f32[1,328,128]{2,1,0:T(8,128)}, f32[1,328,128]{2,1,0:T(8,128)S(1)}, u32[]{:S(2)}, u32[]{:S(2)}) %collective-permute-start) | collective-permute-done | bytes 167968 | tf_op jit(solution)/shard_map/ppermute | solution.py:517
  73.4 5.1 %all-to-all-start.1 = ((f32[8,328,128]{2,1,0:T(8,128)}), f32[8,328,128]{2,1,0:T(8,128)S(1)}, u32[]{:S(2)}, u32[]{:S(2)}) async-start(f32[8,328,128]{2,1,0:T(8,128)} %bitcast.20), calls=%async_computation.1 | async-start | bytes 2686976 | tf_op jit(solution)/shard_map/all_to_all | solution.py:519
  78.4 2.3 %collective-permute-start.1 = (f32[1,328,128]{2,1,0:T(8,128)}, f32[1,328,128]{2,1,0:T(8,128)S(1)}, u32[]{:S(2)}, u32[]{:S(2)}) collective-permute-start(f32[1,328,128]{2,1,0:T(8,128)} %bitcast.8), channel_id=1, source_target_pairs={{0,10},{1,11},{2,8},{3,9},{4,14},{5,15},{6,12},{7,13},{8,2},{9,3},... | collective-permute-start | bytes 503816 | tf_op jit(solution)/shard_map/ppermute | solution.py:517
  83.8 3.0 %collective-permute-start.4 = (f32[1,328,128]{2,1,0:T(8,128)}, f32[1,328,128]{2,1,0:T(8,128)S(1)}, u32[]{:S(2)}, u32[]{:S(2)}) collective-permute-start(f32[1,328,128]{2,1,0:T(8,128)} %bitcast.31), channel_id=1, source_target_pairs={{0,11},{1,10},{2,9},{3,8},{4,15},{5,14},{6,13},{7,12},{8,3},{9,2},... | collective-permute-start | bytes 503816 | tf_op jit(solution)/shard_map/ppermute | solution.py:517
  86.8 12.9 %collective-permute-done.1.refs_4_ = f32[1,328,128]{2,1,0:T(8,128)S(1)} collective-permute-done((f32[1,328,128]{2,1,0:T(8,128)}, f32[1,328,128]{2,1,0:T(8,128)S(1)}, u32[]{:S(2)}, u32[]{:S(2)}) %collective-permute-start.1) | collective-permute-done | bytes 167968 | tf_op jit(solution)/shard_map/ppermute | solution.py:517
  100.3 3.9 %collective-permute-done.3.refs_3_ = f32[1,328,128]{2,1,0:T(8,128)S(1)} collective-permute-done((f32[1,328,128]{2,1,0:T(8,128)}, f32[1,328,128]{2,1,0:T(8,128)S(1)}, u32[]{:S(2)}, u32[]{:S(2)}) %collective-permute-start.3) | collective-permute-done | bytes 167968 | tf_op jit(solution)/shard_map/ppermute | solution.py:517
  104.2 0.7 slice_reduce_fusion.7
  104.9 2.7 %collective-permute-done.4.refs_5_ = f32[1,328,128]{2,1,0:T(8,128)S(1)} collective-permute-done((f32[1,328,128]{2,1,0:T(8,128)}, f32[1,328,128]{2,1,0:T(8,128)S(1)}, u32[]{:S(2)}, u32[]{:S(2)}) %collective-permute-start.4) | collective-permute-done | bytes 167968 | tf_op jit(solution)/shard_map/ppermute | solution.py:517
  108.4 20.6 %collective-permute-done.5.refs_6_ = f32[1,328,128]{2,1,0:T(8,128)S(1)} collective-permute-done((f32[1,328,128]{2,1,0:T(8,128)}, f32[1,328,128]{2,1,0:T(8,128)S(1)}, u32[]{:S(2)}, u32[]{:S(2)}) %collective-permute-start.5) | collective-permute-done | bytes 167968 | tf_op jit(solution)/shard_map/ppermute | solution.py:517
  129.6 2.8 %collective-permute-done.6.refs_8_ = f32[1,328,128]{2,1,0:T(8,128)S(1)} collective-permute-done((f32[1,328,128]{2,1,0:T(8,128)}, f32[1,328,128]{2,1,0:T(8,128)S(1)}, u32[]{:S(2)}, u32[]{:S(2)}) %collective-permute-start.6) | collective-permute-done | bytes 167968 | tf_op jit(solution)/shard_map/ppermute | solution.py:517
  133.1 3.2 %collective-permute-done.7.refs_9_ = f32[1,328,128]{2,1,0:T(8,128)S(1)} collective-permute-done((f32[1,328,128]{2,1,0:T(8,128)}, f32[1,328,128]{2,1,0:T(8,128)S(1)}, u32[]{:S(2)}, u32[]{:S(2)}) %collective-permute-start.7) | collective-permute-done | bytes 167968 | tf_op jit(solution)/shard_map/ppermute | solution.py:517
  136.3 0.7 slice_reduce_fusion.1
  137.6 1.3 slice_reduce_fusion.3
  139.6 4.2 %all-to-all-start.2 = ((f32[16,64,128]{2,1,0:T(8,128)}), f32[16,64,128]{2,1,0:T(8,128)S(1)}, u32[]{:S(2)}, u32[]{:S(2)}) async-start(f32[16,64,128]{2,1,0:T(8,128)} %bitcast.21), calls=%async_computation.2 | async-start | bytes 1048576 | tf_op jit(solution)/shard_map/all_to_all | solution.py:506
  149.6 18.3 %correlate.2.refs_2_ = bf16[24,2,512,512]{3,2,1,0:T(8,128)(2,1)} custom-call(f32[1]{0:T(128)} %bitcast.13.factor_ref, s32[20]{0:T(128)} %bitcast.34, s32[16]{0:T(128)} %compare_select_fusion.6.index_ref, f32[16,192,128]{2,1,0:T(8,128)} %copy-done, f32[8,328,128]{2,1,0:T(8,128)} %copy-done.2, f32[1,328,128]{2,1,0:T(8,128)} %copy-done.4, ...), custom_call_target="tpu_custom_call" | custom-call | flops 10737418240 | bytes 24903680 | tf_op jit(solution)/shard_map/correlate/pallas_call | solution.py:478
  168.7 5.8 %correlate.3 = bf16[24,2,512,512]{3,2,1,0:T(8,128)(2,1)} custom-call(f32[1]{0:T(128)} %bitcast.13.factor_ref, s32[4]{0:T(128)} %slice.42.used_ref, s32[16]{0:T(128)} %iota.25.index_ref, f32[16,192,128]{2,1,0:T(8,128)} %copy-done, f32[16,64,128]{2,1,0:T(8,128)} %copy-done.1, bf16[24,2,512,512]{3,2,1,0:T(8,128)(2,1)} %correlate.2.refs_2_), custom_call_target="tpu_custom_call", output_to_operand_aliasing={{}: (5, {})} | custom-call | flops 2147483648 | bytes 4980736 | tf_op jit(solution)/shard_map/correlate/pallas_call | solution.py:478
  (47 shorter events, 7.8 us)
Async XLA Ops:
  23.2 6.6 %copy-start.3 = (s32[256,1]{0,1:T(1,128)S(1)}, s32[256,1]{0,1:T(1,128)}, u32[]{:S(2)}) copy-start(s32[256,1]{0,1:T(1,128)} %param.7) | copy-start | bytes 3076
  23.2 50.2 %all-to-all-start = ((f32[16,192,128]{2,1,0:T(8,128)}), f32[16,192,128]{2,1,0:T(8,128)S(1)}, u32[]{:S(2)}, u32[]{:S(2)}) async-start(f32[16,192,128]{2,1,0:T(8,128)} %bitcast.19), calls=%async_computation | async-start | bytes 3145728 | tf_op jit(solution)/shard_map/all_to_all | solution.py:506
  63.3 10.1 %collective-permute-start = (f32[1,328,128]{2,1,0:T(8,128)}, f32[1,328,128]{2,1,0:T(8,128)S(1)}, u32[]{:S(2)}, u32[]{:S(2)}) collective-permute-start(f32[1,328,128]{2,1,0:T(8,128)} %bitcast.33), channel_id=1, source_target_pairs={{0,8},{1,9},{2,10},{3,11},{4,12},{5,13},{6,14},{7,15},{8,0},{9,1},... | collective-permute-start | bytes 503816 | tf_op jit(solution)/shard_map/ppermute | solution.py:517
  73.4 66.2 %copy-start.4 = (f32[1,328,128]{2,1,0:T(8,128)}, f32[1,328,128]{2,1,0:T(8,128)S(1)}, u32[]{:S(2)}) copy-start(f32[1,328,128]{2,1,0:T(8,128)S(1)} %collective-permute-done.refs_2_) | copy-start | bytes 503812
  73.4 66.2 %copy-start = (f32[16,192,128]{2,1,0:T(8,128)}, f32[16,192,128]{2,1,0:T(8,128)S(1)}, u32[]{:S(2)}) copy-start(f32[16,192,128]{2,1,0:T(8,128)S(1)} %all-to-all-done.refs_0_) | copy-start | bytes 4718596
  73.4 64.2 %all-to-all-start.1 = ((f32[8,328,128]{2,1,0:T(8,128)}), f32[8,328,128]{2,1,0:T(8,128)S(1)}, u32[]{:S(2)}, u32[]{:S(2)}) async-start(f32[8,328,128]{2,1,0:T(8,128)} %bitcast.20), calls=%async_computation.1 | async-start | bytes 2686976 | tf_op jit(solution)/shard_map/all_to_all | solution.py:519
  78.4 21.2 %collective-permute-start.1 = (f32[1,328,128]{2,1,0:T(8,128)}, f32[1,328,128]{2,1,0:T(8,128)S(1)}, u32[]{:S(2)}, u32[]{:S(2)}) collective-permute-start(f32[1,328,128]{2,1,0:T(8,128)} %bitcast.8), channel_id=1, source_target_pairs={{0,10},{1,11},{2,8},{3,9},{4,14},{5,15},{6,12},{7,13},{8,2},{9,3},... | collective-permute-start | bytes 503816 | tf_op jit(solution)/shard_map/ppermute | solution.py:517
  80.7 23.5 %collective-permute-start.3 = (f32[1,328,128]{2,1,0:T(8,128)}, f32[1,328,128]{2,1,0:T(8,128)S(1)}, u32[]{:S(2)}, u32[]{:S(2)}) collective-permute-start(f32[1,328,128]{2,1,0:T(8,128)} %bitcast.32), channel_id=1, source_target_pairs={{0,9},{1,8},{2,11},{3,10},{4,13},{5,12},{6,15},{7,14},{8,1},{9,0},... | collective-permute-start | bytes 503816 | tf_op jit(solution)/shard_map/ppermute | solution.py:517
  82.6 67.0 %copy-start.11 = (s32[24]{0:T(128)}, s32[24]{0:T(128)S(1)}, u32[]{:S(2)}) copy-start(s32[24]{0:T(128)S(1)} %convert_element_type.11) | copy-start | bytes 292
  83.8 23.8 %collective-permute-start.4 = (f32[1,328,128]{2,1,0:T(8,128)}, f32[1,328,128]{2,1,0:T(8,128)S(1)}, u32[]{:S(2)}, u32[]{:S(2)}) collective-permute-start(f32[1,328,128]{2,1,0:T(8,128)} %bitcast.31), channel_id=1, source_target_pairs={{0,11},{1,10},{2,9},{3,8},{4,15},{5,14},{6,13},{7,12},{8,3},{9,2},... | collective-permute-start | bytes 503816 | tf_op jit(solution)/shard_map/ppermute | solution.py:517
  99.6 39.9 %copy-start.5 = (f32[1,328,128]{2,1,0:T(8,128)}, f32[1,328,128]{2,1,0:T(8,128)S(1)}, u32[]{:S(2)}) copy-start(f32[1,328,128]{2,1,0:T(8,128)S(1)} %collective-permute-done.1.refs_4_) | copy-start | bytes 503812
  100.3 37.3 %collective-permute-start.2 = (f32[1,328,128]{2,1,0:T(8,128)}, f32[1,328,128]{2,1,0:T(8,128)}, u32[]{:S(2)}, u32[]{:S(2)}) collective-permute-start(f32[1,328,128]{2,1,0:T(8,128)} %bitcast.27), channel_id=1, source_target_pairs={{0,13},{1,12},{2,15},{3,14},{4,9},{5,8},{6,11},{7,10},{8,5},{9,4},... | collective-permute-start | bytes 503816 | tf_op jit(solution)/shard_map/ppermute | solution.py:517
  104.2 35.4 %copy-start.6 = (f32[1,328,128]{2,1,0:T(8,128)}, f32[1,328,128]{2,1,0:T(8,128)S(1)}, u32[]{:S(2)}) copy-start(f32[1,328,128]{2,1,0:T(8,128)S(1)} %collective-permute-done.3.refs_3_) | copy-start | bytes 503812
  104.2 24.8 %collective-permute-start.5 = (f32[1,328,128]{2,1,0:T(8,128)}, f32[1,328,128]{2,1,0:T(8,128)S(1)}, u32[]{:S(2)}, u32[]{:S(2)}) collective-permute-start(f32[1,328,128]{2,1,0:T(8,128)} %bitcast.30), channel_id=1, source_target_pairs={{0,12},{1,13},{2,14},{3,15},{4,8},{5,9},{6,10},{7,11},{8,4},{9,5},... | collective-permute-start | bytes 503816 | tf_op jit(solution)/shard_map/ppermute | solution.py:517
  107.6 30.0 %copy-start.7 = (f32[1,328,128]{2,1,0:T(8,128)}, f32[1,328,128]{2,1,0:T(8,128)S(1)}, u32[]{:S(2)}) copy-start(f32[1,328,128]{2,1,0:T(8,128)S(1)} %collective-permute-done.4.refs_5_) | copy-start | bytes 503812
  107.6 24.9 %collective-permute-start.6 = (f32[1,328,128]{2,1,0:T(8,128)}, f32[1,328,128]{2,1,0:T(8,128)S(1)}, u32[]{:S(2)}, u32[]{:S(2)}) collective-permute-start(f32[1,328,128]{2,1,0:T(8,128)} %bitcast.29), channel_id=1, source_target_pairs={{0,14},{1,15},{2,12},{3,13},{4,10},{5,11},{6,8},{7,9},{8,6},{9,7},... | collective-permute-start | bytes 503816 | tf_op jit(solution)/shard_map/ppermute | solution.py:517
  129.0 8.6 %copy-start.8 = (f32[1,328,128]{2,1,0:T(8,128)}, f32[1,328,128]{2,1,0:T(8,128)S(1)}, u32[]{:S(2)}) copy-start(f32[1,328,128]{2,1,0:T(8,128)S(1)} %collective-permute-done.5.refs_6_) | copy-start | bytes 503812
  129.0 7.3 %collective-permute-start.7 = (f32[1,328,128]{2,1,0:T(8,128)}, f32[1,328,128]{2,1,0:T(8,128)S(1)}, u32[]{:S(2)}, u32[]{:S(2)}) collective-permute-start(f32[1,328,128]{2,1,0:T(8,128)} %bitcast.28), channel_id=1, source_target_pairs={{0,15},{1,14},{2,13},{3,12},{4,11},{5,10},{6,9},{7,8},{8,7},{9,6},... | collective-permute-start | bytes 503816 | tf_op jit(solution)/shard_map/ppermute | solution.py:517
  132.5 5.1 %copy-start.9 = (f32[1,328,128]{2,1,0:T(8,128)}, f32[1,328,128]{2,1,0:T(8,128)S(1)}, u32[]{:S(2)}) copy-start(f32[1,328,128]{2,1,0:T(8,128)S(1)} %collective-permute-done.6.refs_8_) | copy-start | bytes 503812
  136.3 1.3 copy-start.10
  137.6 12.0 %copy-start.2 = (f32[8,328,128]{2,1,0:T(8,128)}, f32[8,328,128]{2,1,0:T(8,128)S(1)}, u32[]{:S(2)}) copy-start(f32[8,328,128]{2,1,0:T(8,128)S(1)} %all-to-all-done.1.refs_1_) | copy-start | bytes 4030468
  139.6 28.4 %all-to-all-start.2 = ((f32[16,64,128]{2,1,0:T(8,128)}), f32[16,64,128]{2,1,0:T(8,128)S(1)}, u32[]{:S(2)}, u32[]{:S(2)}) async-start(f32[16,64,128]{2,1,0:T(8,128)} %bitcast.21), calls=%async_computation.2 | async-start | bytes 1048576 | tf_op jit(solution)/shard_map/all_to_all | solution.py:506
  167.9 0.8 copy-start.1

commit v10 on v9

--- a/solution.py
+++ b/solution.py
@@ -515,7 +515,6 @@
         if k >= flight:
             block, arrived[k - flight] = lax.optimization_barrier((block, arrived[k - flight]))
         arrived.append(lax.ppermute(block, "feed", [(i, i ^ (half + k)) for i in range(devices)]))
-    near, arrived[0] = lax.optimization_barrier((near, arrived[0]))
     close = lax.all_to_all(
         near, "feed", split_axis=0, concat_axis=0, axis_index_groups=groups, tiled=True
     )
@@ -545,7 +544,7 @@
         samples=jnp.transpose(samples, (1, 0, 2)),
     )
     half = devices // 2
-    middle = capacity - 4
+    middle = capacity * 2 // 3
     me = lax.axis_index("feed")
     widths = [2 * n * in_local // LANES for n in (FIRST, SPEC - FIRST)]
 
@@ -562,32 +561,30 @@
     )
     received_a = exchange(block_a)
     rows = widths[1] // 8
-    head, tail = middle * rows + 1, (capacity - middle) * rows
+    head, tail = middle * rows, (capacity - middle) * rows + 1
     row_of = jnp.where(
         ranks < middle,
-        place(owners) * head + ranks * rows,
-        devices * head + owners * tail + (ranks - middle) * rows,
-    )
-    near, *far, block_c = call(
+        devices * tail + place(owners) * head + ranks * rows,
+        owners * tail + (ranks - middle) * rows,
+    )
+    block_c, near, *far = call(
         FIRST,
         SPEC - FIRST,
-        [(half, 8 * head)] + [(1, 8 * head)] * half + [(devices, 8 * tail)],
+        [(devices, 8 * tail), (half, 8 * head)] + [(1, 8 * head)] * half,
         jnp.where(dead, -1, row_of),
         power,
     )
-    near, received_a = lax.optimization_barrier((near, received_a))
+    block_c, received_a = lax.optimization_barrier((block_c, received_a))
+    received_c = exchange(block_c)
+    near, received_c = lax.optimization_barrier((near, received_c))
     close, arrived = exchange_halves(near, far, 3)
-    late = half - 3
-    block_c, close, arrived[late] = lax.optimization_barrier((block_c, close, arrived[late]))
-    received_c = exchange(block_c)
     received_b = [close] + arrived
 
     kept = jnp.sum(jnp.logical_not(dead).astype(jnp.float32))
     mine = (owners == lax.axis_index("feed")) & jnp.logical_not(dead)
     slots = jnp.arange(capacity, dtype=jnp.int32)
     used = jnp.any((ranks[None, :] == slots[:, None]) & mine[None, :], axis=1).astype(jnp.int32)
-    powers = jnp.concatenate([block[:, -8:] for block in received_b])
-    mean_power = jnp.sum(powers) / (NIN * SPEC * kept)
+    mean_power = jnp.sum(received_c[:, -8:]) / (NIN * SPEC * kept)
     factor = jnp.reshape(1.0 / (SPEC * mean_power), (1,))
     everyone = jnp.arange(devices, dtype=jnp.int32)
     run = functools.partial(
@@ -599,16 +596,16 @@
         in_local=in_local,
     )
     vis = run(
+        received_a, [received_c], begin=middle, low=middle, high=capacity, index=everyone, before=None
+    )
+    return run(
         received_a,
         received_b,
         begin=0,
         low=0,
         high=middle,
         index=place(everyone).astype(jnp.int32),
-        before=None,
-    )
-    return run(
-        received_a, [received_c], begin=middle, low=middle, high=capacity, index=everyone, before=vis
+        before=vis,
     )
 
 

time: 176 us -> 171 us (0.972)
  blocking collectives: 0 us -> 31.3 us
  waiting for transfers between devices: 54 us -> 32.1 us
  other arithmetic: 11.8 us -> 6.01 us
  between operations: 6.75 us -> 1.7 us
  starting transfers between devices: 24.1 us -> 20.1 us
    all_to_all x0 -> x1, blocking collectives: none -> 31.3 us  [exchange(): lax.all_to_all(block, 'feed', split_axis=0, concat_axis=0, tiled=True)]
    ppermute x8, waiting for transfers between devices: 54 us -> 29.5 us  [exchange_halves(): lax.ppermute(block, 'feed', [(i, i ^ half + k) for i in range(devices)])]
    reduce_sum x9 -> x1, other arithmetic: 6.43 us -> 0.61 us  [local_blocks(): mean_power = jnp.sum(received_c[:, -8:]) / (NIN * SPEC * kept)]
    all_to_all x2 -> x1, starting transfers between devices: 10.8 us -> 6.57 us  [exchange(): lax.all_to_all(block, 'feed', split_axis=0, concat_axis=0, tiled=True)]
    all_to_all x2 -> x1, waiting for transfers between devices: 0.01 us -> 2.63 us  [exchange(): lax.all_to_all(block, 'feed', split_axis=0, concat_axis=0, tiled=True)]
  transfers between devices with their start and end apart: 11 -> 10, of which waited for: 7 -> 6; matrix products, arithmetic and copies ran while one was open for 4% -> 2% of each run, Pallas kernels for 29% -> 25%
where the time goes in v10:
time: 171 us; the launch traced here: 169 us
  Pallas kernels  76.3 us (45%)
  waiting for transfers between devices  32.1 us (19%)
  blocking collectives  31.3 us (18%)
  starting transfers between devices  20.1 us (12%)
  other arithmetic  6.01 us (4%)
  local copies, waits for them, and re-layouts  1.81 us (1%)
    pallas_call x2, Pallas kernels, spectra_call(): pl.pallas_call(functools.partial(spectra_kernel, count, last, devices, me...  52.6 us
    all_to_all x1, blocking collectives, exchange(): lax.all_to_all(block, 'feed', split_axis=0, concat_axis=0, tiled=True)  31.3 us
    ppermute x8, waiting for transfers between devices, exchange_halves(): lax.ppermute(block, 'feed', [(i, i ^ half + k) for i in range(devices)])  29.5 us
    pallas_call x2, Pallas kernels, correlate_call(): pl.pallas_call(functools.partial(correlate_kernel, widths, low, count, le...  23.7 us
    ppermute x8, starting transfers between devices, exchange_halves(): lax.ppermute(block, 'feed', [(i, i ^ half + k) for i in range(devices)])  6.93 us
    all_to_all x1, starting transfers between devices, exchange(): lax.all_to_all(block, 'feed', split_axis=0, concat_axis=0, tiled=True)  6.57 us
    all_to_all x1, starting transfers between devices, exchange_halves(): lax.all_to_all(near, 'feed', split_axis=0, concat_axis=0, axis_index_grou...  6.57 us
  transfers between devices with their start and end apart: 10, of which 6 were waited for; matrix products, arithmetic and copies ran while one was open for 2% of the time, Pallas kernels for 25%

profile of v10, /device:TPU:13, one launch (start us, length us, event | category | flops | bytes accessed | tf_op | source)
XLA Modules:
  0.0 169.2 jit_solution(3086323141385499676)
XLA Ops:
  0.0 0.7 pad_add_fusion
  0.7 0.8 select_reduce_fusion
  1.5 0.7 compare_and_fusion
  2.2 1.2 add_select_fusion
  3.5 19.7 %spectra.2 = (f32[3072,128]{1,0:T(8,128)}, f32[8,128]{1,0:T(8,128)}) custom-call(s32[256]{0:T(256)} %get-tuple-element.59.refs_0_, f32[4,8192]{1,0:T(4,128)} %refs_2_.3, f32[4,8192]{1,0:T(4,128)} %refs_2_.3, bf16[51,32,8192]{2,1,0:T(8,128)(2,1)} %bitcast.15, bf16[51,32,8192]{2,1,0:T(8,128)(2,1)} %bitcast.16, ...), custom_call_target="tpu_custom_call" | custom-call | flops 6442450944 | bytes 31457280 | tf_op jit(solution)/shard_map/spectra/pallas_call | solution.py:307
  23.1 6.6 %all-to-all-start = ((f32[16,192,128]{2,1,0:T(8,128)}), f32[16,192,128]{2,1,0:T(8,128)S(1)}, u32[]{:S(2)}, u32[]{:S(2)}) async-start(f32[16,192,128]{2,1,0:T(8,128)} %bitcast.19), calls=%async_computation | async-start | bytes 3145728 | tf_op jit(solution)/shard_map/all_to_all | solution.py:506
  29.7 0.6 fusion.5.refs_0_
  30.3 32.9 %spectra.3 = (f32[2176,128]{1,0:T(8,128)}, f32[2048,128]{1,0:T(8,128)}, f32[256,128]{1,0:T(8,128)}, f32[256,128]{1,0:T(8,128)}, f32[256,128]{1,0:T(8,128)}, /*in...) custom-call(s32[256]{0:T(256)} %fusion.5.refs_0_, ...), custom_call_target="tpu_custom_call" | custom-call | flops 12884901888 | bytes 31457280 | tf_op jit(solution)/shard_map/spectra/pallas_call | solution.py:307
  63.3 2.6 %all-to-all-done.refs_0_ = f32[16,192,128]{2,1,0:T(8,128)S(1)} async-done(((f32[16,192,128]{2,1,0:T(8,128)}), f32[16,192,128]{2,1,0:T(8,128)S(1)}, u32[]{:S(2)}, u32[]{:S(2)}) %all-to-all-start) | async-done | bytes 1572896 | tf_op jit(solution)/shard_map/all_to_all | solution.py:506
  65.9 31.3 %all_to_all.15.refs_1_ = f32[16,136,128]{2,1,0:T(8,128)S(1)} all-to-all(f32[16,136,128]{2,1,0:T(8,128)} %bitcast.20), channel_id=1, replica_groups=mesh['grp'=2,'feed'=16] {'feed'}, dimensions={0} | all-to-all | bytes 2228224 | tf_op jit(solution)/shard_map/all_to_all | solution.py:506
  97.2 6.6 %all-to-all-start.2 = ((f32[8,256,128]{2,1,0:T(8,128)}), f32[8,256,128]{2,1,0:T(8,128)}, u32[]{:S(2)}, u32[]{:S(2)}) async-start(f32[8,256,128]{2,1,0:T(8,128)} %bitcast.21), calls=%async_computation.2 | async-start | bytes 2097152 | tf_op jit(solution)/shard_map/all_to_all | solution.py:518
  104.3 2.3 %collective-permute-start.1 = (f32[1,256,128]{2,1,0:T(8,128)}, f32[1,256,128]{2,1,0:T(8,128)S(1)}, u32[]{:S(2)}, u32[]{:S(2)}) collective-permute-start(f32[1,256,128]{2,1,0:T(8,128)} %bitcast.34), channel_id=1, source_target_pairs={{0,9},{1,8},{2,11},{3,10},{4,13},{5,12},{6,15},{7,14},{8,1},{9,0},... | collective-permute-start | bytes 393224 | tf_op jit(solution)/shard_map/ppermute | solution.py:517
  107.3 12.0 %collective-permute-done.refs_2_ = f32[1,256,128]{2,1,0:T(8,128)S(1)} collective-permute-done((f32[1,256,128]{2,1,0:T(8,128)}, f32[1,256,128]{2,1,0:T(8,128)S(1)}, u32[]{:S(2)}, u32[]{:S(2)}) %collective-permute-start) | collective-permute-done | bytes 131104 | tf_op jit(solution)/shard_map/ppermute | solution.py:517
  119.9 3.2 %collective-permute-done.1.refs_3_ = f32[1,256,128]{2,1,0:T(8,128)S(1)} collective-permute-done((f32[1,256,128]{2,1,0:T(8,128)}, f32[1,256,128]{2,1,0:T(8,128)S(1)}, u32[]{:S(2)}, u32[]{:S(2)}) %collective-permute-start.1) | collective-permute-done | bytes 131104 | tf_op jit(solution)/shard_map/ppermute | solution.py:517
  123.1 0.9 collective-permute-start.4
  126.8 8.5 %collective-permute-done.3.refs_5_ = f32[1,256,128]{2,1,0:T(8,128)S(1)} collective-permute-done((f32[1,256,128]{2,1,0:T(8,128)S(1)}, f32[1,256,128]{2,1,0:T(8,128)S(1)}, u32[]{:S(2)}, u32[]{:S(2)}) %collective-permute-start.3) | collective-permute-done | bytes 131104 | tf_op jit(solution)/shard_map/ppermute | solution.py:517
  135.3 0.7 collective-permute-start.6
  136.0 3.4 %collective-permute-done.4.refs_6_ = f32[1,256,128]{2,1,0:T(8,128)S(1)} collective-permute-done((f32[1,256,128]{2,1,0:T(8,128)S(1)}, f32[1,256,128]{2,1,0:T(8,128)S(1)}, u32[]{:S(2)}, u32[]{:S(2)}) %collective-permute-start.4) | collective-permute-done | bytes 131104 | tf_op jit(solution)/shard_map/ppermute | solution.py:517
  139.4 1.0 collective-permute-start.7
  140.4 0.6 slice_reduce_fusion
  142.3 8.8 %correlate.2.refs_10_ = bf16[24,2,512,512]{3,2,1,0:T(8,128)(2,1)} custom-call(f32[1]{0:T(128)} %bitcast.5.factor_ref, s32[8]{0:T(128)} %slice.11.used_ref, s32[16]{0:T(128)} %iota.27.index_ref, f32[16,192,128]{2,1,0:T(8,128)} %copy-done, f32[16,136,128]{2,1,0:T(8,128)} %copy-done.1), custom_call_target="tpu_custom_call" | custom-call | flops 4294967296 | bytes 9961472 | tf_op jit(solution)/shard_map/correlate/pallas_call | solution.py:478
  151.2 2.3 %collective-permute-done.7.refs_9_ = f32[1,256,128]{2,1,0:T(8,128)S(1)} collective-permute-done((f32[1,256,128]{2,1,0:T(8,128)S(1)}, f32[1,256,128]{2,1,0:T(8,128)S(1)}, u32[]{:S(2)}, u32[]{:S(2)}) %collective-permute-start.7) | collective-permute-done | bytes 131104 | tf_op jit(solution)/shard_map/ppermute | solution.py:517
  153.5 0.6 copy-done.9
  154.2 14.9 %correlate.3 = bf16[24,2,512,512]{3,2,1,0:T(8,128)(2,1)} custom-call(f32[1]{0:T(128)} %bitcast.5.factor_ref, s32[16]{0:T(128)} %bitcast.27, s32[16]{0:T(128)} %compare_select_fusion.6.index_ref, f32[16,192,128]{2,1,0:T(8,128)} %copy-done, f32[8,256,128]{2,1,0:T(8,128)} %all-to-all-done.2.refs_1_, ...), custom_call_target="tpu_custom_call", output_to_operand_aliasing={{}: (13, {})} | custom-call | flops 8589934592 | bytes 19922944 | tf_op jit(solution)/shard_map/correlate/pallas_call | solution.py:478
  (50 shorter events, 4.5 us)
Async XLA Ops:
  23.1 42.8 %all-to-all-start = ((f32[16,192,128]{2,1,0:T(8,128)}), f32[16,192,128]{2,1,0:T(8,128)S(1)}, u32[]{:S(2)}, u32[]{:S(2)}) async-start(f32[16,192,128]{2,1,0:T(8,128)} %bitcast.19), calls=%async_computation | async-start | bytes 3145728 | tf_op jit(solution)/shard_map/all_to_all | solution.py:506
  65.9 31.3 %copy-start = (f32[16,192,128]{2,1,0:T(8,128)}, f32[16,192,128]{2,1,0:T(8,128)S(1)}, u32[]{:S(2)}) copy-start(f32[16,192,128]{2,1,0:T(8,128)S(1)} %all-to-all-done.refs_0_) | copy-start | bytes 4718596
  97.2 45.1 %copy-start.1 = (f32[16,136,128]{2,1,0:T(8,128)}, f32[16,136,128]{2,1,0:T(8,128)S(1)}, u32[]{:S(2)}) copy-start(f32[16,136,128]{2,1,0:T(8,128)S(1)} %all_to_all.15.refs_1_) | copy-start | bytes 3342340
  97.2 9.5 %copy-start.17 = (f32[256,128]{1,0:T(8,128)S(1)}, f32[256,128]{1,0:T(8,128)}, u32[]{:S(2)}) copy-start(f32[256,128]{1,0:T(8,128)} %get-tuple-element.46) | copy-start | bytes 393220
  97.2 22.2 %copy-start.16 = (f32[256,128]{1,0:T(8,128)S(1)}, f32[256,128]{1,0:T(8,128)}, u32[]{:S(2)}) copy-start(f32[256,128]{1,0:T(8,128)} %get-tuple-element.39) | copy-start | bytes 393220
  97.2 25.9 %copy-start.15 = (f32[256,128]{1,0:T(8,128)S(1)}, f32[256,128]{1,0:T(8,128)}, u32[]{:S(2)}) copy-start(f32[256,128]{1,0:T(8,128)} %get-tuple-element.42) | copy-start | bytes 393220
  97.2 29.3 %copy-start.14 = (f32[256,128]{1,0:T(8,128)S(1)}, f32[256,128]{1,0:T(8,128)}, u32[]{:S(2)}) copy-start(f32[256,128]{1,0:T(8,128)} %get-tuple-element.45) | copy-start | bytes 393220
  97.2 38.1 %copy-start.13 = (f32[256,128]{1,0:T(8,128)S(1)}, f32[256,128]{1,0:T(8,128)}, u32[]{:S(2)}) copy-start(f32[256,128]{1,0:T(8,128)} %get-tuple-element.48) | copy-start | bytes 393220
  97.2 42.2 %copy-start.12 = (f32[256,128]{1,0:T(8,128)S(1)}, f32[256,128]{1,0:T(8,128)}, u32[]{:S(2)}) copy-start(f32[256,128]{1,0:T(8,128)} %get-tuple-element.51) | copy-start | bytes 393220
  97.2 56.3 %all-to-all-start.2 = ((f32[8,256,128]{2,1,0:T(8,128)}), f32[8,256,128]{2,1,0:T(8,128)}, u32[]{:S(2)}, u32[]{:S(2)}) async-start(f32[8,256,128]{2,1,0:T(8,128)} %bitcast.21), calls=%async_computation.2 | async-start | bytes 2097152 | tf_op jit(solution)/shard_map/all_to_all | solution.py:518
  103.8 15.6 %collective-permute-start = (f32[1,256,128]{2,1,0:T(8,128)}, f32[1,256,128]{2,1,0:T(8,128)S(1)}, u32[]{:S(2)}, u32[]{:S(2)}) collective-permute-start(f32[1,256,128]{2,1,0:T(8,128)} %bitcast.35), channel_id=1, source_target_pairs={{0,8},{1,9},{2,10},{3,11},{4,12},{5,13},{6,14},{7,15},{8,0},{9,1},... | collective-permute-start | bytes 393224 | tf_op jit(solution)/shard_map/ppermute | solution.py:517
  104.3 18.8 %collective-permute-start.1 = (f32[1,256,128]{2,1,0:T(8,128)}, f32[1,256,128]{2,1,0:T(8,128)S(1)}, u32[]{:S(2)}, u32[]{:S(2)}) collective-permute-start(f32[1,256,128]{2,1,0:T(8,128)} %bitcast.34), channel_id=1, source_target_pairs={{0,9},{1,8},{2,11},{3,10},{4,13},{5,12},{6,15},{7,14},{8,1},{9,0},... | collective-permute-start | bytes 393224 | tf_op jit(solution)/shard_map/ppermute | solution.py:517
  106.7 19.8 %collective-permute-start.2 = (f32[1,256,128]{2,1,0:T(8,128)S(1)}, f32[1,256,128]{2,1,0:T(8,128)S(1)}, u32[]{:S(2)}, u32[]{:S(2)}) collective-permute-start(f32[1,256,128]{2,1,0:T(8,128)S(1)} %bitcast.33), channel_id=1, source_target_pairs={{0,10},{1,11},{2,8},{3,9},{4,14},{5,15},{6,12},{7,13},{8,2},{9,3},... | collective-permute-start | bytes 393224 | tf_op jit(solution)/shard_map/ppermute | solution.py:517
  119.4 31.7 %copy-start.2 = (f32[1,256,128]{2,1,0:T(8,128)}, f32[1,256,128]{2,1,0:T(8,128)S(1)}, u32[]{:S(2)}) copy-start(f32[1,256,128]{2,1,0:T(8,128)S(1)} %collective-permute-done.refs_2_) | copy-start | bytes 393220
  119.4 15.9 %collective-permute-start.3 = (f32[1,256,128]{2,1,0:T(8,128)S(1)}, f32[1,256,128]{2,1,0:T(8,128)S(1)}, u32[]{:S(2)}, u32[]{:S(2)}) collective-permute-start(f32[1,256,128]{2,1,0:T(8,128)S(1)} %bitcast.32), channel_id=1, source_target_pairs={{0,11},{1,10},{2,9},{3,8},{4,15},{5,14},{6,13},{7,12},{8,3},{9,2},... | collective-permute-start | bytes 393224 | tf_op jit(solution)/shard_map/ppermute | solution.py:517
  123.1 28.0 %copy-start.3 = (f32[1,256,128]{2,1,0:T(8,128)}, f32[1,256,128]{2,1,0:T(8,128)S(1)}, u32[]{:S(2)}) copy-start(f32[1,256,128]{2,1,0:T(8,128)S(1)} %collective-permute-done.1.refs_3_) | copy-start | bytes 393220
  123.1 16.3 %collective-permute-start.4 = (f32[1,256,128]{2,1,0:T(8,128)S(1)}, f32[1,256,128]{2,1,0:T(8,128)S(1)}, u32[]{:S(2)}, u32[]{:S(2)}) collective-permute-start(f32[1,256,128]{2,1,0:T(8,128)S(1)} %bitcast.31), channel_id=1, source_target_pairs={{0,12},{1,13},{2,14},{3,15},{4,8},{5,9},{6,10},{7,11},{8,4},{9,5},... | collective-permute-start | bytes 393224 | tf_op jit(solution)/shard_map/ppermute | solution.py:517
  124.6 26.5 %copy-start.11 = (s32[24]{0:T(128)}, s32[24]{0:T(128)S(1)}, u32[]{:S(2)}) copy-start(s32[24]{0:T(128)S(1)} %convert_element_type.11) | copy-start | bytes 292
  126.5 24.6 %copy-start.4 = (f32[1,256,128]{2,1,0:T(8,128)}, f32[1,256,128]{2,1,0:T(8,128)S(1)}, u32[]{:S(2)}) copy-start(f32[1,256,128]{2,1,0:T(8,128)S(1)} %collective-permute-done.2.refs_4_) | copy-start | bytes 393220
  126.5 24.7 %collective-permute-start.5 = (f32[1,256,128]{2,1,0:T(8,128)S(1)}, f32[1,256,128]{2,1,0:T(8,128)S(1)}, u32[]{:S(2)}, u32[]{:S(2)}) collective-permute-start(f32[1,256,128]{2,1,0:T(8,128)S(1)} %bitcast.30), channel_id=1, source_target_pairs={{0,13},{1,12},{2,15},{3,14},{4,9},{5,8},{6,11},{7,10},{8,5},{9,4},... | collective-permute-start | bytes 393224 | tf_op jit(solution)/shard_map/ppermute | solution.py:517
  135.3 15.8 %copy-start.5 = (f32[1,256,128]{2,1,0:T(8,128)}, f32[1,256,128]{2,1,0:T(8,128)S(1)}, u32[]{:S(2)}) copy-start(f32[1,256,128]{2,1,0:T(8,128)S(1)} %collective-permute-done.3.refs_5_) | copy-start | bytes 393220
  135.3 15.9 %collective-permute-start.6 = (f32[1,256,128]{2,1,0:T(8,128)S(1)}, f32[1,256,128]{2,1,0:T(8,128)S(1)}, u32[]{:S(2)}, u32[]{:S(2)}) collective-permute-start(f32[1,256,128]{2,1,0:T(8,128)S(1)} %bitcast.29), channel_id=1, source_target_pairs={{0,14},{1,15},{2,12},{3,13},{4,10},{5,11},{6,8},{7,9},{8,6},{9,7},... | collective-permute-start | bytes 393224 | tf_op jit(solution)/shard_map/ppermute | solution.py:517
  139.4 11.7 %copy-start.6 = (f32[1,256,128]{2,1,0:T(8,128)}, f32[1,256,128]{2,1,0:T(8,128)S(1)}, u32[]{:S(2)}) copy-start(f32[1,256,128]{2,1,0:T(8,128)S(1)} %collective-permute-done.4.refs_6_) | copy-start | bytes 393220
  139.4 14.1 %collective-permute-start.7 = (f32[1,256,128]{2,1,0:T(8,128)S(1)}, f32[1,256,128]{2,1,0:T(8,128)S(1)}, u32[]{:S(2)}, u32[]{:S(2)}) collective-permute-start(f32[1,256,128]{2,1,0:T(8,128)S(1)} %bitcast.28), channel_id=1, source_target_pairs={{0,15},{1,14},{2,13},{3,12},{4,11},{5,10},{6,9},{7,8},{8,7},{9,6},... | collective-permute-start | bytes 393224 | tf_op jit(solution)/shard_map/ppermute | solution.py:517
  (4 other events, 12.0 us)

commit v11 on v10

--- a/solution.py
+++ b/solution.py
@@ -506,19 +506,20 @@
     return lax.all_to_all(block, "feed", split_axis=0, concat_axis=0, tiled=True)
 
 
-def exchange_halves(near, far, flight):
-    devices = 2 * near.shape[0]
-    half = near.shape[0]
-    groups = [list(range(half)), list(range(half, devices))]
-    arrived = []
-    for k, block in enumerate(far):
+def exchange_pairs(far, flight):
+    devices = len(far) + 1
+    half = devices // 2
+    order = []
+    for k in range(half):
+        order += [half + k] + ([k] if k else [])
+    arrived = [None] * len(far)
+    for k, d in enumerate(order):
+        block = far[d - 1]
         if k >= flight:
-            block, arrived[k - flight] = lax.optimization_barrier((block, arrived[k - flight]))
-        arrived.append(lax.ppermute(block, "feed", [(i, i ^ (half + k)) for i in range(devices)]))
-    close = lax.all_to_all(
-        near, "feed", split_axis=0, concat_axis=0, axis_index_groups=groups, tiled=True
-    )
-    return close, arrived
+            e = order[k - flight] - 1
+            block, arrived[e] = lax.optimization_barrier((block, arrived[e]))
+        arrived[d - 1] = lax.ppermute(block, "feed", [(i, i ^ d) for i in range(devices)])
+    return arrived
 
 
 def channel_tables(owners, dropped_channels):
@@ -543,13 +544,9 @@
         fir_taps=fir_taps,
         samples=jnp.transpose(samples, (1, 0, 2)),
     )
-    half = devices // 2
     middle = capacity * 2 // 3
     me = lax.axis_index("feed")
     widths = [2 * n * in_local // LANES for n in (FIRST, SPEC - FIRST)]
-
-    def place(device):
-        return jnp.where(device // half == me // half, device % half, half + (device ^ me) % half)
 
     rows = widths[0] // 8
     block_a, power = call(
@@ -564,21 +561,19 @@
     head, tail = middle * rows, (capacity - middle) * rows + 1
     row_of = jnp.where(
         ranks < middle,
-        devices * tail + place(owners) * head + ranks * rows,
+        devices * tail + (owners ^ me) * head + ranks * rows,
         owners * tail + (ranks - middle) * rows,
     )
-    block_c, near, *far = call(
+    block_c, own, *far = call(
         FIRST,
         SPEC - FIRST,
-        [(devices, 8 * tail), (half, 8 * head)] + [(1, 8 * head)] * half,
+        [(devices, 8 * tail)] + [(1, 8 * head)] * devices,
         jnp.where(dead, -1, row_of),
         power,
     )
     block_c, received_a = lax.optimization_barrier((block_c, received_a))
     received_c = exchange(block_c)
-    near, received_c = lax.optimization_barrier((near, received_c))
-    close, arrived = exchange_halves(near, far, 3)
-    received_b = [close] + arrived
+    received_b = [own] + exchange_pairs(far, 4)
 
     kept = jnp.sum(jnp.logical_not(dead).astype(jnp.float32))
     mine = (owners == lax.axis_index("feed")) & jnp.logical_not(dead)
@@ -604,7 +599,7 @@
         begin=0,
         low=0,
         high=middle,
-        index=place(everyone).astype(jnp.int32),
+        index=everyone ^ me,
         before=vis,
     )
 

time: 171 us -> 166 us (0.971)
  the two profiles are of different devices: /device:TPU:13 before, /device:TPU:0 now
where the time goes in v11:
time: 166 us; the launch traced here: 165 us
  Pallas kernels  76.5 us (46%)
  waiting for transfers between devices  47.4 us (29%)
  starting transfers between devices  32.4 us (20%)
  other arithmetic  6.12 us (4%)
  between operations  1.76 us (1%)
    pallas_call x2, Pallas kernels, spectra_call(): pl.pallas_call(functools.partial(spectra_kernel, count, last, devices, me...  52.7 us
    ppermute x15, waiting for transfers between devices, exchange_pairs(): lax.ppermute(block, 'feed', [(i, i ^ d) for i in range(devices)])  47.4 us
    pallas_call x2, Pallas kernels, correlate_call(): pl.pallas_call(functools.partial(correlate_kernel, widths, low, count, le...  23.8 us
    ppermute x15, starting transfers between devices, exchange_pairs(): lax.ppermute(block, 'feed', [(i, i ^ d) for i in range(devices)])  17.5 us
    all_to_all x2, starting transfers between devices, exchange(): lax.all_to_all(block, 'feed', split_axis=0, concat_axis=0, tiled=True)  14.9 us
  transfers between devices with their start and end apart: 17, of which 6 were waited for; matrix products, arithmetic and copies ran while one was open for 2% of the time, Pallas kernels for 25%

profile of v11, /device:TPU:0, one launch (start us, length us, event | category | flops | bytes accessed | tf_op | source)
XLA Modules:
  0.0 165.4 jit_solution(7312584917457387637)
XLA Ops:
  0.0 0.7 pad_add_fusion
  0.7 0.8 select_reduce_fusion
  1.5 0.7 compare_and_fusion
  2.2 1.3 add_select_fusion
  3.5 19.7 %spectra.2 = (f32[3072,128]{1,0:T(8,128)}, f32[8,128]{1,0:T(8,128)}) custom-call(s32[256]{0:T(256)} %get-tuple-element.93.refs_0_, f32[4,8192]{1,0:T(4,128)} %refs_2_.3, f32[4,8192]{1,0:T(4,128)} %refs_2_.3, bf16[51,32,8192]{2,1,0:T(8,128)(2,1)} %bitcast.22, bf16[51,32,8192]{2,1,0:T(8,128)(2,1)} %bitcast.23, ...), custom_call_target="tpu_custom_call" | custom-call | flops 6442450944 | bytes 31457280 | tf_op jit(solution)/shard_map/spectra/pallas_call | solution.py:307
  23.2 7.4 %all-to-all-start = ((f32[16,192,128]{2,1,0:T(8,128)}), f32[16,192,128]{2,1,0:T(8,128)S(1)}, u32[]{:S(2)}, u32[]{:S(2)}) async-start(f32[16,192,128]{2,1,0:T(8,128)} %bitcast.26), calls=%async_computation | async-start | bytes 3145728 | tf_op jit(solution)/shard_map/all_to_all | solution.py:506
  31.2 33.0 %spectra.3 = (f32[2176,128]{1,0:T(8,128)}, f32[256,128]{1,0:T(8,128)}, f32[256,128]{1,0:T(8,128)}, f32[256,128]{1,0:T(8,128)}, f32[256,128]{1,0:T(8,128)}, /*ind...) custom-call(s32[256]{0:T(256)} %fusion.5.refs_0_, ...), custom_call_target="tpu_custom_call" | custom-call | flops 12884901888 | bytes 31457280 | tf_op jit(solution)/shard_map/spectra/pallas_call | solution.py:307
  64.3 7.4 %all-to-all-start.1 = ((f32[16,136,128]{2,1,0:T(8,128)}), f32[16,136,128]{2,1,0:T(8,128)S(1)}, u32[]{:S(2)}, u32[]{:S(2)}) async-start(f32[16,136,128]{2,1,0:T(8,128)} %bitcast.27), calls=%async_computation.1 | async-start | bytes 2228224 | tf_op jit(solution)/shard_map/all_to_all | solution.py:506
  72.2 2.6 %collective-permute-start.1 = (f32[1,256,128]{2,1,0:T(8,128)S(1)}, f32[1,256,128]{2,1,0:T(8,128)S(1)}, u32[]{:S(2)}, u32[]{:S(2)}) collective-permute-start(f32[1,256,128]{2,1,0:T(8,128)S(1)} %bitcast.45), channel_id=1, source_target_pairs={{0,8},{1,9},{2,10},{3,11},{4,12},{5,13},{6,14},{7,15},{8,0},{9,1},... | collective-permute-start | bytes 393224 | tf_op jit(solution)/shard_map/ppermute | solution.py:521
  74.8 3.5 %collective-permute-start.9 = (f32[1,256,128]{2,1,0:T(8,128)}, f32[1,256,128]{2,1,0:T(8,128)S(1)}, u32[]{:S(2)}, u32[]{:S(2)}) collective-permute-start(f32[1,256,128]{2,1,0:T(8,128)} %bitcast.17), channel_id=1, source_target_pairs={{0,10},{1,11},{2,8},{3,9},{4,14},{5,15},{6,12},{7,13},{8,2},{9,3},... | collective-permute-start | bytes 393224 | tf_op jit(solution)/shard_map/ppermute | solution.py:521
  78.6 32.8 %collective-permute-done.1.refs_9_ = f32[1,256,128]{2,1,0:T(8,128)S(1)} collective-permute-done((f32[1,256,128]{2,1,0:T(8,128)S(1)}, f32[1,256,128]{2,1,0:T(8,128)S(1)}, u32[]{:S(2)}, u32[]{:S(2)}) %collective-permute-start.1) | collective-permute-done | bytes 131104 | tf_op jit(solution)/shard_map/ppermute | solution.py:521
  111.4 1.5 collective-permute-start.2
  113.7 6.6 %collective-permute-done.9.refs_11_ = f32[1,256,128]{2,1,0:T(8,128)S(1)} collective-permute-done((f32[1,256,128]{2,1,0:T(8,128)}, f32[1,256,128]{2,1,0:T(8,128)S(1)}, u32[]{:S(2)}, u32[]{:S(2)}) %collective-permute-start.9) | collective-permute-done | bytes 131104 | tf_op jit(solution)/shard_map/ppermute | solution.py:521
  120.5 5.6 %collective-permute-done.10.refs_12_ = f32[1,256,128]{2,1,0:T(8,128)} collective-permute-done((f32[1,256,128]{2,1,0:T(8,128)}, f32[1,256,128]{2,1,0:T(8,128)}, u32[]{:S(2)}, u32[]{:S(2)}) %collective-permute-start.10) | collective-permute-done | bytes 131104 | tf_op jit(solution)/shard_map/ppermute | solution.py:521
  126.1 1.8 %collective-permute-start.12 = (f32[1,256,128]{2,1,0:T(8,128)}, f32[1,256,128]{2,1,0:T(8,128)}, u32[]{:S(2)}, u32[]{:S(2)}) collective-permute-start(f32[1,256,128]{2,1,0:T(8,128)} %bitcast.39), channel_id=1, source_target_pairs={{0,13},{1,12},{2,15},{3,14},{4,9},{5,8},{6,11},{7,10},{8,5},{9,4},... | collective-permute-start | bytes 393224 | tf_op jit(solution)/shard_map/ppermute | solution.py:521
  127.9 0.6 fusion.4
  128.5 0.6 slice.11.used_ref
  130.4 0.6 collective-permute-start.13
  131.0 3.0 %collective-permute-start.6 = (f32[1,256,128]{2,1,0:T(8,128)}, f32[1,256,128]{2,1,0:T(8,128)}, u32[]{:S(2)}, u32[]{:S(2)}) collective-permute-start(f32[1,256,128]{2,1,0:T(8,128)} %bitcast.36), channel_id=1, source_target_pairs={{0,6},{1,7},{2,4},{3,5},{4,2},{5,3},{6,0},{7,1},{8,14},{9,15},{10,... | collective-permute-start | bytes 393224 | tf_op jit(solution)/shard_map/ppermute | solution.py:521
  134.2 3.3 %collective-permute-start.14 = (f32[1,256,128]{2,1,0:T(8,128)}, f32[1,256,128]{2,1,0:T(8,128)}, u32[]{:S(2)}, u32[]{:S(2)}) collective-permute-start(f32[1,256,128]{2,1,0:T(8,128)} %bitcast.35), channel_id=1, source_target_pairs={{0,15},{1,14},{2,13},{3,12},{4,11},{5,10},{6,9},{7,8},{8,7},{9,6},... | collective-permute-start | bytes 393224 | tf_op jit(solution)/shard_map/ppermute | solution.py:521
  137.5 0.7 slice_reduce_fusion
  139.5 8.8 %correlate.2.refs_17_ = bf16[24,2,512,512]{3,2,1,0:T(8,128)(2,1)} custom-call(f32[1]{0:T(128)} %bitcast.4.factor_ref, s32[8]{0:T(128)} %slice.11.used_ref, s32[16]{0:T(128)} %iota.22.index_ref, f32[16,192,128]{2,1,0:T(8,128)} %copy-done, f32[16,136,128]{2,1,0:T(8,128)} %copy-done.1), custom_call_target="tpu_custom_call" | custom-call | flops 4294967296 | bytes 9961472 | tf_op jit(solution)/shard_map/correlate/pallas_call | solution.py:478
  148.4 1.9 %collective-permute-done.14.refs_16_ = f32[1,256,128]{2,1,0:T(8,128)} collective-permute-done((f32[1,256,128]{2,1,0:T(8,128)}, f32[1,256,128]{2,1,0:T(8,128)}, u32[]{:S(2)}, u32[]{:S(2)}) %collective-permute-start.14) | collective-permute-done | bytes 131104 | tf_op jit(solution)/shard_map/ppermute | solution.py:521
  150.3 15.0 %correlate.3 = bf16[24,2,512,512]{3,2,1,0:T(8,128)(2,1)} custom-call(f32[1]{0:T(128)} %bitcast.4.factor_ref, s32[16]{0:T(128)} %bitcast.34, s32[16]{0:T(128)} %iota_xor_fusion.index_ref, f32[16,192,128]{2,1,0:T(8,128)} %copy-done, f32[1,256,128]{2,1,0:T(8,128)} %bitcast.28, f32[1,256,128]{2,1,0:T(8,128)} %copy-done.2, ...), custom_call_target="tpu_custom_call", output_to_operand_aliasing={{}: (20, {})} | custom-call | flops 8589934592 | bytes 19922944 | tf_op jit(solution)/shard_map/correlate/pallas_call | solution.py:478
  (51 shorter events, 3.8 us)
Async XLA Ops:
  23.2 41.1 %all-to-all-start = ((f32[16,192,128]{2,1,0:T(8,128)}), f32[16,192,128]{2,1,0:T(8,128)S(1)}, u32[]{:S(2)}, u32[]{:S(2)}) async-start(f32[16,192,128]{2,1,0:T(8,128)} %bitcast.26), calls=%async_computation | async-start | bytes 3145728 | tf_op jit(solution)/shard_map/all_to_all | solution.py:506
  64.3 75.2 %copy-start = (f32[16,192,128]{2,1,0:T(8,128)}, f32[16,192,128]{2,1,0:T(8,128)S(1)}, u32[]{:S(2)}) copy-start(f32[16,192,128]{2,1,0:T(8,128)S(1)} %all-to-all-done.refs_0_) | copy-start | bytes 4718596
  64.3 73.2 %all-to-all-start.1 = ((f32[16,136,128]{2,1,0:T(8,128)}), f32[16,136,128]{2,1,0:T(8,128)S(1)}, u32[]{:S(2)}, u32[]{:S(2)}) async-start(f32[16,136,128]{2,1,0:T(8,128)} %bitcast.27), calls=%async_computation.1 | async-start | bytes 2228224 | tf_op jit(solution)/shard_map/all_to_all | solution.py:506
  71.7 6.5 %collective-permute-start = (f32[1,256,128]{2,1,0:T(8,128)S(1)}, f32[1,256,128]{2,1,0:T(8,128)S(1)}, u32[]{:S(2)}, u32[]{:S(2)}) collective-permute-start(f32[1,256,128]{2,1,0:T(8,128)S(1)} %bitcast.46), channel_id=1, source_target_pairs={{0,1},{1,0},{2,3},{3,2},{4,5},{5,4},{6,7},{7,6},{8,9},{9,8},{10,11... | collective-permute-start | bytes 393224 | tf_op jit(solution)/shard_map/ppermute | solution.py:521
  72.2 39.2 %collective-permute-start.1 = (f32[1,256,128]{2,1,0:T(8,128)S(1)}, f32[1,256,128]{2,1,0:T(8,128)S(1)}, u32[]{:S(2)}, u32[]{:S(2)}) collective-permute-start(f32[1,256,128]{2,1,0:T(8,128)S(1)} %bitcast.45), channel_id=1, source_target_pairs={{0,8},{1,9},{2,10},{3,11},{4,12},{5,13},{6,14},{7,15},{8,0},{9,1},... | collective-permute-start | bytes 393224 | tf_op jit(solution)/shard_map/ppermute | solution.py:521
  74.8 38.5 %collective-permute-start.8 = (f32[1,256,128]{2,1,0:T(8,128)}, f32[1,256,128]{2,1,0:T(8,128)S(1)}, u32[]{:S(2)}, u32[]{:S(2)}) collective-permute-start(f32[1,256,128]{2,1,0:T(8,128)} %bitcast.15), channel_id=1, source_target_pairs={{0,9},{1,8},{2,11},{3,10},{4,13},{5,12},{6,15},{7,14},{8,1},{9,0},... | collective-permute-start | bytes 393224 | tf_op jit(solution)/shard_map/ppermute | solution.py:521
  74.8 45.5 %collective-permute-start.9 = (f32[1,256,128]{2,1,0:T(8,128)}, f32[1,256,128]{2,1,0:T(8,128)S(1)}, u32[]{:S(2)}, u32[]{:S(2)}) collective-permute-start(f32[1,256,128]{2,1,0:T(8,128)} %bitcast.17), channel_id=1, source_target_pairs={{0,10},{1,11},{2,8},{3,9},{4,14},{5,15},{6,12},{7,13},{8,2},{9,3},... | collective-permute-start | bytes 393224 | tf_op jit(solution)/shard_map/ppermute | solution.py:521
  78.3 70.0 %copy-start.2 = (f32[1,256,128]{2,1,0:T(8,128)}, f32[1,256,128]{2,1,0:T(8,128)S(1)}, u32[]{:S(2)}) copy-start(f32[1,256,128]{2,1,0:T(8,128)S(1)} %collective-permute-done.refs_2_) | copy-start | bytes 393220
  78.3 42.0 %collective-permute-start.3 = (f32[1,256,128]{2,1,0:T(8,128)}, f32[1,256,128]{2,1,0:T(8,128)S(1)}, u32[]{:S(2)}, u32[]{:S(2)}) collective-permute-start(f32[1,256,128]{2,1,0:T(8,128)} %bitcast.6), channel_id=1, source_target_pairs={{0,3},{1,2},{2,1},{3,0},{4,7},{5,6},{6,5},{7,4},{8,11},{9,10},{10,... | collective-permute-start | bytes 393224 | tf_op jit(solution)/shard_map/ppermute | solution.py:521
  111.4 36.9 %copy-start.3 = (f32[1,256,128]{2,1,0:T(8,128)}, f32[1,256,128]{2,1,0:T(8,128)S(1)}, u32[]{:S(2)}) copy-start(f32[1,256,128]{2,1,0:T(8,128)S(1)} %collective-permute-done.1.refs_9_) | copy-start | bytes 393220
  111.4 9.0 %collective-permute-start.2 = (f32[1,256,128]{2,1,0:T(8,128)}, f32[1,256,128]{2,1,0:T(8,128)S(1)}, u32[]{:S(2)}, u32[]{:S(2)}) collective-permute-start(f32[1,256,128]{2,1,0:T(8,128)} %bitcast.44), channel_id=1, source_target_pairs={{0,2},{1,3},{2,0},{3,1},{4,6},{5,7},{6,4},{7,5},{8,10},{9,11},{10,... | collective-permute-start | bytes 393224 | tf_op jit(solution)/shard_map/ppermute | solution.py:521
  113.3 35.0 %copy-start.4 = (f32[1,256,128]{2,1,0:T(8,128)}, f32[1,256,128]{2,1,0:T(8,128)S(1)}, u32[]{:S(2)}) copy-start(f32[1,256,128]{2,1,0:T(8,128)S(1)} %collective-permute-done.8.refs_10_) | copy-start | bytes 393220
  113.3 12.8 %collective-permute-start.10 = (f32[1,256,128]{2,1,0:T(8,128)}, f32[1,256,128]{2,1,0:T(8,128)}, u32[]{:S(2)}, u32[]{:S(2)}) collective-permute-start(f32[1,256,128]{2,1,0:T(8,128)} %bitcast.43), channel_id=1, source_target_pairs={{0,11},{1,10},{2,9},{3,8},{4,15},{5,14},{6,13},{7,12},{8,3},{9,2},... | collective-permute-start | bytes 393224 | tf_op jit(solution)/shard_map/ppermute | solution.py:521
  120.3 28.0 %copy-start.5 = (f32[1,256,128]{2,1,0:T(8,128)}, f32[1,256,128]{2,1,0:T(8,128)S(1)}, u32[]{:S(2)}) copy-start(f32[1,256,128]{2,1,0:T(8,128)S(1)} %collective-permute-done.9.refs_11_) | copy-start | bytes 393220
  120.3 10.0 %collective-permute-start.11 = (f32[1,256,128]{2,1,0:T(8,128)}, f32[1,256,128]{2,1,0:T(8,128)}, u32[]{:S(2)}, u32[]{:S(2)}) collective-permute-start(f32[1,256,128]{2,1,0:T(8,128)} %bitcast.42), channel_id=1, source_target_pairs={{0,12},{1,13},{2,14},{3,15},{4,8},{5,9},{6,10},{7,11},{8,4},{9,5},... | collective-permute-start | bytes 393224 | tf_op jit(solution)/shard_map/ppermute | solution.py:521
  120.3 28.0 %copy-start.6 = (f32[1,256,128]{2,1,0:T(8,128)}, f32[1,256,128]{2,1,0:T(8,128)S(1)}, u32[]{:S(2)}) copy-start(f32[1,256,128]{2,1,0:T(8,128)S(1)} %collective-permute-done.3.refs_4_) | copy-start | bytes 393220
  120.3 10.6 %collective-permute-start.5 = (f32[1,256,128]{2,1,0:T(8,128)}, f32[1,256,128]{2,1,0:T(8,128)}, u32[]{:S(2)}, u32[]{:S(2)}) collective-permute-start(f32[1,256,128]{2,1,0:T(8,128)} %bitcast.41), channel_id=1, source_target_pairs={{0,5},{1,4},{2,7},{3,6},{4,1},{5,0},{6,3},{7,2},{8,13},{9,12},{10,... | collective-permute-start | bytes 393224 | tf_op jit(solution)/shard_map/ppermute | solution.py:521
  120.4 27.9 %copy-start.7 = (f32[1,256,128]{2,1,0:T(8,128)}, f32[1,256,128]{2,1,0:T(8,128)S(1)}, u32[]{:S(2)}) copy-start(f32[1,256,128]{2,1,0:T(8,128)S(1)} %collective-permute-done.2.refs_3_) | copy-start | bytes 393220
  120.4 10.5 %collective-permute-start.4 = (f32[1,256,128]{2,1,0:T(8,128)}, f32[1,256,128]{2,1,0:T(8,128)}, u32[]{:S(2)}, u32[]{:S(2)}) collective-permute-start(f32[1,256,128]{2,1,0:T(8,128)} %bitcast.40), channel_id=1, source_target_pairs={{0,4},{1,5},{2,6},{3,7},{4,0},{5,1},{6,2},{7,3},{8,12},{9,13},{10,... | collective-permute-start | bytes 393224 | tf_op jit(solution)/shard_map/ppermute | solution.py:521
  126.1 8.1 %collective-permute-start.12 = (f32[1,256,128]{2,1,0:T(8,128)}, f32[1,256,128]{2,1,0:T(8,128)}, u32[]{:S(2)}, u32[]{:S(2)}) collective-permute-start(f32[1,256,128]{2,1,0:T(8,128)} %bitcast.39), channel_id=1, source_target_pairs={{0,13},{1,12},{2,15},{3,14},{4,9},{5,8},{6,11},{7,10},{8,5},{9,4},... | collective-permute-start | bytes 393224 | tf_op jit(solution)/shard_map/ppermute | solution.py:521
  130.4 18.0 %collective-permute-start.13 = (f32[1,256,128]{2,1,0:T(8,128)}, f32[1,256,128]{2,1,0:T(8,128)}, u32[]{:S(2)}, u32[]{:S(2)}) collective-permute-start(f32[1,256,128]{2,1,0:T(8,128)} %bitcast.38), channel_id=1, source_target_pairs={{0,14},{1,15},{2,12},{3,13},{4,10},{5,11},{6,8},{7,9},{8,6},{9,7},... | collective-permute-start | bytes 393224 | tf_op jit(solution)/shard_map/ppermute | solution.py:521
  131.0 17.4 %collective-permute-start.7 = (f32[1,256,128]{2,1,0:T(8,128)}, f32[1,256,128]{2,1,0:T(8,128)}, u32[]{:S(2)}, u32[]{:S(2)}) collective-permute-start(f32[1,256,128]{2,1,0:T(8,128)} %bitcast.37), channel_id=1, source_target_pairs={{0,7},{1,6},{2,5},{3,4},{4,3},{5,2},{6,1},{7,0},{8,15},{9,14},{10,... | collective-permute-start | bytes 393224 | tf_op jit(solution)/shard_map/ppermute | solution.py:521
  131.0 17.4 %collective-permute-start.6 = (f32[1,256,128]{2,1,0:T(8,128)}, f32[1,256,128]{2,1,0:T(8,128)}, u32[]{:S(2)}, u32[]{:S(2)}) collective-permute-start(f32[1,256,128]{2,1,0:T(8,128)} %bitcast.36), channel_id=1, source_target_pairs={{0,6},{1,7},{2,4},{3,5},{4,2},{5,3},{6,0},{7,1},{8,14},{9,15},{10,... | collective-permute-start | bytes 393224 | tf_op jit(solution)/shard_map/ppermute | solution.py:521
  134.2 16.1 %collective-permute-start.14 = (f32[1,256,128]{2,1,0:T(8,128)}, f32[1,256,128]{2,1,0:T(8,128)}, u32[]{:S(2)}, u32[]{:S(2)}) collective-permute-start(f32[1,256,128]{2,1,0:T(8,128)} %bitcast.35), channel_id=1, source_target_pairs={{0,15},{1,14},{2,13},{3,12},{4,11},{5,10},{6,9},{7,8},{8,7},{9,6},... | collective-permute-start | bytes 393224 | tf_op jit(solution)/shard_map/ppermute | solution.py:521
  (5 other events, 44.8 us)

commit v12 on v11

--- a/solution.py
+++ b/solution.py
@@ -506,7 +506,7 @@
     return lax.all_to_all(block, "feed", split_axis=0, concat_axis=0, tiled=True)
 
 
-def exchange_pairs(far, flight):
+def exchange_pairs(far, flight, ahead):
     devices = len(far) + 1
     half = devices // 2
     order = []
@@ -518,8 +518,10 @@
         if k >= flight:
             e = order[k - flight] - 1
             block, arrived[e] = lax.optimization_barrier((block, arrived[e]))
+        if d == order[-1]:
+            block, ahead = lax.optimization_barrier((block, ahead))
         arrived[d - 1] = lax.ppermute(block, "feed", [(i, i ^ d) for i in range(devices)])
-    return arrived
+    return arrived, ahead
 
 
 def channel_tables(owners, dropped_channels):
@@ -573,8 +575,6 @@
     )
     block_c, received_a = lax.optimization_barrier((block_c, received_a))
     received_c = exchange(block_c)
-    received_b = [own] + exchange_pairs(far, 4)
-
     kept = jnp.sum(jnp.logical_not(dead).astype(jnp.float32))
     mine = (owners == lax.axis_index("feed")) & jnp.logical_not(dead)
     slots = jnp.arange(capacity, dtype=jnp.int32)
@@ -593,9 +593,10 @@
     vis = run(
         received_a, [received_c], begin=middle, low=middle, high=capacity, index=everyone, before=None
     )
+    arrived, vis = exchange_pairs(far, 4, vis)
     return run(
         received_a,
-        received_b,
+        [own] + arrived,
         begin=0,
         low=0,
         high=middle,

time: 166 us -> 170 us (1.024)
  the two profiles are of different devices: /device:TPU:0 before, /device:TPU:13 now
where the time goes in v12:
time: 170 us; the launch traced here: 168 us
  Pallas kernels  76.5 us (45%)
  waiting for transfers between devices  49.2 us (29%)
  starting transfers between devices  33.1 us (19%)
  other arithmetic  6.03 us (4%)
  local copies, waits for them, and re-layouts  1.8 us (1%)
    pallas_call x2, Pallas kernels, spectra_call(): pl.pallas_call(functools.partial(spectra_kernel, count, last, devices, me...  52.6 us
    ppermute x15, waiting for transfers between devices, exchange_pairs(): lax.ppermute(block, 'feed', [(i, i ^ d) for i in range(devices)])  46.7 us
    pallas_call x2, Pallas kernels, correlate_call(): pl.pallas_call(functools.partial(correlate_kernel, widths, low, count, le...  23.8 us
    ppermute x15, starting transfers between devices, exchange_pairs(): lax.ppermute(block, 'feed', [(i, i ^ d) for i in range(devices)])  21.7 us
    all_to_all x2, starting transfers between devices, exchange(): lax.all_to_all(block, 'feed', split_axis=0, concat_axis=0, tiled=True)  11.5 us
  transfers between devices with their start and end apart: 17, of which 8 were waited for; matrix products, arithmetic and copies ran while one was open for 2% of the time, Pallas kernels for 25%

profile of v12, /device:TPU:13, one launch (start us, length us, event | category | flops | bytes accessed | tf_op | source)
XLA Modules:
  0.0 168.4 jit_solution(8187981349195446499)
XLA Ops:
  2.2 1.3 add_select_fusion
  3.5 19.7 %spectra.2 = (f32[3072,128]{1,0:T(8,128)}, f32[8,128]{1,0:T(8,128)}) custom-call(s32[256]{0:T(256)} %get-tuple-element.97.refs_0_, f32[4,8192]{1,0:T(4,128)} %refs_2_.3, f32[4,8192]{1,0:T(4,128)} %refs_2_.3, bf16[51,32,8192]{2,1,0:T(8,128)(2,1)} %bitcast.22, bf16[51,32,8192]{2,1,0:T(8,128)(2,1)} %bitcast.23, ...), custom_call_target="tpu_custom_call" | custom-call | flops 6442450944 | bytes 31457280 | tf_op jit(solution)/shard_map/spectra/pallas_call | solution.py:307
  23.2 6.6 %all-to-all-start = ((f32[16,192,128]{2,1,0:T(8,128)}), f32[16,192,128]{2,1,0:T(8,128)S(1)}, u32[]{:S(2)}, u32[]{:S(2)}) async-start(f32[16,192,128]{2,1,0:T(8,128)} %bitcast.26), calls=%async_computation | async-start | bytes 3145728 | tf_op jit(solution)/shard_map/all_to_all | solution.py:506
  30.4 33.0 %spectra.3 = (f32[2176,128]{1,0:T(8,128)}, f32[256,128]{1,0:T(8,128)}, f32[256,128]{1,0:T(8,128)}, f32[256,128]{1,0:T(8,128)}, f32[256,128]{1,0:T(8,128)}, /*ind...) custom-call(s32[256]{0:T(256)} %fusion.5.refs_0_, ...), custom_call_target="tpu_custom_call" | custom-call | flops 12884901888 | bytes 31457280 | tf_op jit(solution)/shard_map/spectra/pallas_call | solution.py:307
  63.4 2.6 %all-to-all-done.refs_0_ = f32[16,192,128]{2,1,0:T(8,128)S(1)} async-done(((f32[16,192,128]{2,1,0:T(8,128)}), f32[16,192,128]{2,1,0:T(8,128)S(1)}, u32[]{:S(2)}, u32[]{:S(2)}) %all-to-all-start) | async-done | bytes 1572896 | tf_op jit(solution)/shard_map/all_to_all | solution.py:506
  66.0 4.9 %all-to-all-start.1 = ((f32[16,136,128]{2,1,0:T(8,128)}), f32[16,136,128]{2,1,0:T(8,128)S(1)}, u32[]{:S(2)}, u32[]{:S(2)}) async-start(f32[16,136,128]{2,1,0:T(8,128)} %bitcast.27), calls=%async_computation.1 | async-start | bytes 2228224 | tf_op jit(solution)/shard_map/all_to_all | solution.py:506
  71.3 2.1 %collective-permute-start.1 = (f32[1,256,128]{2,1,0:T(8,128)S(1)}, f32[1,256,128]{2,1,0:T(8,128)S(1)}, u32[]{:S(2)}, u32[]{:S(2)}) collective-permute-start(f32[1,256,128]{2,1,0:T(8,128)S(1)} %bitcast.45), channel_id=1, source_target_pairs={{0,8},{1,9},{2,10},{3,11},{4,12},{5,13},{6,14},{7,15},{8,0},{9,1},... | collective-permute-start | bytes 393224 | tf_op jit(solution)/shard_map/ppermute | solution.py:523
  74.0 2.1 %collective-permute-start.9 = (f32[1,256,128]{2,1,0:T(8,128)}, f32[1,256,128]{2,1,0:T(8,128)S(1)}, u32[]{:S(2)}, u32[]{:S(2)}) collective-permute-start(f32[1,256,128]{2,1,0:T(8,128)} %bitcast.17), channel_id=1, source_target_pairs={{0,10},{1,11},{2,8},{3,9},{4,14},{5,15},{6,12},{7,13},{8,2},{9,3},... | collective-permute-start | bytes 393224 | tf_op jit(solution)/shard_map/ppermute | solution.py:523
  76.1 1.4 collective-permute-start.3
  77.5 28.8 %collective-permute-done.1.refs_9_ = f32[1,256,128]{2,1,0:T(8,128)S(1)} collective-permute-done((f32[1,256,128]{2,1,0:T(8,128)S(1)}, f32[1,256,128]{2,1,0:T(8,128)S(1)}, u32[]{:S(2)}, u32[]{:S(2)}) %collective-permute-start.1) | collective-permute-done | bytes 131104 | tf_op jit(solution)/shard_map/ppermute | solution.py:523
  106.5 2.6 %collective-permute-done.8.refs_10_ = f32[1,256,128]{2,1,0:T(8,128)S(1)} collective-permute-done((f32[1,256,128]{2,1,0:T(8,128)}, f32[1,256,128]{2,1,0:T(8,128)S(1)}, u32[]{:S(2)}, u32[]{:S(2)}) %collective-permute-start.8) | collective-permute-done | bytes 131104 | tf_op jit(solution)/shard_map/ppermute | solution.py:523
  109.2 3.3 %collective-permute-start.10 = (f32[1,256,128]{2,1,0:T(8,128)}, f32[1,256,128]{2,1,0:T(8,128)}, u32[]{:S(2)}, u32[]{:S(2)}) collective-permute-start(f32[1,256,128]{2,1,0:T(8,128)} %bitcast.43), channel_id=1, source_target_pairs={{0,11},{1,10},{2,9},{3,8},{4,15},{5,14},{6,13},{7,12},{8,3},{9,2},... | collective-permute-start | bytes 393224 | tf_op jit(solution)/shard_map/ppermute | solution.py:523
  112.5 1.2 collective-permute-start.11
  113.7 3.6 %collective-permute-start.5 = (f32[1,256,128]{2,1,0:T(8,128)}, f32[1,256,128]{2,1,0:T(8,128)}, u32[]{:S(2)}, u32[]{:S(2)}) collective-permute-start(f32[1,256,128]{2,1,0:T(8,128)} %bitcast.41), channel_id=1, source_target_pairs={{0,5},{1,4},{2,7},{3,6},{4,1},{5,0},{6,3},{7,2},{8,13},{9,12},{10,... | collective-permute-start | bytes 393224 | tf_op jit(solution)/shard_map/ppermute | solution.py:523
  117.5 3.9 %collective-permute-done.10.refs_12_ = f32[1,256,128]{2,1,0:T(8,128)} collective-permute-done((f32[1,256,128]{2,1,0:T(8,128)}, f32[1,256,128]{2,1,0:T(8,128)}, u32[]{:S(2)}, u32[]{:S(2)}) %collective-permute-start.10) | collective-permute-done | bytes 131104 | tf_op jit(solution)/shard_map/ppermute | solution.py:523
  121.4 0.9 collective-permute-start.12
  124.3 1.4 collective-permute-done.11.refs_13_
  125.7 1.3 collective-permute-start.13
  127.0 3.3 %collective-permute-done.4.refs_5_ = f32[1,256,128]{2,1,0:T(8,128)} collective-permute-done((f32[1,256,128]{2,1,0:T(8,128)}, f32[1,256,128]{2,1,0:T(8,128)}, u32[]{:S(2)}, u32[]{:S(2)}) %collective-permute-start.4) | collective-permute-done | bytes 131104 | tf_op jit(solution)/shard_map/ppermute | solution.py:523
  130.4 1.0 collective-permute-done.12.refs_14_
  131.4 3.6 %collective-permute-start.14 = (f32[1,256,128]{2,1,0:T(8,128)}, f32[1,256,128]{2,1,0:T(8,128)}, u32[]{:S(2)}, u32[]{:S(2)}) collective-permute-start(f32[1,256,128]{2,1,0:T(8,128)} %bitcast.36), channel_id=1, source_target_pairs={{0,15},{1,14},{2,13},{3,12},{4,11},{5,10},{6,9},{7,8},{8,7},{9,6},... | collective-permute-start | bytes 393224 | tf_op jit(solution)/shard_map/ppermute | solution.py:523
  136.8 8.8 %correlate.2.refs_17_ = bf16[24,2,512,512]{3,2,1,0:T(8,128)(2,1)} custom-call(f32[1]{0:T(128)} %bitcast.4.factor_ref, s32[8]{0:T(128)} %slice.11.used_ref, s32[16]{0:T(128)} %iota.22.index_ref, f32[16,192,128]{2,1,0:T(8,128)} %copy-done, f32[16,136,128]{2,1,0:T(8,128)} %copy-done.1), custom_call_target="tpu_custom_call" | custom-call | flops 4294967296 | bytes 9961472 | tf_op jit(solution)/shard_map/correlate/pallas_call | solution.py:478
  147.0 5.6 %collective-permute-done.7.refs_8_ = f32[1,256,128]{2,1,0:T(8,128)S(1)} collective-permute-done((f32[1,256,128]{2,1,0:T(8,128)S(1)}, f32[1,256,128]{2,1,0:T(8,128)S(1)}, u32[]{:S(2)}, u32[]{:S(2)}) %collective-permute-start.7) | collective-permute-done | bytes 131104 | tf_op jit(solution)/shard_map/ppermute | solution.py:523
  153.2 15.0 %correlate.3 = bf16[24,2,512,512]{3,2,1,0:T(8,128)(2,1)} custom-call(f32[1]{0:T(128)} %bitcast.4.factor_ref, s32[16]{0:T(128)} %bitcast.34, s32[16]{0:T(128)} %iota_xor_fusion.index_ref, f32[16,192,128]{2,1,0:T(8,128)} %copy-done, f32[1,256,128]{2,1,0:T(8,128)} %bitcast.28, f32[1,256,128]{2,1,0:T(8,128)} %copy-done.2, ...), custom_call_target="tpu_custom_call", output_to_operand_aliasing={{}: (20, {})} | custom-call | flops 8589934592 | bytes 19922944 | tf_op jit(solution)/shard_map/correlate/pallas_call | solution.py:478
  (55 shorter events, 8.8 us)
Async XLA Ops:
  23.2 42.8 %all-to-all-start = ((f32[16,192,128]{2,1,0:T(8,128)}), f32[16,192,128]{2,1,0:T(8,128)S(1)}, u32[]{:S(2)}, u32[]{:S(2)}) async-start(f32[16,192,128]{2,1,0:T(8,128)} %bitcast.26), calls=%async_computation | async-start | bytes 3145728 | tf_op jit(solution)/shard_map/all_to_all | solution.py:506
  66.0 70.9 %copy-start = (f32[16,192,128]{2,1,0:T(8,128)}, f32[16,192,128]{2,1,0:T(8,128)S(1)}, u32[]{:S(2)}) copy-start(f32[16,192,128]{2,1,0:T(8,128)S(1)} %all-to-all-done.refs_0_) | copy-start | bytes 4718596
  66.0 69.0 %all-to-all-start.1 = ((f32[16,136,128]{2,1,0:T(8,128)}), f32[16,136,128]{2,1,0:T(8,128)S(1)}, u32[]{:S(2)}, u32[]{:S(2)}) async-start(f32[16,136,128]{2,1,0:T(8,128)} %bitcast.27), calls=%async_computation.1 | async-start | bytes 2228224 | tf_op jit(solution)/shard_map/all_to_all | solution.py:506
  70.9 5.2 %collective-permute-start = (f32[1,256,128]{2,1,0:T(8,128)S(1)}, f32[1,256,128]{2,1,0:T(8,128)S(1)}, u32[]{:S(2)}, u32[]{:S(2)}) collective-permute-start(f32[1,256,128]{2,1,0:T(8,128)S(1)} %bitcast.46), channel_id=1, source_target_pairs={{0,1},{1,0},{2,3},{3,2},{4,5},{5,4},{6,7},{7,6},{8,9},{9,8},{10,11... | collective-permute-start | bytes 393224 | tf_op jit(solution)/shard_map/ppermute | solution.py:523
  71.3 35.0 %collective-permute-start.1 = (f32[1,256,128]{2,1,0:T(8,128)S(1)}, f32[1,256,128]{2,1,0:T(8,128)S(1)}, u32[]{:S(2)}, u32[]{:S(2)}) collective-permute-start(f32[1,256,128]{2,1,0:T(8,128)S(1)} %bitcast.45), channel_id=1, source_target_pairs={{0,8},{1,9},{2,10},{3,11},{4,12},{5,13},{6,14},{7,15},{8,0},{9,1},... | collective-permute-start | bytes 393224 | tf_op jit(solution)/shard_map/ppermute | solution.py:523
  73.4 35.8 %collective-permute-start.8 = (f32[1,256,128]{2,1,0:T(8,128)}, f32[1,256,128]{2,1,0:T(8,128)S(1)}, u32[]{:S(2)}, u32[]{:S(2)}) collective-permute-start(f32[1,256,128]{2,1,0:T(8,128)} %bitcast.15), channel_id=1, source_target_pairs={{0,9},{1,8},{2,11},{3,10},{4,13},{5,12},{6,15},{7,14},{8,1},{9,0},... | collective-permute-start | bytes 393224 | tf_op jit(solution)/shard_map/ppermute | solution.py:523
  74.0 38.5 %collective-permute-start.9 = (f32[1,256,128]{2,1,0:T(8,128)}, f32[1,256,128]{2,1,0:T(8,128)S(1)}, u32[]{:S(2)}, u32[]{:S(2)}) collective-permute-start(f32[1,256,128]{2,1,0:T(8,128)} %bitcast.17), channel_id=1, source_target_pairs={{0,10},{1,11},{2,8},{3,9},{4,14},{5,15},{6,12},{7,13},{8,2},{9,3},... | collective-permute-start | bytes 393224 | tf_op jit(solution)/shard_map/ppermute | solution.py:523
  76.1 69.6 %copy-start.2 = (f32[1,256,128]{2,1,0:T(8,128)}, f32[1,256,128]{2,1,0:T(8,128)S(1)}, u32[]{:S(2)}) copy-start(f32[1,256,128]{2,1,0:T(8,128)S(1)} %collective-permute-done.refs_2_) | copy-start | bytes 393220
  76.1 37.6 %collective-permute-start.3 = (f32[1,256,128]{2,1,0:T(8,128)}, f32[1,256,128]{2,1,0:T(8,128)S(1)}, u32[]{:S(2)}, u32[]{:S(2)}) collective-permute-start(f32[1,256,128]{2,1,0:T(8,128)} %bitcast.6), channel_id=1, source_target_pairs={{0,3},{1,2},{2,1},{3,0},{4,7},{5,6},{6,5},{7,4},{8,11},{9,10},{10,... | collective-permute-start | bytes 393224 | tf_op jit(solution)/shard_map/ppermute | solution.py:523
  106.3 39.4 %copy-start.3 = (f32[1,256,128]{2,1,0:T(8,128)}, f32[1,256,128]{2,1,0:T(8,128)S(1)}, u32[]{:S(2)}) copy-start(f32[1,256,128]{2,1,0:T(8,128)S(1)} %collective-permute-done.1.refs_9_) | copy-start | bytes 393220
  106.3 11.1 %collective-permute-start.2 = (f32[1,256,128]{2,1,0:T(8,128)}, f32[1,256,128]{2,1,0:T(8,128)S(1)}, u32[]{:S(2)}, u32[]{:S(2)}) collective-permute-start(f32[1,256,128]{2,1,0:T(8,128)} %bitcast.44), channel_id=1, source_target_pairs={{0,2},{1,3},{2,0},{3,1},{4,6},{5,7},{6,4},{7,5},{8,10},{9,11},{10,... | collective-permute-start | bytes 393224 | tf_op jit(solution)/shard_map/ppermute | solution.py:523
  109.2 36.5 %copy-start.4 = (f32[1,256,128]{2,1,0:T(8,128)}, f32[1,256,128]{2,1,0:T(8,128)S(1)}, u32[]{:S(2)}) copy-start(f32[1,256,128]{2,1,0:T(8,128)S(1)} %collective-permute-done.8.refs_10_) | copy-start | bytes 393220
  109.2 12.2 %collective-permute-start.10 = (f32[1,256,128]{2,1,0:T(8,128)}, f32[1,256,128]{2,1,0:T(8,128)}, u32[]{:S(2)}, u32[]{:S(2)}) collective-permute-start(f32[1,256,128]{2,1,0:T(8,128)} %bitcast.43), channel_id=1, source_target_pairs={{0,11},{1,10},{2,9},{3,8},{4,15},{5,14},{6,13},{7,12},{8,3},{9,2},... | collective-permute-start | bytes 393224 | tf_op jit(solution)/shard_map/ppermute | solution.py:523
  112.5 33.2 %copy-start.5 = (f32[1,256,128]{2,1,0:T(8,128)}, f32[1,256,128]{2,1,0:T(8,128)S(1)}, u32[]{:S(2)}) copy-start(f32[1,256,128]{2,1,0:T(8,128)S(1)} %collective-permute-done.9.refs_11_) | copy-start | bytes 393220
  112.5 13.3 %collective-permute-start.11 = (f32[1,256,128]{2,1,0:T(8,128)}, f32[1,256,128]{2,1,0:T(8,128)}, u32[]{:S(2)}, u32[]{:S(2)}) collective-permute-start(f32[1,256,128]{2,1,0:T(8,128)} %bitcast.42), channel_id=1, source_target_pairs={{0,12},{1,13},{2,14},{3,15},{4,8},{5,9},{6,10},{7,11},{8,4},{9,5},... | collective-permute-start | bytes 393224 | tf_op jit(solution)/shard_map/ppermute | solution.py:523
  113.7 32.0 %copy-start.6 = (f32[1,256,128]{2,1,0:T(8,128)}, f32[1,256,128]{2,1,0:T(8,128)S(1)}, u32[]{:S(2)}) copy-start(f32[1,256,128]{2,1,0:T(8,128)S(1)} %collective-permute-done.3.refs_4_) | copy-start | bytes 393220
  113.7 13.3 %collective-permute-start.5 = (f32[1,256,128]{2,1,0:T(8,128)}, f32[1,256,128]{2,1,0:T(8,128)}, u32[]{:S(2)}, u32[]{:S(2)}) collective-permute-start(f32[1,256,128]{2,1,0:T(8,128)} %bitcast.41), channel_id=1, source_target_pairs={{0,5},{1,4},{2,7},{3,6},{4,1},{5,0},{6,3},{7,2},{8,13},{9,12},{10,... | collective-permute-start | bytes 393224 | tf_op jit(solution)/shard_map/ppermute | solution.py:523
  117.3 28.4 %copy-start.7 = (f32[1,256,128]{2,1,0:T(8,128)}, f32[1,256,128]{2,1,0:T(8,128)S(1)}, u32[]{:S(2)}) copy-start(f32[1,256,128]{2,1,0:T(8,128)S(1)} %collective-permute-done.2.refs_3_) | copy-start | bytes 393220
  117.3 13.0 %collective-permute-start.4 = (f32[1,256,128]{2,1,0:T(8,128)}, f32[1,256,128]{2,1,0:T(8,128)}, u32[]{:S(2)}, u32[]{:S(2)}) collective-permute-start(f32[1,256,128]{2,1,0:T(8,128)} %bitcast.40), channel_id=1, source_target_pairs={{0,4},{1,5},{2,6},{3,7},{4,0},{5,1},{6,2},{7,3},{8,12},{9,13},{10,... | collective-permute-start | bytes 393224 | tf_op jit(solution)/shard_map/ppermute | solution.py:523
  121.4 10.0 %collective-permute-start.12 = (f32[1,256,128]{2,1,0:T(8,128)}, f32[1,256,128]{2,1,0:T(8,128)}, u32[]{:S(2)}, u32[]{:S(2)}) collective-permute-start(f32[1,256,128]{2,1,0:T(8,128)} %bitcast.39), channel_id=1, source_target_pairs={{0,13},{1,12},{2,15},{3,14},{4,9},{5,8},{6,11},{7,10},{8,5},{9,4},... | collective-permute-start | bytes 393224 | tf_op jit(solution)/shard_map/ppermute | solution.py:523
  125.7 21.2 %collective-permute-start.13 = (f32[1,256,128]{2,1,0:T(8,128)}, f32[1,256,128]{2,1,0:T(8,128)}, u32[]{:S(2)}, u32[]{:S(2)}) collective-permute-start(f32[1,256,128]{2,1,0:T(8,128)} %bitcast.38), channel_id=1, source_target_pairs={{0,14},{1,15},{2,12},{3,13},{4,10},{5,11},{6,8},{7,9},{8,6},{9,7},... | collective-permute-start | bytes 393224 | tf_op jit(solution)/shard_map/ppermute | solution.py:523
  130.4 16.6 %collective-permute-start.6 = (f32[1,256,128]{2,1,0:T(8,128)}, f32[1,256,128]{2,1,0:T(8,128)}, u32[]{:S(2)}, u32[]{:S(2)}) collective-permute-start(f32[1,256,128]{2,1,0:T(8,128)} %bitcast.37), channel_id=1, source_target_pairs={{0,6},{1,7},{2,4},{3,5},{4,2},{5,3},{6,0},{7,1},{8,14},{9,15},{10,... | collective-permute-start | bytes 393224 | tf_op jit(solution)/shard_map/ppermute | solution.py:523
  131.4 15.6 %collective-permute-start.14 = (f32[1,256,128]{2,1,0:T(8,128)}, f32[1,256,128]{2,1,0:T(8,128)}, u32[]{:S(2)}, u32[]{:S(2)}) collective-permute-start(f32[1,256,128]{2,1,0:T(8,128)} %bitcast.36), channel_id=1, source_target_pairs={{0,15},{1,14},{2,13},{3,12},{4,11},{5,10},{6,9},{7,8},{8,7},{9,6},... | collective-permute-start | bytes 393224 | tf_op jit(solution)/shard_map/ppermute | solution.py:523
  145.7 6.8 %collective-permute-start.7 = (f32[1,256,128]{2,1,0:T(8,128)S(1)}, f32[1,256,128]{2,1,0:T(8,128)S(1)}, u32[]{:S(2)}, u32[]{:S(2)}) collective-permute-start(f32[1,256,128]{2,1,0:T(8,128)S(1)} %bitcast.35), channel_id=1, source_target_pairs={{0,7},{1,6},{2,5},{3,4},{4,3},{5,2},{6,1},{7,0},{8,15},{9,14},{10,... | collective-permute-start | bytes 393224 | tf_op jit(solution)/shard_map/ppermute | solution.py:523
  (7 other events, 56.8 us)
